TPU v7x, 32 devices: a whole 2x2x4 slice. The times are simulated.
32 devices in a mesh: seq: 8 (over z, x), head: 4 (over y, core).
Axes of the slice: x: 2, y: 2, z: 4, core: 2. Of those that a mesh axis runs over, the one named last changes fastest.
Arguments:
- hidden: bfloat16 [4096, 3584], P('seq'), may hold values from -6 to 6
- norm_gain: float32 [3584], replicated, may hold values from 0.1 to 1.9
- query_weight: bfloat16 [3584, 3584], P('seq', 'head'), may hold values from -0.09375 to 0.09375
- query_bias: float32 [3584], P('head'), may hold values from -8 to 8
- keyval_weight: bfloat16 [3584, 2, 512], P('seq', None, 'head'), may hold values from -0.09375 to 0.09375
- keyval_bias: float32 [2, 512], P(None, 'head'), may hold values from -8 to 8
- beacon_weight: bfloat16 [3584, 2, 512], P('seq', None, 'head'), may hold values from -0.375 to 0.375
- beacon_bias: float32 [2, 512], P(None, 'head'), may hold values from -8 to 8
- out_weight: bfloat16 [3584, 3584], P('head', 'seq'), may hold values from -0.09375 to 0.09375
- ratios: int32 [2], replicated, may hold values from 8 to 32, as said below
Outputs:
- layer_out: bfloat16 [4096, 3584], P('seq', 'head')
Inputs may be any that keep to these rules, and one draw needn't show every extreme that they name: `ratios`: each ratio is a whole number; at least one segment has ratio 8 and at least one has ratio 4 * 8.
All inputs are finite; a program needn't handle non-finite values.
Results may differ from a plain program's by a relative error of at most 0.012.
The roundings to bfloat16 on the way count: a program that leaves them out, or rounds other values in their place, can miss the bound.
Values may be sent and summed in bfloat16 or wider, within the bound.
No kernel may reach another device: no remote copies, remote signals or barrier semaphores. Data moves between devices by JAX's collectives and lax.ppermute only.
A program may use at most 192 MiB of HBM per device.

v0:
```python
import math

import jax
import jax.numpy as jnp
from jax import lax
from jax.sharding import PartitionSpec as P

QH = 28
KVH = 4
HEAD_DIM = 128
SPLIT = 4
R_MIN = 8


def from_behind(value, axis, steps):
    count = lax.axis_size(axis)
    first, last = (max(0, -steps), min(count, count - steps))
    return lax.ppermute(value, axis, [(source, source + steps) for source in range(first, last)])


def update_state(running, queries, kv_piece, piece_mask):
    row_max, denominator, weighted = running
    row_count = kv_piece.shape[0]
    heads_kv = queries.shape[1]
    key_heads = kv_piece[:, 0].reshape(row_count, heads_kv, HEAD_DIM)
    value_heads = kv_piece[:, 1].reshape(row_count, heads_kv, HEAD_DIM)
    scores = jnp.einsum(
        "tkgd,ukd->kgtu", queries, key_heads, preferred_element_type=jnp.float32
    ) / math.sqrt(HEAD_DIM)
    scores = jnp.where(piece_mask[None, None], scores, -1e30)
    new_max = jnp.maximum(row_max, jnp.max(scores, axis=3))
    weights = jnp.exp(scores - new_max[..., None])
    factor = jnp.exp(row_max - new_max)
    denominator = denominator * factor + jnp.sum(weights, axis=3)
    weighted = weighted * factor[..., None] + jnp.einsum(
        "kgtu,ukd->kgtd",
        weights.astype(jnp.bfloat16),
        value_heads,
        preferred_element_type=jnp.float32,
    )
    return (new_max, denominator, weighted)


def on_device(
    hidden,
    norm_gain,
    query_weight,
    query_bias,
    keyval_weight,
    keyval_bias,
    beacon_weight,
    beacon_bias,
    out_weight,
    ratios,
):
    rows_dev = hidden.shape[0]
    slots_dev = rows_dev // R_MIN
    seq_index = lax.axis_index("seq")
    segment = seq_index // SPLIT
    seg_place = seq_index % SPLIT
    floats = hidden.astype(jnp.float32)
    normed = (
        floats * lax.rsqrt(jnp.mean(floats * floats, axis=1, keepdims=True) + 1e-06) * norm_gain
    ).astype(jnp.bfloat16)
    segment_ids = jnp.arange(ratios.shape[0], dtype=jnp.int32)
    own_ratio = jnp.sum(jnp.where(segment_ids == segment, ratios, 0))
    slot_ids = jnp.arange(slots_dev, dtype=jnp.int32)
    token_ids = jnp.arange(rows_dev, dtype=jnp.int32)
    member = (
        (token_ids[None, :] // own_ratio == slot_ids[:, None])
        & (slot_ids[:, None] < rows_dev // own_ratio)
    ).astype(jnp.bfloat16)
    pooled = (
        jnp.dot(member, normed, preferred_element_type=jnp.float32) / own_ratio.astype(jnp.float32)
    ).astype(jnp.bfloat16)
    query_cols = query_weight.shape[1]
    kv_cols = keyval_weight.shape[2]
    left_cols = normed
    query_sum = jnp.dot(
        left_cols,
        lax.all_gather(query_weight, "seq", axis=0, tiled=True),
        preferred_element_type=jnp.float32,
    )
    shard_rows = (
        lax.all_gather(keyval_weight, "seq", axis=0, tiled=True),
        lax.all_gather(beacon_weight, "seq", axis=0, tiled=True),
    )
    row_count = shard_rows[0].shape[0]
    left_cols = normed
    keyval_part = jnp.dot(
        left_cols, shard_rows[0].reshape(row_count, 2 * kv_cols), preferred_element_type=jnp.float32
    )
    beacon_part = jnp.dot(
        pooled, shard_rows[1].reshape(row_count, 2 * kv_cols), preferred_element_type=jnp.float32
    )
    query = (query_sum + query_bias).astype(jnp.bfloat16)
    keyval = (keyval_part.reshape(rows_dev, 2, kv_cols) + keyval_bias).astype(jnp.bfloat16)
    beacon = (beacon_part.reshape(slots_dev, 2, kv_cols) + beacon_bias).astype(jnp.bfloat16)
    heads_kv = kv_cols // HEAD_DIM
    groups = QH // KVH
    queries = query.reshape(rows_dev, heads_kv, groups, HEAD_DIM)
    query_pos = seg_place * rows_dev + token_ids
    kv_list = []
    mask_list = []
    for offset in range(SPLIT - 1, 0, -1):
        earlier = from_behind(keyval, "seq", offset)
        key_pos = (seg_place - offset) * rows_dev + token_ids
        kv_list.append(earlier)
        mask_list.append((offset <= seg_place) & (key_pos[None, :] <= query_pos[:, None]))
    kv_list.append(keyval)
    mask_list.append(token_ids[None, :] <= token_ids[:, None])
    segment_kv = jnp.concatenate(kv_list, axis=0)
    segment_mask = jnp.concatenate(mask_list, axis=1)
    softmax_state = (
        jnp.full((heads_kv, groups, rows_dev), -1e30, jnp.float32),
        jnp.zeros((heads_kv, groups, rows_dev), jnp.float32),
        jnp.zeros((heads_kv, groups, rows_dev, HEAD_DIM), jnp.float32),
    )
    softmax_state = update_state(softmax_state, queries, segment_kv, segment_mask)
    shard_rows = lax.all_gather(beacon, "seq", axis=0, tiled=True)
    global_slot = jnp.arange(shard_rows.shape[0], dtype=jnp.int32)
    source = global_slot // slots_dev
    source_segment = source // SPLIT
    source_ratio = jnp.sum(
        jnp.where(segment_ids[None, :] == source_segment[:, None], ratios[None, :], 0), axis=1
    )
    slot_local = global_slot % slots_dev
    softmax_state = update_state(
        softmax_state,
        queries,
        shard_rows,
        ((slot_local < rows_dev // source_ratio) & (source_segment < segment))[None, :],
    )
    row_max, denominator, weighted = softmax_state
    attention = (
        jnp.transpose(weighted / denominator[..., None], (2, 0, 1, 3))
        .reshape(rows_dev, query_cols)
        .astype(jnp.bfloat16)
    )
    partials = jnp.dot(
        attention,
        lax.all_gather(out_weight, "seq", axis=1, tiled=True),
        preferred_element_type=jnp.float32,
    )
    return lax.psum_scatter(partials.astype(jnp.bfloat16), "head", scatter_dimension=1, tiled=True)


def solution(mesh):
    return jax.shard_map(
        on_device,
        mesh=mesh,
        in_specs=(
            P("seq", None),
            P(),
            P("seq", "head"),
            P("head"),
            P("seq", None, "head"),
            P(None, "head"),
            P("seq", None, "head"),
            P(None, "head"),
            P("head", "seq"),
            P(),
        ),
        out_specs=P("seq", "head"),
        check_vma=False,
    )
```

profile of v0, /device:TPU:0, one launch (start us, length us, event | category | flops | bytes accessed | tf_op | source)
XLA Modules:
  0.0 384.1 jit_solution(10671201030346026851)
XLA Ops:
  6.5 0.7 all-gather.5.cloned.1.call-update
  7.3 0.0 all-gather.9.cloned.1.call-start
  7.3 0.7 all-gather.9.cloned.1.call-update
  8.0 0.0 all-gather.7.cloned.1.call-start
  8.1 0.7 all-gather.7.cloned.1.call-update
  8.7 0.0 all-gather.11.cloned.1.call-start
  8.8 0.5 all-gather.11.cloned.1.call-update
  9.3 0.0 reduce-scatter.4.cloned.1.call-start
  9.4 0.1 iota_compare_fusion
  9.5 1.3 fusion.67
  12.8 0.8 add_select_fusion
  14.2 0.7 fusion.52
  15.0 0.1 compare_and_fusion.3
  15.1 2.8 fusion.7
  17.9 0.6 compare_and_fusion.2
  18.5 0.4 pad_add_fusion
  18.9 39.6 %all-gather.5.cloned.1.call-done = bf16[3584,2,128]{2,1,0:T(2,128)(2,1)} async-done(((bf16[448,2,128]{2,1,0:T(2,128)(2,1)}), bf16[3584,2,128]{2,1,0:T(2,128)(2,1)}) %all-gather.5.cloned.1.call-update) | async-done | bytes 1835024 | tf_op jit(solution)/shard_map/all_gather | solution.py:85
  58.5 4.5 %copy.52 = bf16[3584,2,128]{0,2,1:T(8,128)(2,1)S(1)} copy(bf16[3584,2,128]{2,1,0:T(2,128)(2,1)} %all-gather.5.cloned.1.call-done) | data formatting | bytes 3670016 | tf_op jit(solution)/shard_map/reshape | solution.py:91
  63.1 0.0 copy-start.3
  63.1 3.2 fusion.31
  66.3 0.0 copy-start.1
  66.3 4.7 %collective-permute-start = (bf16[512,2,128]{2,0,1:T(8,128)(2,1)S(1)}, bf16[512,2,128]{2,0,1:T(8,128)(2,1)}, u32[]{:S(2)}, u32[]{:S(2)}) collective-permute-start(bf16[512,2,128]{2,0,1:T(8,128)(2,1)S(1)} %fusion.31), channel_id=1, source_target_pairs={{0,12},{4,16},{8,20},{12,24},{16,28},{1,13},{5,17},{9,21},{13,25},... | collective-permute-start | bytes 786440 | tf_op jit(solution)/shard_map/ppermute | solution.py:18
  71.0 3.5 collective-permute-start.1
  74.5 3.4 collective-permute-start.2
  77.9 37.8 %all-gather.9.cloned.1.call-done = bf16[3584,2,128]{2,1,0:T(2,128)(2,1)} async-done(((bf16[448,2,128]{2,1,0:T(2,128)(2,1)}), bf16[3584,2,128]{2,1,0:T(2,128)(2,1)}) %all-gather.9.cloned.1.call-update) | async-done | bytes 1835024 | tf_op jit(solution)/shard_map/all_gather | solution.py:86
  115.7 4.5 %copy.54 = bf16[3584,2,128]{0,2,1:T(8,128)(2,1)S(1)} copy(bf16[3584,2,128]{2,1,0:T(2,128)(2,1)} %all-gather.9.cloned.1.call-done) | data formatting | bytes 3670016 | tf_op jit(solution)/shard_map/reshape | solution.py:94
  120.2 0.0 copy-done.3
  120.2 3.8 fusion.39
  124.0 32.0 %all_gather.18 = bf16[512,2,128]{2,0,1:T(8,128)(2,1)S(1)} all-gather(bf16[64,2,128]{2,0,1:T(8,128)(2,1)S(1)} %fusion.39), channel_id=1, replica_groups=mesh['seq'=8,'head'=4] {'seq'}, dimensions={0}, use_global_device_ids=true | all-gather | bytes 294912 | tf_op jit(solution)/shard_map/all_gather | solution.py:120
  156.0 0.0 collective-permute-done
  156.0 0.0 collective-permute-done.1
  156.0 0.0 collective-permute-done.2
  156.0 1.2 pad_maximum_fusion
  157.2 63.3 %all-gather.7.cloned.1.call-done = bf16[3584,896]{1,0:T(8,128)(2,1)} async-done(((bf16[448,896]{1,0:T(8,128)(2,1)}), bf16[3584,896]{1,0:T(8,128)(2,1)}) %all-gather.7.cloned.1.call-update) | async-done | bytes 6422544 | tf_op jit(solution)/shard_map/all_gather | solution.py:81
  220.5 8.9 %add_convert_fusion = bf16[512,896]{1,0:T(8,128)(2,1)} fusion(bf16[3584,896]{1,0:T(8,128)(2,1)} %all-gather.7.cloned.1.call-done, f32[896]{0:T(1024)S(1)} %copy-done.1, bf16[512,3584]{1,0:T(8,128)(2,1)} %param.10, f32[3584]{0:T(1024)S(1)} %copy-done, f32[512]{0:T(512)S(1)} %add_rsqrt_fusion), kind=kOutput, calls=%fused_computation.33 | convolution fusion | flops 3296591872 | bytes 11030016 | tf_op jit(solution)/shard_map/dot_general | solution.py:79
  229.4 1.5 copy.38
  230.9 1.2 bitcast_reduce_fusion
  232.1 12.2 %fusion.2 = (f32[7,512]{1,0:T(8,128)S(1)}, f32[2048,512,7]{1,0,2:T(8,128)}) fusion(pred[512,2048]{0,1:T(8,128)(4,1)S(1)} %pad_add_fusion, bf16[512,7,128]{0,2,1:T(8,128)(2,1)S(1)} %bitcast.118, bf16[2048,2,128]{2,0,1:T(8,128)(2,1)S(1)} %pad_maximum_fusion), kind=kOutput, calls=%fused_computation.4 | convolution fusion | flops 1901064704 | bytes 31864832 | tf_op jit(solution)/shard_map/tkgd,ukd->kgtu/dot_general | solution.py:27
  244.3 1.8 fusion.11
  246.1 12.9 %fusion = f32[7,512]{1,0:T(8,128)S(1)} fusion(f32[2048,512,7]{1,0,2:T(8,128)} %get-tuple-element.14, f32[7,512]{1,0:T(8,128)S(1)} %get-tuple-element.9, pred[512,2048]{0,1:T(8,128)(4,1)S(1)} %pad_add_fusion), kind=kLoop, calls=%fused_computation.2 | loop fusion | flops 29356544 | bytes 30437376 | tf_op jit(solution)/shard_map/reduce_sum | solution.py:34
  259.0 1.9 fusion.18
  260.9 14.0 %divide_convert_fusion = bf16[7,512,128]{1,2,0:T(8,128)(2,1)S(1)} fusion(f32[7,512,128]{1,2,0:T(8,128)S(1)} %fusion.18, f32[2048,512,7]{1,0,2:T(8,128)} %get-tuple-element.14, f32[7,512]{1,0:T(8,128)S(1)} %get-tuple-element.9, pred[512,2048]{0,1:T(8,128)(4,1)S(1)} %pad_add_fusion, f32[7,512]{1,0:T(8,128)S(1)} %get-tuple-element.5, ...), kind=kOutput, calls=%fused_computation.32 | convolution fusion | flops 1910702080 | bytes 33751040 | tf_op jit(solution)/shard_map/kgtu,ukd->kgtd/dot_general | solution.py:35
  274.9 46.5 %all-gather.11.cloned.1.call-done = bf16[896,3584]{0,1:T(8,128)(2,1)} async-done(((bf16[896,448]{0,1:T(8,128)(2,1)}), bf16[896,3584]{0,1:T(8,128)(2,1)}) %all-gather.11.cloned.1.call-update) | async-done | bytes 6422544 | tf_op jit(solution)/shard_map/all_gather | solution.py:142
  321.4 8.4 %convolution_convert_fusion = bf16[512,3584]{1,0:T(8,128)(2,1)} fusion(bf16[512,896]{0,1:T(8,128)(2,1)S(1)} %bitcast.120, bf16[896,3584]{0,1:T(8,128)(2,1)} %all-gather.11.cloned.1.call-done), kind=kOutput, calls=%fused_computation.17 | convolution fusion | flops 3290169344 | bytes 11010048 | tf_op jit(solution)/shard_map/dot_general | solution.py:140
  329.8 5.9 %copy.56 = bf16[512,3584]{0,1:T(8,128)(2,1)} copy(bf16[512,3584]{1,0:T(8,128)(2,1)} %convolution_convert_fusion) | data formatting | bytes 7340032
  335.7 0.0 reduce-scatter.4.cloned.1.call-update
  335.8 39.6 %reduce-scatter.4.cloned.1.call-done = bf16[896,512]{1,0:T(8,128)(2,1)} async-done(((bf16[3584,512]{1,0:T(8,128)(2,1)}), bf16[896,512]{1,0:T(8,128)(2,1)}) %reduce-scatter.4.cloned.1.call-update) | async-done | bytes 917520
  375.3 2.2 copy.57
  (13 shorter events, 0.1 us)
Async XLA Ops:
  6.5 56.5 %copy-start = (f32[3584]{0:T(1024)S(1)}, f32[3584]{0:T(1024)}, u32[]{:S(2)}) copy-start(f32[3584]{0:T(1024)} %param.11) | copy-start | bytes 43012
  6.5 56.5 %copy-start.2 = (f32[2,128]{1,0:T(2,128)S(1)}, f32[2,128]{1,0:T(2,128)}, u32[]{:S(2)}) copy-start(f32[2,128]{1,0:T(2,128)} %param.15) | copy-start | bytes 3076
  6.5 52.0 %all-gather.5.cloned.1.call-start = ((), (), s32[]{:S(2)}) async-start(), calls=%async_computation.1 | async-start | bytes 2064384 | tf_op jit(solution)/shard_map/all_gather | solution.py:85
  7.3 108.4 %all-gather.9.cloned.1.call-start = ((), (), s32[]{:S(2)}) async-start(), calls=%async_computation.3 | async-start | bytes 2064384 | tf_op jit(solution)/shard_map/all_gather | solution.py:86
  8.0 212.5 %all-gather.7.cloned.1.call-start = ((), (), s32[]{:S(2)}) async-start(), calls=%async_computation.2 | async-start | bytes 7225344 | tf_op jit(solution)/shard_map/all_gather | solution.py:81
  8.7 312.7 %all-gather.11.cloned.1.call-start = ((), (), s32[]{:S(2)}) async-start(), calls=%async_computation.4 | async-start | bytes 7225344 | tf_op jit(solution)/shard_map/all_gather | solution.py:142
  9.3 366.0 %reduce-scatter.4.cloned.1.call-start = ((), (), s32[]{:S(2)}) async-start(), calls=%async_computation.5 | async-start | bytes 4587520
  63.1 57.1 %copy-start.3 = (f32[2,128]{1,0:T(2,128)S(1)}, f32[2,128]{1,0:T(2,128)}, u32[]{:S(2)}) copy-start(f32[2,128]{1,0:T(2,128)} %param.17) | copy-start | bytes 3076
  66.3 154.2 %copy-start.1 = (f32[896]{0:T(1024)S(1)}, f32[896]{0:T(1024)}, u32[]{:S(2)}) copy-start(f32[896]{0:T(1024)} %param.13) | copy-start | bytes 10756
  66.3 89.7 %collective-permute-start = (bf16[512,2,128]{2,0,1:T(8,128)(2,1)S(1)}, bf16[512,2,128]{2,0,1:T(8,128)(2,1)}, u32[]{:S(2)}, u32[]{:S(2)}) collective-permute-start(bf16[512,2,128]{2,0,1:T(8,128)(2,1)S(1)} %fusion.31), channel_id=1, source_target_pairs={{0,12},{4,16},{8,20},{12,24},{16,28},{1,13},{5,17},{9,21},{13,25},... | collective-permute-start | bytes 786440 | tf_op jit(solution)/shard_map/ppermute | solution.py:18
  71.0 85.0 %collective-permute-start.1 = (bf16[512,2,128]{2,0,1:T(8,128)(2,1)S(1)}, bf16[512,2,128]{2,0,1:T(8,128)(2,1)}, u32[]{:S(2)}, u32[]{:S(2)}) collective-permute-start(bf16[512,2,128]{2,0,1:T(8,128)(2,1)S(1)} %fusion.31), channel_id=1, source_target_pairs={{0,8},{4,12},{8,16},{12,20},{16,24},{20,28},{1,9},{5,13},{9,17},{1... | collective-permute-start | bytes 786440 | tf_op jit(solution)/shard_map/ppermute | solution.py:18
  74.5 81.5 %collective-permute-start.2 = (bf16[512,2,128]{2,0,1:T(8,128)(2,1)S(1)}, bf16[512,2,128]{2,0,1:T(8,128)(2,1)}, u32[]{:S(2)}, u32[]{:S(2)}) collective-permute-start(bf16[512,2,128]{2,0,1:T(8,128)(2,1)S(1)} %fusion.31), channel_id=1, source_target_pairs={{0,4},{4,8},{8,12},{12,16},{16,20},{20,24},{24,28},{1,5},{5,9},{9,... | collective-permute-start | bytes 786440 | tf_op jit(solution)/shard_map/ppermute | solution.py:18
Sparse Core Ops, SparseCore 0:
  9.5 48.9 all-gather.4
  60.7 54.9 all-gather.8
  117.9 102.6 all-gather.6
  222.6 98.7 all-gather.10
  335.9 39.4 reduce-scatter.3
where the time goes:
time: 385 us; the launch traced here: 384 us
  waiting for transfers between devices  229 us (59%)
  matrix products  53.6 us (14%)
  blocking collectives  32 us (8%)
  other arithmetic  22.7 us (6%)
  local copies, waits for them, and re-layouts  18.6 us (5%)
  between operations  16 us (4%)
  starting transfers between devices  11.7 us (3%)
    all_gather x1, waiting for transfers between devices, on_device(): lax.all_gather(query_weight, 'seq', axis=0, tiled=True)  63.3 us
    all_gather x1, waiting for transfers between devices, on_device(): lax.all_gather(out_weight, 'seq', axis=1, tiled=True)  46.5 us
    unnamed x6, waiting for transfers between devices  42.2 us
    all_gather x1, waiting for transfers between devices, on_device(): lax.all_gather(keyval_weight, 'seq', axis=0, tiled=True)  39.6 us
    all_gather x1, waiting for transfers between devices, on_device(): lax.all_gather(beacon_weight, 'seq', axis=0, tiled=True)  37.8 us
    all_gather x1, blocking collectives, on_device(): shard_rows = lax.all_gather(beacon, 'seq', axis=0, tiled=True)  32 us
    dot_general x2, matrix products, update_state(): jnp.einsum('kgtu,ukd->kgtd', weights.astype(jnp.bfloat16), value_heads, p...  15.9 us
    reduce_sum x2, other arithmetic, update_state(): denominator = denominator * factor + jnp.sum(weights, axis=3)  14.7 us
  transfers between devices with their start and end apart: 8, of which 5 were waited for; matrix products, arithmetic and copies ran while one was open for 20% of the time, Pallas kernels for 0%

commit v1 on v0

v1 whole, which is shorter than its diff:
```python
import functools
import math

import jax
import jax.numpy as jnp
from jax import lax
from jax.experimental import pallas as pl
from jax.experimental.pallas import tpu as pltpu
from jax.sharding import PartitionSpec as P

QH = 28
KVH = 4
HEAD_DIM = 128
SPLIT = 4
R_MIN = 8
AXES = ("seq", "head")
VMEM_LIMIT = 56 * 1024 * 1024


def params():
    return pltpu.CompilerParams(vmem_limit_bytes=VMEM_LIMIT)


def vmem():
    return pl.BlockSpec(memory_space=pltpu.VMEM)


def smem():
    return pl.BlockSpec(memory_space=pltpu.SMEM)


def hbm():
    return pl.BlockSpec(memory_space=pl.ANY)


def moves(n_seq, rule):
    pairs = []
    for s in range(n_seq):
        for h in range(KVH):
            target = rule(s >> 2, (s >> 1) & 1, s & 1, h >> 1, h & 1)
            if target is not None:
                big, l, x, y, c = target
                pairs.append((s * KVH + h, (4 * big + 2 * l + x) * KVH + 2 * y + c))
    return pairs


def send(value, n_seq, rule):
    return lax.ppermute(value, AXES, moves(n_seq, rule))


def norm_kernel(info, hidden, first, second, gain, normed, pooled, buf, sems):
    rows = hidden.shape[0]
    half = rows // 2
    tiles = sems.shape[0]
    tile = rows // tiles
    matched, y_bit, ratio = info[0], info[1], info[2]

    def land(i):
        return buf.at[pl.ds(i * tile, tile), :]

    for i in range(tiles):

        @pl.when(matched == 1)
        def _():
            pltpu.make_async_copy(hidden.at[pl.ds(i * tile, tile), :], land(i), sems.at[i]).start()

        upper = (i * tile) // half
        local = pl.ds(i * tile - upper * half, tile)

        @pl.when((matched == 0) & (y_bit == upper))
        def _():
            pltpu.make_async_copy(first.at[local, :], land(i), sems.at[i]).start()

        @pl.when((matched == 0) & (y_bit != upper))
        def _():
            pltpu.make_async_copy(second.at[local, :], land(i), sems.at[i]).start()

    scale = gain[...]
    for i in range(tiles):
        pltpu.make_async_copy(hidden.at[pl.ds(i * tile, tile), :], land(i), sems.at[i]).wait()
        floats = buf[i * tile : (i + 1) * tile, :].astype(jnp.float32)
        mean = jnp.mean(floats * floats, axis=1, keepdims=True)
        normed[i * tile : (i + 1) * tile, :] = (floats * lax.rsqrt(mean + 1e-06) * scale).astype(
            jnp.bfloat16
        )
    slots = pooled.shape[0]
    token = lax.broadcasted_iota(jnp.int32, (slots, rows), 1)
    slot = lax.broadcasted_iota(jnp.int32, (slots, rows), 0)
    member = (
        (token >= slot * ratio) & (token < (slot + 1) * ratio) & (slot < info[3])
    ).astype(jnp.float32).astype(jnp.bfloat16)
    total = jnp.dot(member, normed[...], preferred_element_type=jnp.float32)
    pooled[...] = (total / ratio.astype(jnp.float32)).astype(jnp.bfloat16)


def norm_and_pool(info, hidden, first, second, gain):
    rows, width = hidden.shape
    tiles = 8
    return pl.pallas_call(
        norm_kernel,
        out_shape=(
            jax.ShapeDtypeStruct((rows, width), jnp.bfloat16),
            jax.ShapeDtypeStruct((rows // R_MIN, width), jnp.bfloat16),
        ),
        in_specs=[smem(), hbm(), hbm(), hbm(), vmem()],
        out_specs=(vmem(), vmem()),
        scratch_shapes=[pltpu.VMEM((rows, width), jnp.bfloat16), pltpu.SemaphoreType.DMA((tiles,))],
        compiler_params=params(),
        cost_estimate=pl.CostEstimate(
            flops=2 * rows * rows // R_MIN * width, bytes_accessed=4 * rows * width, transcendentals=0
        ),
        name="norm_pool",
    )(info, hidden, first, second, gain.reshape(1, width))


def fetch_weights(info, refs, weights, sems, count):
    matched, big, l, x = info[0], info[4], info[5], info[6]
    rows = refs[0].shape[0] // 2
    own, copied = refs[:count], refs[count:]
    half = count // 2

    def spot(i, j):
        flip, m = i // half, i % half
        block = 4 * (big ^ m) + 2 * (l ^ j) + (x ^ flip)
        return weights.at[pl.ds(pl.multiple_of(block * rows, 16), rows), :]

    for i in range(count):
        for j in range(2):
            part = pl.ds(j * rows, rows)

            @pl.when(matched == 1)
            def _():
                pltpu.make_async_copy(own[i].at[part, :], spot(i, j), sems.at[2 * i + j]).start()

            @pl.when(matched == 0)
            def _():
                pltpu.make_async_copy(copied[i].at[part, :], spot(i, j), sems.at[2 * i + j]).start()

    for i in range(count):
        for j in range(2):
            pltpu.make_async_copy(
                own[i].at[pl.ds(j * rows, rows), :], spot(i, j), sems.at[2 * i + j]
            ).wait()


def query_kernel(count, info, normed, bias, *rest):
    refs, (out, weights, sems) = rest[: 2 * count], rest[2 * count :]
    fetch_weights(info, refs, weights, sems, count)
    tile = 256
    for i in range(out.shape[0] // tile):
        rows = slice(i * tile, (i + 1) * tile)
        product = jnp.dot(normed[rows, :], weights[...], preferred_element_type=jnp.float32)
        out[rows, :] = (product + bias[...]).astype(jnp.bfloat16)


def keyval_kernel(count, info, normed, pooled, bias, *rest):
    refs, (out, weights, sems) = rest[: 2 * count], rest[2 * count :]
    fetch_weights(info, refs, weights, sems, count)
    rows = normed.shape[0]
    cols = out.shape[1]
    product = jnp.dot(normed[...], weights[:, :cols], preferred_element_type=jnp.float32)
    out[:rows, :] = (product + bias[:, :cols]).astype(jnp.bfloat16)
    product = jnp.dot(pooled[...], weights[:, cols:], preferred_element_type=jnp.float32)
    out[rows:, :] = (product + bias[:, cols:]).astype(jnp.bfloat16)


def project(kernel, out_rows, out_cols, info, left, bias, own, copied):
    count = len(own)
    width = left[0].shape[1]
    cols = own[0].shape[1]
    return pl.pallas_call(
        functools.partial(kernel, count),
        out_shape=jax.ShapeDtypeStruct((out_rows, out_cols), jnp.bfloat16),
        in_specs=[smem()] + [vmem()] * (len(left) + 1) + [hbm()] * (2 * count),
        out_specs=vmem(),
        scratch_shapes=[
            pltpu.VMEM((width, cols), jnp.bfloat16),
            pltpu.SemaphoreType.DMA((2 * count,)),
        ],
        compiler_params=params(),
        cost_estimate=pl.CostEstimate(
            flops=2 * out_rows * out_cols * width,
            bytes_accessed=2 * width * (out_rows + cols),
            transcendentals=0,
        ),
        name="project",
    )(info, *left, bias.reshape(1, -1), *own, *copied)


def attend_kernel(tokens, beacons, info, ratios, queries, pair, far_pair, *rest):
    beacon_refs, out = rest[:beacons], rest[beacons]
    place = 2 * info[7] + info[6]
    big = info[4]
    scale = 1.0 / math.sqrt(HEAD_DIM)
    stride = pair.shape[0] // 2
    slots = stride - tokens
    tile = min(256, tokens)

    def pieces(variant):
        full = []
        if variant in (1, 3):
            full.append((pair, stride))
        if variant in (2, 3):
            full += [(far_pair, 0), (far_pair, stride)]
        return full

    def score(rows, keys):
        return lax.dot_general(
            rows, keys, (((1,), (1,)), ((), ())), preferred_element_type=jnp.float32
        ) * scale

    def run(variant):
        for start in range(0, tokens, tile):
            rows = queries[start : start + tile, :]
            parts = []
            seen = start + tile
            scores = score(rows, pair[:seen, :HEAD_DIM])
            q_pos = start + lax.broadcasted_iota(jnp.int32, (tile, seen), 0)
            k_pos = lax.broadcasted_iota(jnp.int32, (tile, seen), 1)
            parts.append((jnp.where(k_pos <= q_pos, scores, -1e30), pair[:seen, HEAD_DIM:]))
            for ref, offset in pieces(variant):
                parts.append(
                    (
                        score(rows, ref[offset : offset + tokens, :HEAD_DIM]),
                        ref[offset : offset + tokens, HEAD_DIM:],
                    )
                )
            for m in range(beacons):
                source = big ^ (m + 1)
                count = beacon_refs[m].shape[0]
                live = jnp.where(source < big, tokens // ratios[source], 0)
                local = lax.broadcasted_iota(jnp.int32, (tile, count), 1) % slots
                scores = score(rows, beacon_refs[m][:, :HEAD_DIM])
                parts.append((jnp.where(local < live, scores, -1e30), beacon_refs[m][:, HEAD_DIM:]))
            top = functools.reduce(
                jnp.maximum, [jnp.max(s, axis=1, keepdims=True) for s, _ in parts]
            )
            total = jnp.zeros((tile, 1), jnp.float32)
            mixed = jnp.zeros((tile, HEAD_DIM), jnp.float32)
            for scores, values in parts:
                weights = jnp.exp(scores - top)
                total += jnp.sum(weights, axis=1, keepdims=True)
                mixed += jnp.dot(
                    weights.astype(jnp.bfloat16), values, preferred_element_type=jnp.float32
                )
            out[start : start + tile, :] = (mixed / total).astype(jnp.bfloat16)

    for variant in range(SPLIT):
        pl.when(place == variant)(functools.partial(run, variant))


def attend(info, ratios, queries, pair, far_pair, beacons):
    tokens, cols = queries.shape
    heads = cols // HEAD_DIM
    keys = 4 * tokens + sum(b.shape[0] for b in beacons)
    return pl.pallas_call(
        functools.partial(attend_kernel, tokens, len(beacons)),
        grid=(heads,),
        out_shape=jax.ShapeDtypeStruct((tokens, cols), jnp.bfloat16),
        in_specs=[
            smem(),
            smem(),
            pl.BlockSpec((tokens, HEAD_DIM), lambda i: (0, i)),
            vmem(),
            vmem(),
        ]
        + [vmem()] * len(beacons),
        out_specs=pl.BlockSpec((tokens, HEAD_DIM), lambda i: (0, i)),
        compiler_params=params(),
        cost_estimate=pl.CostEstimate(
            flops=4 * tokens * keys * cols,
            bytes_accessed=4 * tokens * cols,
            transcendentals=tokens * keys * heads,
        ),
        name="attend",
    )(info, ratios, queries, pair, far_pair, *beacons)


def out_kernel(core_flip, info, attention, weights, out):
    width = out.shape[2]
    for j in range(2):
        group = 2 * (info[1] ^ j) + (info[7] ^ core_flip)
        block = weights[pl.ds(pl.multiple_of(group * width, 16), width), :]
        out[j] = lax.dot_general(
            attention[...], block, (((1,), (1,)), ((), ())), preferred_element_type=jnp.float32
        ).astype(jnp.bfloat16)


def out_project(core_flip, info, attention, weights):
    tokens, depth = attention.shape
    width = weights.shape[0] // KVH
    return pl.pallas_call(
        functools.partial(out_kernel, core_flip),
        out_shape=jax.ShapeDtypeStruct((2, tokens, width), jnp.bfloat16),
        in_specs=[smem(), vmem(), vmem()],
        out_specs=vmem(),
        compiler_params=params(),
        cost_estimate=pl.CostEstimate(
            flops=4 * tokens * width * depth, bytes_accessed=4 * width * depth, transcendentals=0
        ),
        name="out_project",
    )(info, attention, weights)


def gather_pieces(shard, n_seq):
    other = send(
        shard, n_seq, lambda big, l, x, y, c: (big, 1 - l, x, y, c) if c != l else None
    )
    near = [jnp.concatenate([shard, other], axis=0)]
    bit = 1
    while bit < n_seq // SPLIT:
        near += [
            send(
                piece,
                n_seq,
                lambda big, l, x, y, c: (big ^ bit, l, x, y, c) if c == l else None,
            )
            for piece in near
        ]
        bit *= 2
    across = [
        send(piece, n_seq, lambda big, l, x, y, c: (big, l, 1 - x, y, c) if c == l else None)
        for piece in near
    ]
    own = near + across
    copied = [
        send(piece, n_seq, lambda big, l, x, y, c: (big, l, x, y, 1 - c) if c == l else None)
        for piece in own
    ]
    return own, copied


def on_device(
    hidden,
    norm_gain,
    query_weight,
    query_bias,
    keyval_weight,
    keyval_bias,
    beacon_weight,
    beacon_bias,
    out_weight,
    ratios,
):
    n_seq = lax.axis_size("seq")
    rows_dev = hidden.shape[0]
    half = rows_dev // 2
    seq_index = lax.axis_index("seq")
    head_index = lax.axis_index("head")
    big, l, x = seq_index // 4, (seq_index // 2) % 2, seq_index % 2
    y, c = head_index // 2, head_index % 2
    matched = c == l
    segment_ids = jnp.arange(ratios.shape[0], dtype=jnp.int32)
    own_ratio = jnp.sum(jnp.where(segment_ids == big, ratios, 0))
    info = jnp.stack(
        [matched.astype(jnp.int32), y, own_ratio, rows_dev // own_ratio, big, l, x, c]
    ).astype(jnp.int32)

    own_half = lax.dynamic_slice_in_dim(hidden, y * half, half, 0)
    first = send(
        own_half, n_seq, lambda big, l, x, y, c: (big, 1 - l, x, y, 1 - c) if c != l else None
    )
    second = send(first, n_seq, lambda big, l, x, y, c: (big, l, x, 1 - y, c) if c != l else None)

    kv_cols = 2 * keyval_weight.shape[2]
    depth = keyval_weight.shape[0]
    small = jnp.concatenate(
        [keyval_weight.reshape(depth, kv_cols), beacon_weight.reshape(depth, kv_cols)], axis=1
    )
    biases = jnp.concatenate([query_bias, keyval_bias.reshape(-1), beacon_bias.reshape(-1)])
    other_biases = send(biases, n_seq, lambda big, l, x, y, c: (big, l, x, y, 1 - c))
    biases = jnp.where(matched, biases, other_biases)
    query_cols = query_weight.shape[1]

    small_own, small_copied = gather_pieces(small, n_seq)
    query_own, query_copied = gather_pieces(query_weight, n_seq)
    out_rows = lax.all_gather(out_weight.T, "seq", axis=0, tiled=True)

    normed, pooled = norm_and_pool(info, hidden, first, second, norm_gain)
    slots_dev = rows_dev // R_MIN
    keyval = project(
        keyval_kernel,
        rows_dev + slots_dev,
        kv_cols,
        info,
        [normed, pooled],
        biases[query_cols:],
        small_own,
        small_copied,
    )
    beside = send(keyval, n_seq, lambda big, l, x, y, c: (big, l, 1 - x, y, c))
    pair = jnp.concatenate([keyval, beside], axis=0)
    far_pair = send(pair, n_seq, lambda big, l, x, y, c: (big, l, x, y, 1 - c))
    stride = rows_dev + slots_dev
    beacons = [
        jnp.concatenate(
            [
                pair[rows_dev:stride],
                pair[stride + rows_dev :],
                far_pair[rows_dev:stride],
                far_pair[stride + rows_dev :],
            ],
            axis=0,
        )
    ]
    bit = 1
    while bit < n_seq // SPLIT:
        beacons += [
            send(piece, n_seq, lambda big, l, x, y, c: (big ^ bit, l, x, y, c)) for piece in beacons
        ]
        bit *= 2
    query = project(
        query_kernel,
        rows_dev,
        query_cols,
        info,
        [normed],
        biases[:query_cols],
        query_own,
        query_copied,
    )
    attention = attend(info, ratios, query, pair, far_pair, beacons[1:])
    swapped = send(
        attention, n_seq, lambda big, l, x, y, c: (big, 1 - l, x, y, 1 - c) if c != l else None
    )
    attention = jnp.where(matched, attention, swapped)

    away = out_project(1, info, attention, out_rows)
    from_core = send(away, n_seq, lambda big, l, x, y, c: (big, l, x, y, 1 - c))
    kept = out_project(0, info, attention, out_rows)
    sums = kept.astype(jnp.float32) + from_core.astype(jnp.float32)
    from_y = send(
        sums[1].astype(jnp.bfloat16), n_seq, lambda big, l, x, y, c: (big, l, x, 1 - y, c)
    )
    return (sums[0] + from_y.astype(jnp.float32)).astype(jnp.bfloat16)


def solution(mesh):
    return jax.shard_map(
        on_device,
        mesh=mesh,
        in_specs=(
            P("seq", None),
            P(),
            P("seq", "head"),
            P("head"),
            P("seq", None, "head"),
            P(None, "head"),
            P("seq", None, "head"),
            P(None, "head"),
            P("head", "seq"),
            P(),
        ),
        out_specs=P("seq", "head"),
        check_vma=False,
    )
```

time: 385 us -> 329 us (0.85)
  starting transfers between devices: 11.7 us -> 72.6 us
  matrix products: 53.6 us -> 0 us
  waiting for transfers between devices: 229 us -> 177 us
  Pallas kernels: 0 us -> 44 us
  blocking collectives: 32 us -> 0 us
  other arithmetic: 22.7 us -> 6.99 us
  local copies, waits for them, and re-layouts: 18.6 us -> 9.56 us
    all_gather x4 -> x1, waiting for transfers between devices: 187 us -> 0.01 us  [on_device(): out_rows = lax.all_gather(out_weight.T, 'seq', axis=0, tiled=True)]
    ppermute x3 -> x25, waiting for transfers between devices: 0.01 us -> 176 us  [send(): return lax.ppermute(value, AXES, moves(n_seq, rule))]
    ppermute x3 -> x25, starting transfers between devices: 11.6 us -> 72.6 us  [send(): return lax.ppermute(value, AXES, moves(n_seq, rule))]
    dot_general x8 -> x0, matrix products: 53.6 us -> none  [the longest x2 15.9 us: update_state(): jnp.einsum('kgtu,ukd->kgtd', weights.astype(jnp.bfloat16), value_heads, p...]
    pallas_call x0 -> x6, Pallas kernels: none -> 44 us  [the longest x2 16.3 us: project(): pl.pallas_call(functools.partial(kernel, count), out_shape=jax.ShapeDtype...]
    unnamed x6 -> x1, waiting for transfers between devices: 42.2 us -> 0.71 us
    all_gather x1 -> x0, blocking collectives: 32 us -> none  [on_device(): shard_rows = lax.all_gather(beacon, 'seq', axis=0, tiled=True)]
    reduce_sum x5 -> x1, other arithmetic: 19.5 us -> 0.71 us  [on_device(): own_ratio = jnp.sum(jnp.where(segment_ids == big, ratios, 0))]
  transfers between devices with their start and end apart: 8 -> 26, of which waited for: 5 -> 10; matrix products, arithmetic and copies ran while one was open for 20% -> 3% of each run, Pallas kernels for 0% -> 11%
where the time goes in v1:
time: 329 us; the launch traced here: 326 us
  waiting for transfers between devices  177 us (54%)
  starting transfers between devices  72.6 us (22%)
  Pallas kernels  44 us (13%)
  between operations  16.1 us (5%)
  local copies, waits for them, and re-layouts  9.56 us (3%)
  other arithmetic  6.99 us (2%)
    ppermute x25, waiting for transfers between devices, send(): return lax.ppermute(value, AXES, moves(n_seq, rule))  176 us
    ppermute x25, starting transfers between devices, send(): return lax.ppermute(value, AXES, moves(n_seq, rule))  72.6 us
    pallas_call x2, Pallas kernels, project(): pl.pallas_call(functools.partial(kernel, count), out_shape=jax.ShapeDtype...  16.3 us
    pallas_call x2, Pallas kernels, out_project(): pl.pallas_call(functools.partial(out_kernel, core_flip), out_shape=jax.Sh...  13.5 us
    pallas_call x1, Pallas kernels, attend(): pl.pallas_call(functools.partial(attend_kernel, tokens, len(beacons)), gr...  8.76 us
  transfers between devices with their start and end apart: 26, of which 10 were waited for; matrix products, arithmetic and copies ran while one was open for 3% of the time, Pallas kernels for 11%

profile of v1, /device:TPU:0, one launch (start us, length us, event | category | flops | bytes accessed | tf_op | source)
XLA Modules:
  0.0 326.4 jit_solution(13404103525617460843)
XLA Ops:
  6.5 0.7 all-gather.2.cloned.1.call-update
  7.3 1.3 collective-permute-start.3
  8.6 1.7 constant_dynamic-slice_fusion
  10.3 1.9 collective-permute-start
  12.3 1.3 collective-permute-start.11
  13.8 8.1 %collective-permute-done.3 = bf16[448,896]{1,0:T(8,128)(2,1)S(1)} collective-permute-done((bf16[448,896]{1,0:T(8,128)(2,1)}, bf16[448,896]{1,0:T(8,128)(2,1)S(1)}, u32[]{:S(2)}, u32[]{:S(2)}) %collective-permute-start.3) | collective-permute-done | bytes 802848 | tf_op jit(solution)/shard_map/ppermute | solution.py:48
  22.0 5.6 %collective-permute-start.4 = (bf16[896,896]{1,0:T(8,128)(2,1)S(1)}, bf16[896,896]{1,0:T(8,128)(2,1)}, u32[]{:S(2)}, u32[]{:S(2)}) collective-permute-start(bf16[896,896]{1,0:T(8,128)(2,1)S(1)} %constant_dynamic-update-slice_fusion.rest_0_), channel_id=1, source_target_pairs={{0,16},{2,18},{4,20},{6,22},{9,25},{11,27},{13,29},{15,31},{16,0},... | collective-permute-start | bytes 4816904 | tf_op jit(solution)/shard_map/ppermute | solution.py:48
  27.6 92.4 %collective-permute-done.11 = bf16[448,512]{1,0:T(8,128)(2,1)S(1)} collective-permute-done((bf16[448,512]{1,0:T(8,128)(2,1)S(1)}, bf16[448,512]{1,0:T(8,128)(2,1)S(1)}, u32[]{:S(2)}, u32[]{:S(2)}) %collective-permute-start.11) | collective-permute-done | bytes 458784 | tf_op jit(solution)/shard_map/ppermute | solution.py:48
  120.1 1.9 collective-permute-start.12
  122.0 11.0 %collective-permute-start.13 = (bf16[896,512]{1,0:T(8,128)(2,1)S(1)}, bf16[896,512]{1,0:T(8,128)(2,1)}, u32[]{:S(2)}, u32[]{:S(2)}) collective-permute-start(bf16[896,512]{1,0:T(8,128)(2,1)S(1)} %pad_maximum_fusion.rest_0_), channel_id=1, source_target_pairs={{0,4},{2,6},{4,0},{6,2},{9,13},{11,15},{13,9},{15,11},{16,20},{18,... | collective-permute-start | bytes 2752520 | tf_op jit(solution)/shard_map/ppermute | solution.py:48
  133.1 1.2 collective-permute-done.2
  134.3 2.1 collective-permute-start.15
  136.4 23.3 %collective-permute-done.12.rest_1_ = bf16[896,512]{1,0:T(8,128)(2,1)S(1)} collective-permute-done((bf16[896,512]{1,0:T(8,128)(2,1)S(1)}, bf16[896,512]{1,0:T(8,128)(2,1)S(1)}, u32[]{:S(2)}, u32[]{:S(2)}) %collective-permute-start.12) | collective-permute-done | bytes 917536 | tf_op jit(solution)/shard_map/ppermute | solution.py:48
  159.7 3.4 %collective-permute-start.14 = (bf16[896,512]{1,0:T(8,128)(2,1)S(1)}, bf16[896,512]{1,0:T(8,128)(2,1)}, u32[]{:S(2)}, u32[]{:S(2)}) collective-permute-start(bf16[896,512]{1,0:T(8,128)(2,1)S(1)} %collective-permute-done.12.rest_1_), channel_id=1, source_target_pairs={{0,4},{2,6},{4,0},{6,2},{9,13},{11,15},{13,9},{15,11},{16,20},{18,... | collective-permute-start | bytes 2752520 | tf_op jit(solution)/shard_map/ppermute | solution.py:48
  163.1 1.9 collective-permute-start.1
  165.1 2.4 collective-permute-start.5
  167.5 3.4 %collective-permute-start.6 = (bf16[896,896]{1,0:T(8,128)(2,1)}, bf16[896,896]{1,0:T(8,128)(2,1)}, u32[]{:S(2)}, u32[]{:S(2)}) collective-permute-start(bf16[896,896]{1,0:T(8,128)(2,1)} %collective-permute-done.4.rest_1_), channel_id=1, source_target_pairs={{0,4},{2,6},{4,0},{6,2},{9,13},{11,15},{13,9},{15,11},{16,20},{18,... | collective-permute-start | bytes 4816904 | tf_op jit(solution)/shard_map/ppermute | solution.py:48
  171.0 1.3 collective-permute-start.16
  172.3 2.8 collective-permute-done.14.rest_3_
  175.1 2.2 collective-permute-start.17
  177.3 0.9 copy-done.6
  178.3 2.3 collective-permute-start.18
  180.6 0.7 fusion.3
  184.0 1.4 stack.39.info
  185.4 1.4 collective-permute-start.7
  186.7 5.5 %collective-permute-done.5.rest_2_ = bf16[896,896]{1,0:T(8,128)(2,1)} collective-permute-done((bf16[896,896]{1,0:T(8,128)(2,1)S(1)}, bf16[896,896]{1,0:T(8,128)(2,1)}, u32[]{:S(2)}, u32[]{:S(2)}) %collective-permute-start.5) | collective-permute-done | bytes 1605664 | tf_op jit(solution)/shard_map/ppermute | solution.py:48
  192.3 1.4 collective-permute-start.8
  193.7 2.5 collective-permute-start.9
  196.2 16.5 %collective-permute-done.6.rest_3_ = bf16[896,896]{1,0:T(8,128)(2,1)} collective-permute-done((bf16[896,896]{1,0:T(8,128)(2,1)}, bf16[896,896]{1,0:T(8,128)(2,1)}, u32[]{:S(2)}, u32[]{:S(2)}) %collective-permute-start.6) | collective-permute-done | bytes 1605664 | tf_op jit(solution)/shard_map/ppermute | solution.py:48
  212.6 2.5 collective-permute-start.10
  215.7 5.5 %norm_pool.1 = (bf16[512,3584]{1,0:T(8,128)(2,1)}, bf16[64,3584]{1,0:T(8,128)(2,1)}) custom-call(s32[8]{0:T(128)} %stack.39.info, bf16[512,3584]{1,0:T(8,128)(2,1)} %hidden.1, bf16[256,3584]{1,0:T(8,128)(2,1)} %collective-permute-done.first, bf16[256,3584]{1,0:T(8,128)(2,1)} %collective-permute-done.1.second, f32[1,3584]{1,0:T(1,128)} %reshape.22.gain), custom_call_target="tpu_custom_call" | custom-call | flops 234881024 | bytes 7340032 | tf_op jit(solution)/shard_map/norm_pool/pallas_call | solution.py:99
  221.3 6.4 %project.3 = bf16[576,256]{1,0:T(8,128)(2,1)} custom-call(s32[8]{0:T(128)} %stack.39.info, bf16[512,3584]{1,0:T(8,128)(2,1)} %get-tuple-element.7.normed, bf16[64,3584]{1,0:T(8,128)(2,1)} %get-tuple-element.8.pooled, f32[1,512]{1,0:T(1,128)} %bitcast.29, bf16[896,512]{1,0:T(8,128)(2,1)} %copy-done, bf16[896,512]{1,0:T(8,128)(2,1)} %copy-done.4, ...), custom_call_target="tpu_custom_call" | custom-call | flops 1056964608 | bytes 7798784 | tf_op jit(solution)/shard_map/project/pallas_call | solution.py:171
  227.7 1.6 collective-permute-start.19
  229.3 5.4 %collective-permute-done.19 = bf16[576,256]{1,0:T(8,128)(2,1)S(1)} collective-permute-done((bf16[576,256]{1,0:T(8,128)(2,1)}, bf16[576,256]{1,0:T(8,128)(2,1)S(1)}, u32[]{:S(2)}, u32[]{:S(2)}) %collective-permute-start.19) | collective-permute-done | bytes 294944 | tf_op jit(solution)/shard_map/ppermute | solution.py:48
  234.7 1.0 pad_maximum_fusion.1.pair
  235.8 0.7 reshape.25.bias
  236.5 0.8 slice.35
  238.0 1.2 copy-done.2
  239.8 9.8 %project.2.queries = bf16[512,896]{1,0:T(8,128)(2,1)} custom-call(s32[8]{0:T(128)} %stack.39.info, bf16[512,3584]{1,0:T(8,128)(2,1)} %get-tuple-element.7.normed, f32[1,896]{1,0:T(1,128)} %reshape.25.bias, bf16[896,896]{1,0:T(8,128)(2,1)} %copy-done.1, bf16[896,896]{1,0:T(8,128)(2,1)} %collective-permute-done.4.rest_1_, ...), custom_call_target="tpu_custom_call" | custom-call | flops 3288334336 | bytes 10092544 | tf_op jit(solution)/shard_map/project/pallas_call | solution.py:171
  250.3 8.8 %attend.1 = bf16[512,896]{1,0:T(8,128)(2,1)} custom-call(s32[8]{0:T(128)} %stack.39.info, s32[2]{0:T(128)} %ratios.1, bf16[512,896]{1,0:T(8,128)(2,1)} %project.2.queries, bf16[1152,256]{1,0:T(8,128)(2,1)} %copy-done.8, bf16[1152,256]{1,0:T(8,128)(2,1)} %copy-done.13, bf16[256,256]{1,0:T(8,128)(2,1)} %copy-done.16), custom_call_target="tpu_custom_call" | custom-call | flops 4227858432 | bytes 1835008 | tf_op jit(solution)/shard_map/attend/pallas_call | solution.py:256
  259.8 2.2 broadcast_select_fusion.attention
  262.0 6.8 %out_project.3 = bf16[2,512,896]{2,1,0:T(8,128)(2,1)} custom-call(s32[8]{0:T(128)} %stack.39.info, bf16[512,896]{1,0:T(8,128)(2,1)} %broadcast_select_fusion.attention, bf16[3584,896]{1,0:T(8,128)(2,1)} %all-gather.2.cloned.1.call-done.weights), custom_call_target="tpu_custom_call" | custom-call | flops 1644167168 | bytes 3211264 | tf_op jit(solution)/shard_map/out_project/pallas_call | solution.py:292
  268.8 18.6 %collective-permute-start.23 = (bf16[2,512,896]{2,1,0:T(8,128)(2,1)}, bf16[2,512,896]{2,1,0:T(8,128)(2,1)S(1)}, u32[]{:S(2)}, u32[]{:S(2)}) collective-permute-start(bf16[2,512,896]{2,1,0:T(8,128)(2,1)} %out_project.3), channel_id=1, source_target_pairs={{0,1},{1,0},{2,3},{3,2},{4,5},{5,4},{6,7},{7,6},{8,9},{9,8},{10,11... | collective-permute-start | bytes 5505032 | tf_op jit(solution)/shard_map/ppermute | solution.py:48
  287.4 6.7 %out_project.2 = bf16[2,512,896]{2,1,0:T(8,128)(2,1)} custom-call(s32[8]{0:T(128)} %stack.39.info, bf16[512,896]{1,0:T(8,128)(2,1)} %broadcast_select_fusion.attention, bf16[3584,896]{1,0:T(8,128)(2,1)} %all-gather.2.cloned.1.call-done.weights), custom_call_target="tpu_custom_call" | custom-call | flops 1644167168 | bytes 3211264 | tf_op jit(solution)/shard_map/out_project/pallas_call | solution.py:292
  294.1 1.9 convert_add_fusion
  296.1 1.6 collective-permute-start.24
  297.7 20.7 %collective-permute-done.24 = bf16[512,896]{1,0:T(8,128)(2,1)S(1)} collective-permute-done((bf16[512,896]{1,0:T(8,128)(2,1)S(1)}, bf16[512,896]{1,0:T(8,128)(2,1)S(1)}, u32[]{:S(2)}, u32[]{:S(2)}) %collective-permute-start.24) | collective-permute-done | bytes 917536 | tf_op jit(solution)/shard_map/ppermute | solution.py:48
  318.4 1.1 fusion.1
  (70 shorter events, 4.5 us)
Async XLA Ops:
  6.5 255.5 %all-gather.2.cloned.1.call-start = ((), (), s32[]{:S(2)}) async-start(), calls=%async_computation | async-start | bytes 7225344 | tf_op jit(solution)/shard_map/all_gather | solution.py:377
  7.3 14.7 %collective-permute-start.3 = (bf16[448,896]{1,0:T(8,128)(2,1)}, bf16[448,896]{1,0:T(8,128)(2,1)S(1)}, u32[]{:S(2)}, u32[]{:S(2)}) collective-permute-start(bf16[448,896]{1,0:T(8,128)(2,1)} %param.12), channel_id=1, source_target_pairs={{1,9},{3,11},{5,13},{7,15},{8,0},{10,2},{12,4},{14,6},{17,25},{19,... | collective-permute-start | bytes 2408456 | tf_op jit(solution)/shard_map/ppermute | solution.py:48
  8.6 3.7 %copy-start.9 = (bf16[448,2,128]{2,1,0:T(2,128)(2,1)S(1)}, bf16[448,2,128]{2,1,0:T(2,128)(2,1)}, u32[]{:S(2)}) copy-start(bf16[448,2,128]{2,1,0:T(2,128)(2,1)} %param.14) | copy-start | bytes 688132
  8.6 3.7 %copy-start.10 = (bf16[448,2,128]{2,1,0:T(2,128)(2,1)S(1)}, bf16[448,2,128]{2,1,0:T(2,128)(2,1)}, u32[]{:S(2)}) copy-start(bf16[448,2,128]{2,1,0:T(2,128)(2,1)} %param.16) | copy-start | bytes 688132
  8.6 5.0 %copy-start.7 = (bf16[448,896]{1,0:T(8,128)(2,1)S(1)}, bf16[448,896]{1,0:T(8,128)(2,1)}, u32[]{:S(2)}) copy-start(bf16[448,896]{1,0:T(8,128)(2,1)} %param.12) | copy-start | bytes 2408452
  10.3 152.8 %collective-permute-start = (bf16[256,3584]{1,0:T(8,128)(2,1)S(1)}, bf16[256,3584]{1,0:T(8,128)(2,1)}, u32[]{:S(2)}, u32[]{:S(2)}) collective-permute-start(bf16[256,3584]{1,0:T(8,128)(2,1)S(1)} %constant_dynamic-slice_fusion), channel_id=1, source_target_pairs={{1,8},{3,10},{5,12},{7,14},{8,1},{10,3},{12,5},{14,7},{17,24},{19,... | collective-permute-start | bytes 5505032 | tf_op jit(solution)/shard_map/ppermute | solution.py:48
  12.3 107.7 %collective-permute-start.11 = (bf16[448,512]{1,0:T(8,128)(2,1)S(1)}, bf16[448,512]{1,0:T(8,128)(2,1)S(1)}, u32[]{:S(2)}, u32[]{:S(2)}) collective-permute-start(bf16[448,512]{1,0:T(8,128)(2,1)S(1)} %bitcast_dynamic-update-slice_fusion), channel_id=1, source_target_pairs={{1,9},{3,11},{5,13},{7,15},{8,0},{10,2},{12,4},{14,6},{17,25},{19,... | collective-permute-start | bytes 1376264 | tf_op jit(solution)/shard_map/ppermute | solution.py:48
  13.7 119.3 %copy-start.11 = (f32[896]{0:T(1024)S(1)}, f32[896]{0:T(1024)}, u32[]{:S(2)}) copy-start(f32[896]{0:T(1024)} %param.13) | copy-start | bytes 10756
  13.7 119.3 %copy-start.14 = (f32[2,128]{1,0:T(2,128)S(1)}, f32[2,128]{1,0:T(2,128)}, u32[]{:S(2)}) copy-start(f32[2,128]{1,0:T(2,128)} %param.17) | copy-start | bytes 3076
  13.7 119.3 %copy-start.15 = (f32[2,128]{1,0:T(2,128)S(1)}, f32[2,128]{1,0:T(2,128)}, u32[]{:S(2)}) copy-start(f32[2,128]{1,0:T(2,128)} %param.15) | copy-start | bytes 3076
  13.7 166.8 %copy-start.17 = (s32[2]{0:T(128)S(1)}, s32[2]{0:T(128)}, u32[]{:S(2)}) copy-start(s32[2]{0:T(128)} %ratios.1) | copy-start | bytes 28
  13.7 169.6 %copy-start.12 = (f32[3584]{0:T(1024)S(1)}, f32[3584]{0:T(1024)}, u32[]{:S(2)}) copy-start(f32[3584]{0:T(1024)} %param.11) | copy-start | bytes 43012
  22.0 199.2 %copy-start.1 = (bf16[896,896]{1,0:T(8,128)(2,1)}, bf16[896,896]{1,0:T(8,128)(2,1)S(1)}, u32[]{:S(2)}) copy-start(bf16[896,896]{1,0:T(8,128)(2,1)S(1)} %constant_dynamic-update-slice_fusion.rest_0_) | copy-start | bytes 4816900
  22.0 145.4 %collective-permute-start.4 = (bf16[896,896]{1,0:T(8,128)(2,1)S(1)}, bf16[896,896]{1,0:T(8,128)(2,1)}, u32[]{:S(2)}, u32[]{:S(2)}) collective-permute-start(bf16[896,896]{1,0:T(8,128)(2,1)S(1)} %constant_dynamic-update-slice_fusion.rest_0_), channel_id=1, source_target_pairs={{0,16},{2,18},{4,20},{6,22},{9,25},{11,27},{13,29},{15,31},{16,0},... | collective-permute-start | bytes 4816904 | tf_op jit(solution)/shard_map/ppermute | solution.py:48
  120.1 101.2 %copy-start = (bf16[896,512]{1,0:T(8,128)(2,1)}, bf16[896,512]{1,0:T(8,128)(2,1)S(1)}, u32[]{:S(2)}) copy-start(bf16[896,512]{1,0:T(8,128)(2,1)S(1)} %pad_maximum_fusion.rest_0_) | copy-start | bytes 2752516
  120.1 39.6 %collective-permute-start.12 = (bf16[896,512]{1,0:T(8,128)(2,1)S(1)}, bf16[896,512]{1,0:T(8,128)(2,1)S(1)}, u32[]{:S(2)}, u32[]{:S(2)}) collective-permute-start(bf16[896,512]{1,0:T(8,128)(2,1)S(1)} %pad_maximum_fusion.rest_0_), channel_id=1, source_target_pairs={{0,16},{2,18},{4,20},{6,22},{9,25},{11,27},{13,29},{15,31},{16,0},... | collective-permute-start | bytes 2752520 | tf_op jit(solution)/shard_map/ppermute | solution.py:48
  122.0 43.1 %collective-permute-start.13 = (bf16[896,512]{1,0:T(8,128)(2,1)S(1)}, bf16[896,512]{1,0:T(8,128)(2,1)}, u32[]{:S(2)}, u32[]{:S(2)}) collective-permute-start(bf16[896,512]{1,0:T(8,128)(2,1)S(1)} %pad_maximum_fusion.rest_0_), channel_id=1, source_target_pairs={{0,4},{2,6},{4,0},{6,2},{9,13},{11,15},{13,9},{15,11},{16,20},{18,... | collective-permute-start | bytes 2752520 | tf_op jit(solution)/shard_map/ppermute | solution.py:48
  133.1 1.2 collective-permute-start.2
  134.3 36.6 %collective-permute-start.15 = (bf16[896,512]{1,0:T(8,128)(2,1)S(1)}, bf16[896,512]{1,0:T(8,128)(2,1)S(1)}, u32[]{:S(2)}, u32[]{:S(2)}) collective-permute-start(bf16[896,512]{1,0:T(8,128)(2,1)S(1)} %pad_maximum_fusion.rest_0_), channel_id=1, source_target_pairs={{0,1},{2,3},{4,5},{6,7},{9,8},{11,10},{13,12},{15,14},{16,17},{18,... | collective-permute-start | bytes 2752520 | tf_op jit(solution)/shard_map/ppermute | solution.py:48
  159.7 61.6 %copy-start.4 = (bf16[896,512]{1,0:T(8,128)(2,1)}, bf16[896,512]{1,0:T(8,128)(2,1)S(1)}, u32[]{:S(2)}) copy-start(bf16[896,512]{1,0:T(8,128)(2,1)S(1)} %collective-permute-done.12.rest_1_) | copy-start | bytes 2752516
  159.7 15.4 %collective-permute-start.14 = (bf16[896,512]{1,0:T(8,128)(2,1)S(1)}, bf16[896,512]{1,0:T(8,128)(2,1)}, u32[]{:S(2)}, u32[]{:S(2)}) collective-permute-start(bf16[896,512]{1,0:T(8,128)(2,1)S(1)} %collective-permute-done.12.rest_1_), channel_id=1, source_target_pairs={{0,4},{2,6},{4,0},{6,2},{9,13},{11,15},{13,9},{15,11},{16,20},{18,... | collective-permute-start | bytes 2752520 | tf_op jit(solution)/shard_map/ppermute | solution.py:48
  163.1 30.5 %collective-permute-start.1 = (bf16[256,3584]{1,0:T(8,128)(2,1)}, bf16[256,3584]{1,0:T(8,128)(2,1)}, u32[]{:S(2)}, u32[]{:S(2)}) collective-permute-start(bf16[256,3584]{1,0:T(8,128)(2,1)} %collective-permute-done.first), channel_id=1, source_target_pairs={{1,3},{3,1},{5,7},{7,5},{8,10},{10,8},{12,14},{14,12},{17,19},{19,... | collective-permute-start | bytes 5505032 | tf_op jit(solution)/shard_map/ppermute | solution.py:48
  165.1 27.2 %collective-permute-start.5 = (bf16[896,896]{1,0:T(8,128)(2,1)S(1)}, bf16[896,896]{1,0:T(8,128)(2,1)}, u32[]{:S(2)}, u32[]{:S(2)}) collective-permute-start(bf16[896,896]{1,0:T(8,128)(2,1)S(1)} %constant_dynamic-update-slice_fusion.rest_0_), channel_id=1, source_target_pairs={{0,4},{2,6},{4,0},{6,2},{9,13},{11,15},{13,9},{15,11},{16,20},{18,... | collective-permute-start | bytes 4816904 | tf_op jit(solution)/shard_map/ppermute | solution.py:48
  167.5 45.2 %collective-permute-start.6 = (bf16[896,896]{1,0:T(8,128)(2,1)}, bf16[896,896]{1,0:T(8,128)(2,1)}, u32[]{:S(2)}, u32[]{:S(2)}) collective-permute-start(bf16[896,896]{1,0:T(8,128)(2,1)} %collective-permute-done.4.rest_1_), channel_id=1, source_target_pairs={{0,4},{2,6},{4,0},{6,2},{9,13},{11,15},{13,9},{15,11},{16,20},{18,... | collective-permute-start | bytes 4816904 | tf_op jit(solution)/shard_map/ppermute | solution.py:48
  171.0 6.4 %copy-start.5 = (bf16[896,512]{1,0:T(8,128)(2,1)}, bf16[896,512]{1,0:T(8,128)(2,1)S(1)}, u32[]{:S(2)}) copy-start(bf16[896,512]{1,0:T(8,128)(2,1)S(1)} %collective-permute-done.15.rest_4_) | copy-start | bytes 2752516
  171.0 6.3 %collective-permute-start.16 = (bf16[896,512]{1,0:T(8,128)(2,1)S(1)}, bf16[896,512]{1,0:T(8,128)(2,1)S(1)}, u32[]{:S(2)}, u32[]{:S(2)}) collective-permute-start(bf16[896,512]{1,0:T(8,128)(2,1)S(1)} %collective-permute-done.12.rest_1_), channel_id=1, source_target_pairs={{0,1},{2,3},{4,5},{6,7},{9,8},{11,10},{13,12},{15,14},{16,17},{18,... | collective-permute-start | bytes 2752520 | tf_op jit(solution)/shard_map/ppermute | solution.py:48
  175.1 10.3 %collective-permute-start.17 = (bf16[896,512]{1,0:T(8,128)(2,1)}, bf16[896,512]{1,0:T(8,128)(2,1)}, u32[]{:S(2)}, u32[]{:S(2)}) collective-permute-start(bf16[896,512]{1,0:T(8,128)(2,1)} %collective-permute-done.13.rest_2_), channel_id=1, source_target_pairs={{0,1},{2,3},{4,5},{6,7},{9,8},{11,10},{13,12},{15,14},{16,17},{18,... | collective-permute-start | bytes 2752520 | tf_op jit(solution)/shard_map/ppermute | solution.py:48
  177.3 0.9 copy-start.6
  178.3 43.0 %collective-permute-start.18 = (bf16[896,512]{1,0:T(8,128)(2,1)}, bf16[896,512]{1,0:T(8,128)(2,1)}, u32[]{:S(2)}, u32[]{:S(2)}) collective-permute-start(bf16[896,512]{1,0:T(8,128)(2,1)} %collective-permute-done.14.rest_3_), channel_id=1, source_target_pairs={{0,1},{2,3},{4,5},{6,7},{9,8},{11,10},{13,12},{15,14},{16,17},{18,... | collective-permute-start | bytes 2752520 | tf_op jit(solution)/shard_map/ppermute | solution.py:48
  185.4 52.6 %collective-permute-start.7 = (bf16[896,896]{1,0:T(8,128)(2,1)S(1)}, bf16[896,896]{1,0:T(8,128)(2,1)S(1)}, u32[]{:S(2)}, u32[]{:S(2)}) collective-permute-start(bf16[896,896]{1,0:T(8,128)(2,1)S(1)} %constant_dynamic-update-slice_fusion.rest_0_), channel_id=1, source_target_pairs={{0,1},{2,3},{4,5},{6,7},{9,8},{11,10},{13,12},{15,14},{16,17},{18,... | collective-permute-start | bytes 4816904 | tf_op jit(solution)/shard_map/ppermute | solution.py:48
  192.3 45.7 %collective-permute-start.8 = (bf16[896,896]{1,0:T(8,128)(2,1)}, bf16[896,896]{1,0:T(8,128)(2,1)S(1)}, u32[]{:S(2)}, u32[]{:S(2)}) collective-permute-start(bf16[896,896]{1,0:T(8,128)(2,1)} %collective-permute-done.4.rest_1_), channel_id=1, source_target_pairs={{0,1},{2,3},{4,5},{6,7},{9,8},{11,10},{13,12},{15,14},{16,17},{18,... | collective-permute-start | bytes 4816904 | tf_op jit(solution)/shard_map/ppermute | solution.py:48
  193.7 44.3 %collective-permute-start.9 = (bf16[896,896]{1,0:T(8,128)(2,1)}, bf16[896,896]{1,0:T(8,128)(2,1)}, u32[]{:S(2)}, u32[]{:S(2)}) collective-permute-start(bf16[896,896]{1,0:T(8,128)(2,1)} %collective-permute-done.5.rest_2_), channel_id=1, source_target_pairs={{0,1},{2,3},{4,5},{6,7},{9,8},{11,10},{13,12},{15,14},{16,17},{18,... | collective-permute-start | bytes 4816904 | tf_op jit(solution)/shard_map/ppermute | solution.py:48
  212.6 25.3 %collective-permute-start.10 = (bf16[896,896]{1,0:T(8,128)(2,1)}, bf16[896,896]{1,0:T(8,128)(2,1)}, u32[]{:S(2)}, u32[]{:S(2)}) collective-permute-start(bf16[896,896]{1,0:T(8,128)(2,1)} %collective-permute-done.6.rest_3_), channel_id=1, source_target_pairs={{0,1},{2,3},{4,5},{6,7},{9,8},{11,10},{13,12},{15,14},{16,17},{18,... | collective-permute-start | bytes 4816904 | tf_op jit(solution)/shard_map/ppermute | solution.py:48
  227.7 7.0 %collective-permute-start.19 = (bf16[576,256]{1,0:T(8,128)(2,1)}, bf16[576,256]{1,0:T(8,128)(2,1)S(1)}, u32[]{:S(2)}, u32[]{:S(2)}) collective-permute-start(bf16[576,256]{1,0:T(8,128)(2,1)} %project.3), channel_id=1, source_target_pairs={{0,4},{1,5},{2,6},{3,7},{4,0},{5,1},{6,2},{7,3},{8,12},{9,13},{10,... | collective-permute-start | bytes 884744 | tf_op jit(solution)/shard_map/ppermute | solution.py:48
  235.7 13.9 %copy-start.8 = (bf16[1152,256]{1,0:T(8,128)(2,1)}, bf16[1152,256]{1,0:T(8,128)(2,1)S(1)}, u32[]{:S(2)}) copy-start(bf16[1152,256]{1,0:T(8,128)(2,1)S(1)} %pad_maximum_fusion.1.pair) | copy-start | bytes 1769476
  235.7 2.1 collective-permute-start.20
  237.8 11.8 %copy-start.13 = (bf16[1152,256]{1,0:T(8,128)(2,1)}, bf16[1152,256]{1,0:T(8,128)(2,1)S(1)}, u32[]{:S(2)}) copy-start(bf16[1152,256]{1,0:T(8,128)(2,1)S(1)} %collective-permute-done.20.far_pair) | copy-start | bytes 1769476
  237.8 11.8 %collective-permute-start.21 = (bf16[256,256]{1,0:T(8,128)(2,1)S(1)}, bf16[256,256]{1,0:T(8,128)(2,1)S(1)}, u32[]{:S(2)}, u32[]{:S(2)}) collective-permute-start(bf16[256,256]{1,0:T(8,128)(2,1)S(1)} %pad_maximum_fusion.2), channel_id=1, source_target_pairs={{0,16},{1,17},{2,18},{3,19},{4,20},{5,21},{6,22},{7,23},{8,24},{9,... | collective-permute-start | bytes 393224 | tf_op jit(solution)/shard_map/ppermute | solution.py:48
  237.9 1.2 copy-start.2
  237.9 1.8 copy-start.3
  249.7 0.7 copy-start.16
  259.1 0.7 collective-permute-start.22
  268.8 25.3 %collective-permute-start.23 = (bf16[2,512,896]{2,1,0:T(8,128)(2,1)}, bf16[2,512,896]{2,1,0:T(8,128)(2,1)S(1)}, u32[]{:S(2)}, u32[]{:S(2)}) collective-permute-start(bf16[2,512,896]{2,1,0:T(8,128)(2,1)} %out_project.3), channel_id=1, source_target_pairs={{0,1},{1,0},{2,3},{3,2},{4,5},{5,4},{6,7},{7,6},{8,9},{9,8},{10,11... | collective-permute-start | bytes 5505032 | tf_op jit(solution)/shard_map/ppermute | solution.py:48
  296.1 22.3 %collective-permute-start.24 = (bf16[512,896]{1,0:T(8,128)(2,1)S(1)}, bf16[512,896]{1,0:T(8,128)(2,1)S(1)}, u32[]{:S(2)}, u32[]{:S(2)}) collective-permute-start(bf16[512,896]{1,0:T(8,128)(2,1)S(1)} %fusion.2), channel_id=1, source_target_pairs={{0,2},{1,3},{2,0},{3,1},{4,6},{5,7},{6,4},{7,5},{8,10},{9,11},{10,... | collective-permute-start | bytes 2752520 | tf_op jit(solution)/shard_map/ppermute | solution.py:48
Sparse Core Ops, SparseCore 0:
  9.5 139.5 all-gather.1

commit v2 on v1

--- a/solution.py
+++ b/solution.py
@@ -114,33 +114,31 @@
 
 
 def fetch_weights(info, refs, weights, sems, count):
-    matched, big, l, x = info[0], info[4], info[5], info[6]
+    matched, big, l, x, swap = info[0], info[4], info[5], info[6], info[8]
     rows = refs[0].shape[0] // 2
     own, copied = refs[:count], refs[count:]
     half = count // 2
 
-    def spot(i, j):
+    def copy(source, i, j):
         flip, m = i // half, i % half
-        block = 4 * (big ^ m) + 2 * (l ^ j) + (x ^ flip)
-        return weights.at[pl.ds(pl.multiple_of(block * rows, 16), rows), :]
+        place = j if (copied or m == 0) else j ^ swap
+        block = 4 * (big ^ m) + 2 * (l ^ place) + (x ^ flip)
+        return pltpu.make_async_copy(
+            source[i].at[pl.ds(j * rows, rows), :],
+            weights.at[pl.ds(pl.multiple_of(block * rows, 16), rows), :],
+            sems.at[2 * i + j],
+        )
 
     for i in range(count):
         for j in range(2):
-            part = pl.ds(j * rows, rows)
-
-            @pl.when(matched == 1)
-            def _():
-                pltpu.make_async_copy(own[i].at[part, :], spot(i, j), sems.at[2 * i + j]).start()
-
-            @pl.when(matched == 0)
-            def _():
-                pltpu.make_async_copy(copied[i].at[part, :], spot(i, j), sems.at[2 * i + j]).start()
-
+            if copied:
+                pl.when(matched == 1)(copy(own, i, j).start)
+                pl.when(matched == 0)(copy(copied, i, j).start)
+            else:
+                copy(own, i, j).start()
     for i in range(count):
         for j in range(2):
-            pltpu.make_async_copy(
-                own[i].at[pl.ds(j * rows, rows), :], spot(i, j), sems.at[2 * i + j]
-            ).wait()
+            copy(own, i, j).wait()
 
 
 def query_kernel(count, info, normed, bias, *rest):
@@ -187,7 +185,7 @@
     )(info, *left, bias.reshape(1, -1), *own, *copied)
 
 
-def attend_kernel(tokens, beacons, info, ratios, queries, pair, far_pair, *rest):
+def attend_kernel(tokens, beacons, first_row, info, ratios, queries, pair, far_pair, *rest):
     beacon_refs, out = rest[:beacons], rest[beacons]
     place = 2 * info[7] + info[6]
     big = info[4]
@@ -210,7 +208,8 @@
         ) * scale
 
     def run(variant):
-        for start in range(0, tokens, tile):
+        for local_start in range(0, out.shape[0], tile):
+            start = first_row + local_start
             rows = queries[start : start + tile, :]
             parts = []
             seen = start + tile
@@ -243,20 +242,20 @@
                 mixed += jnp.dot(
                     weights.astype(jnp.bfloat16), values, preferred_element_type=jnp.float32
                 )
-            out[start : start + tile, :] = (mixed / total).astype(jnp.bfloat16)
+            out[local_start : local_start + tile, :] = (mixed / total).astype(jnp.bfloat16)
 
     for variant in range(SPLIT):
         pl.when(place == variant)(functools.partial(run, variant))
 
 
-def attend(info, ratios, queries, pair, far_pair, beacons):
+def attend(first_row, row_count, info, ratios, queries, pair, far_pair, beacons):
     tokens, cols = queries.shape
     heads = cols // HEAD_DIM
     keys = 4 * tokens + sum(b.shape[0] for b in beacons)
     return pl.pallas_call(
-        functools.partial(attend_kernel, tokens, len(beacons)),
+        functools.partial(attend_kernel, tokens, len(beacons), first_row),
         grid=(heads,),
-        out_shape=jax.ShapeDtypeStruct((tokens, cols), jnp.bfloat16),
+        out_shape=jax.ShapeDtypeStruct((row_count, cols), jnp.bfloat16),
         in_specs=[
             smem(),
             smem(),
@@ -265,41 +264,49 @@
             vmem(),
         ]
         + [vmem()] * len(beacons),
-        out_specs=pl.BlockSpec((tokens, HEAD_DIM), lambda i: (0, i)),
+        out_specs=pl.BlockSpec((row_count, HEAD_DIM), lambda i: (0, i)),
         compiler_params=params(),
         cost_estimate=pl.CostEstimate(
-            flops=4 * tokens * keys * cols,
+            flops=4 * row_count * keys * cols,
             bytes_accessed=4 * tokens * cols,
-            transcendentals=tokens * keys * heads,
+            transcendentals=row_count * keys * heads,
         ),
         name="attend",
     )(info, ratios, queries, pair, far_pair, *beacons)
 
 
-def out_kernel(core_flip, info, attention, weights, out):
-    width = out.shape[2]
-    for j in range(2):
-        group = 2 * (info[1] ^ j) + (info[7] ^ core_flip)
-        block = weights[pl.ds(pl.multiple_of(group * width, 16), width), :]
-        out[j] = lax.dot_general(
-            attention[...], block, (((1,), (1,)), ((), ())), preferred_element_type=jnp.float32
-        ).astype(jnp.bfloat16)
-
-
-def out_project(core_flip, info, attention, weights):
+def out_kernel(count, info, attention, *rest):
+    refs, (out, weights, sems) = rest[:count], rest[count:]
+    fetch_weights(info, refs, weights, sems, count)
+    width = out.shape[3]
+    for i in (1, 0):
+        for j in (1, 0):
+            group = 2 * (info[1] ^ j) + (info[7] ^ i)
+            block = weights[pl.ds(pl.multiple_of(group * width, 16), width), :]
+            out[i, j] = lax.dot_general(
+                attention[...], block, (((1,), (1,)), ((), ())), preferred_element_type=jnp.float32
+            ).astype(jnp.bfloat16)
+
+
+def out_project(info, attention, pieces):
     tokens, depth = attention.shape
-    width = weights.shape[0] // KVH
+    count = len(pieces)
+    width = count * pieces[0].shape[0] // KVH
     return pl.pallas_call(
-        functools.partial(out_kernel, core_flip),
-        out_shape=jax.ShapeDtypeStruct((2, tokens, width), jnp.bfloat16),
-        in_specs=[smem(), vmem(), vmem()],
+        functools.partial(out_kernel, count),
+        out_shape=jax.ShapeDtypeStruct((2, 2, tokens, width), jnp.bfloat16),
+        in_specs=[smem(), vmem()] + [hbm()] * count,
         out_specs=vmem(),
+        scratch_shapes=[
+            pltpu.VMEM((KVH * width, depth), jnp.bfloat16),
+            pltpu.SemaphoreType.DMA((2 * count,)),
+        ],
         compiler_params=params(),
         cost_estimate=pl.CostEstimate(
-            flops=4 * tokens * width * depth, bytes_accessed=4 * width * depth, transcendentals=0
+            flops=8 * tokens * width * depth, bytes_accessed=8 * width * depth, transcendentals=0
         ),
         name="out_project",
-    )(info, attention, weights)
+    )(info, attention, *pieces)
 
 
 def gather_pieces(shard, n_seq):
@@ -330,6 +337,28 @@
     return own, copied
 
 
+def gather_output_pieces(shard, inner, n_seq):
+    other = send(shard, n_seq, lambda big, l, x, y, c: (big, 1 - l, x, y, c))
+    near = [jnp.concatenate([shard, other], axis=0)]
+    if n_seq == 2 * SPLIT:
+        middle = send(
+            near[0], n_seq, lambda big, l, x, y, c: (1 - big, 1 - l, x, y, c) if big != l else None
+        )
+        outer = send(
+            middle, n_seq, lambda big, l, x, y, c: (big, 1 - l, x, y, c) if big != l else None
+        )
+        near.append(jnp.where(inner, middle, outer))
+    else:
+        bit = 1
+        while bit < n_seq // SPLIT:
+            near += [
+                send(piece, n_seq, lambda big, l, x, y, c: (big ^ bit, l, x, y, c))
+                for piece in near
+            ]
+            bit *= 2
+    return near + [send(p, n_seq, lambda big, l, x, y, c: (big, l, 1 - x, y, c)) for p in near]
+
+
 def on_device(
     hidden,
     norm_gain,
@@ -352,8 +381,19 @@
     matched = c == l
     segment_ids = jnp.arange(ratios.shape[0], dtype=jnp.int32)
     own_ratio = jnp.sum(jnp.where(segment_ids == big, ratios, 0))
+    inner = (big != l) & (n_seq == 2 * SPLIT)
     info = jnp.stack(
-        [matched.astype(jnp.int32), y, own_ratio, rows_dev // own_ratio, big, l, x, c]
+        [
+            matched.astype(jnp.int32),
+            y,
+            own_ratio,
+            rows_dev // own_ratio,
+            big,
+            l,
+            x,
+            c,
+            inner.astype(jnp.int32),
+        ]
     ).astype(jnp.int32)
 
     own_half = lax.dynamic_slice_in_dim(hidden, y * half, half, 0)
@@ -374,7 +414,8 @@
 
     small_own, small_copied = gather_pieces(small, n_seq)
     query_own, query_copied = gather_pieces(query_weight, n_seq)
-    out_rows = lax.all_gather(out_weight.T, "seq", axis=0, tiled=True)
+    out_shard, _ = lax.optimization_barrier((out_weight.T, query_own[1]))
+    out_pieces = gather_output_pieces(out_shard, inner, n_seq)
 
     normed, pooled = norm_and_pool(info, hidden, first, second, norm_gain)
     slots_dev = rows_dev // R_MIN
@@ -419,20 +460,23 @@
         query_own,
         query_copied,
     )
-    attention = attend(info, ratios, query, pair, far_pair, beacons[1:])
-    swapped = send(
-        attention, n_seq, lambda big, l, x, y, c: (big, 1 - l, x, y, 1 - c) if c != l else None
-    )
-    attention = jnp.where(matched, attention, swapped)
-
-    away = out_project(1, info, attention, out_rows)
-    from_core = send(away, n_seq, lambda big, l, x, y, c: (big, l, x, y, 1 - c))
-    kept = out_project(0, info, attention, out_rows)
-    sums = kept.astype(jnp.float32) + from_core.astype(jnp.float32)
-    from_y = send(
-        sums[1].astype(jnp.bfloat16), n_seq, lambda big, l, x, y, c: (big, l, x, 1 - y, c)
-    )
-    return (sums[0] + from_y.astype(jnp.float32)).astype(jnp.bfloat16)
+    parts = 2
+    part = rows_dev // parts
+    results = []
+    for i in range(parts):
+        attention = attend(i * part, part, info, ratios, query, pair, far_pair, beacons[1:])
+        swapped = send(
+            attention, n_seq, lambda big, l, x, y, c: (big, 1 - l, x, y, 1 - c) if c != l else None
+        )
+        attention = jnp.where(matched, attention, swapped)
+        partial = out_project(info, attention, out_pieces)
+        from_core = send(partial[1], n_seq, lambda big, l, x, y, c: (big, l, x, y, 1 - c))
+        sums = partial[0].astype(jnp.float32) + from_core.astype(jnp.float32)
+        from_y = send(
+            sums[1].astype(jnp.bfloat16), n_seq, lambda big, l, x, y, c: (big, l, x, 1 - y, c)
+        )
+        results.append((sums[0] + from_y.astype(jnp.float32)).astype(jnp.bfloat16))
+    return jnp.concatenate(results, axis=0)
 
 
 def solution(mesh):

time: 329 us -> 288 us (0.88)
  waiting for transfers between devices: 177 us -> 154 us
  starting transfers between devices: 72.6 us -> 57.1 us
  between operations: 16.1 us -> 2.68 us
  Pallas kernels: 44 us -> 51.1 us
  local copies, waits for them, and re-layouts: 9.56 us -> 13.6 us
    ppermute x25 -> x33, waiting for transfers between devices: 176 us -> 154 us  [send(): return lax.ppermute(value, AXES, moves(n_seq, rule))]
    ppermute x25 -> x33, starting transfers between devices: 72.6 us -> 57.1 us  [send(): return lax.ppermute(value, AXES, moves(n_seq, rule))]
    pallas_call x3 -> x4, Pallas kernels: 22.2 us -> 29.4 us  [the longest x2 15.2 us: out_project(): pl.pallas_call(functools.partial(out_kernel, count), out_shape=jax.ShapeD...]
  transfers between devices with their start and end apart: 26 -> 33, of which waited for: 10 -> 12; matrix products, arithmetic and copies ran while one was open for 3% -> 6% of each run, Pallas kernels for 11% -> 18%
where the time goes in v2:
time: 288 us; the launch traced here: 285 us
  waiting for transfers between devices  154 us (53%)
  starting transfers between devices  57.1 us (20%)
  Pallas kernels  51.1 us (18%)
  local copies, waits for them, and re-layouts  13.6 us (5%)
  other arithmetic  6.68 us (2%)
    ppermute x33, waiting for transfers between devices, send(): return lax.ppermute(value, AXES, moves(n_seq, rule))  154 us
    ppermute x33, starting transfers between devices, send(): return lax.ppermute(value, AXES, moves(n_seq, rule))  57.1 us
    pallas_call x2, Pallas kernels, project(): pl.pallas_call(functools.partial(kernel, count), out_shape=jax.ShapeDtype...  16.3 us
    pallas_call x2, Pallas kernels, out_project(): pl.pallas_call(functools.partial(out_kernel, count), out_shape=jax.ShapeD...  15.2 us
    pallas_call x2, Pallas kernels, attend(): pl.pallas_call(functools.partial(attend_kernel, tokens, len(beacons), fir...  14.3 us
  transfers between devices with their start and end apart: 33, of which 12 were waited for; matrix products, arithmetic and copies ran while one was open for 6% of the time, Pallas kernels for 18%

profile of v2, /device:TPU:0, one launch (start us, length us, event | category | flops | bytes accessed | tf_op | source)
XLA Modules:
  0.0 285.0 jit_solution(15033388052212207061)
XLA Ops:
  0.0 1.3 collective-permute-start.3
  1.3 2.1 constant_dynamic-update-slice_fusion.1
  3.4 11.2 %collective-permute-done.3 = bf16[448,896]{1,0:T(8,128)(2,1)S(1)} collective-permute-done((bf16[448,896]{1,0:T(8,128)(2,1)}, bf16[448,896]{1,0:T(8,128)(2,1)S(1)}, u32[]{:S(2)}, u32[]{:S(2)}) %collective-permute-start.3) | collective-permute-done | bytes 802848 | tf_op jit(solution)/shard_map/ppermute | solution.py:48
  15.6 5.7 %collective-permute-start.4 = (bf16[896,896]{1,0:T(8,128)(2,1)}, bf16[896,896]{1,0:T(8,128)(2,1)}, u32[]{:S(2)}, u32[]{:S(2)}) collective-permute-start(bf16[896,896]{1,0:T(8,128)(2,1)} %constant_dynamic-update-slice_fusion.rest_0_), channel_id=1, source_target_pairs={{0,16},{2,18},{4,20},{6,22},{9,25},{11,27},{13,29},{15,31},{16,0},... | collective-permute-start | bytes 4816904 | tf_op jit(solution)/shard_map/ppermute | solution.py:48
  21.3 1.6 constant_dynamic-slice_fusion
  23.8 1.3 collective-permute-start.11
  25.1 32.0 %collective-permute-done.4.rest_1_ = bf16[896,896]{1,0:T(8,128)(2,1)} collective-permute-done((bf16[896,896]{1,0:T(8,128)(2,1)}, bf16[896,896]{1,0:T(8,128)(2,1)}, u32[]{:S(2)}, u32[]{:S(2)}) %collective-permute-start.4) | collective-permute-done | bytes 1605664 | tf_op jit(solution)/shard_map/ppermute | solution.py:48
  57.2 16.7 %collective-permute-done.11 = bf16[448,512]{1,0:T(8,128)(2,1)S(1)} collective-permute-done((bf16[448,512]{1,0:T(8,128)(2,1)S(1)}, bf16[448,512]{1,0:T(8,128)(2,1)S(1)}, u32[]{:S(2)}, u32[]{:S(2)}) %collective-permute-start.11) | collective-permute-done | bytes 458784 | tf_op jit(solution)/shard_map/ppermute | solution.py:48
  74.0 2.1 collective-permute-start.12
  76.0 3.5 %collective-permute-start.13 = (bf16[896,512]{1,0:T(8,128)(2,1)S(1)}, bf16[896,512]{1,0:T(8,128)(2,1)}, u32[]{:S(2)}, u32[]{:S(2)}) collective-permute-start(bf16[896,512]{1,0:T(8,128)(2,1)S(1)} %pad_maximum_fusion.rest_0_), channel_id=1, source_target_pairs={{0,4},{2,6},{4,0},{6,2},{9,13},{11,15},{13,9},{15,11},{16,20},{18,... | collective-permute-start | bytes 2752520 | tf_op jit(solution)/shard_map/ppermute | solution.py:48
  80.4 4.1 %collective-permute-done.23 = bf16[448,896]{1,0:T(8,128)(2,1)S(1)} collective-permute-done((bf16[448,896]{1,0:T(8,128)(2,1)S(1)}, bf16[448,896]{1,0:T(8,128)(2,1)S(1)}, u32[]{:S(2)}, u32[]{:S(2)}) %collective-permute-start.23) | collective-permute-done | bytes 802848 | tf_op jit(solution)/shard_map/ppermute | solution.py:48
  84.6 1.9 collective-permute-start.24
  86.5 1.2 collective-permute-done.2
  87.7 2.1 collective-permute-start.15
  89.8 11.8 %collective-permute-done.12.rest_1_ = bf16[896,512]{1,0:T(8,128)(2,1)S(1)} collective-permute-done((bf16[896,512]{1,0:T(8,128)(2,1)S(1)}, bf16[896,512]{1,0:T(8,128)(2,1)S(1)}, u32[]{:S(2)}, u32[]{:S(2)}) %collective-permute-start.12) | collective-permute-done | bytes 917536 | tf_op jit(solution)/shard_map/ppermute | solution.py:48
  101.6 6.7 %collective-permute-start.14 = (bf16[896,512]{1,0:T(8,128)(2,1)S(1)}, bf16[896,512]{1,0:T(8,128)(2,1)}, u32[]{:S(2)}, u32[]{:S(2)}) collective-permute-start(bf16[896,512]{1,0:T(8,128)(2,1)S(1)} %collective-permute-done.12.rest_1_), channel_id=1, source_target_pairs={{0,4},{2,6},{4,0},{6,2},{9,13},{11,15},{13,9},{15,11},{16,20},{18,... | collective-permute-start | bytes 2752520 | tf_op jit(solution)/shard_map/ppermute | solution.py:48
  108.4 1.3 collective-permute-start.16
  109.8 1.9 collective-permute-start.5
  111.7 8.1 %collective-permute-done.14.rest_3_ = bf16[896,512]{1,0:T(8,128)(2,1)} collective-permute-done((bf16[896,512]{1,0:T(8,128)(2,1)S(1)}, bf16[896,512]{1,0:T(8,128)(2,1)}, u32[]{:S(2)}, u32[]{:S(2)}) %collective-permute-start.14) | collective-permute-done | bytes 917536 | tf_op jit(solution)/shard_map/ppermute | solution.py:48
  119.8 3.9 %collective-permute-start.6 = (bf16[896,896]{1,0:T(8,128)(2,1)}, bf16[896,896]{1,0:T(8,128)(2,1)}, u32[]{:S(2)}, u32[]{:S(2)}) collective-permute-start(bf16[896,896]{1,0:T(8,128)(2,1)} %collective-permute-done.4.rest_1_), channel_id=1, source_target_pairs={{0,4},{2,6},{4,0},{6,2},{9,13},{11,15},{13,9},{15,11},{16,20},{18,... | collective-permute-start | bytes 4816904 | tf_op jit(solution)/shard_map/ppermute | solution.py:48
  123.8 2.3 collective-permute-start.17
  126.1 2.3 collective-permute-start.18
  128.4 1.3 collective-permute-start.25
  133.0 1.3 stack.47.info
  134.9 5.5 %norm_pool.1 = (bf16[512,3584]{1,0:T(8,128)(2,1)}, bf16[64,3584]{1,0:T(8,128)(2,1)}) custom-call(s32[9]{0:T(128)} %stack.47.info, bf16[512,3584]{1,0:T(8,128)(2,1)} %hidden.1, bf16[256,3584]{1,0:T(8,128)(2,1)} %copy-done.7, bf16[256,3584]{1,0:T(8,128)(2,1)} %copy-done.8, f32[1,3584]{1,0:T(1,128)} %reshape.27.gain), custom_call_target="tpu_custom_call" | custom-call | flops 234881024 | bytes 7340032 | tf_op jit(solution)/shard_map/norm_pool/pallas_call | solution.py:99
  140.4 1.4 collective-permute-start.7
  141.8 6.4 %project.3 = bf16[576,256]{1,0:T(8,128)(2,1)} custom-call(s32[9]{0:T(128)} %stack.47.info, bf16[512,3584]{1,0:T(8,128)(2,1)} %get-tuple-element.8.normed, bf16[64,3584]{1,0:T(8,128)(2,1)} %get-tuple-element.9.pooled, f32[1,512]{1,0:T(1,128)} %bitcast.53, bf16[896,512]{1,0:T(8,128)(2,1)} %copy-done.6, bf16[896,512]{1,0:T(8,128)(2,1)} %copy-done.10, ...), custom_call_target="tpu_custom_call" | custom-call | flops 1056964608 | bytes 7798784 | tf_op jit(solution)/shard_map/project/pallas_call | solution.py:169
  148.3 2.5 collective-permute-start.8
  150.8 9.7 %collective-permute-done.19 = bf16[576,256]{1,0:T(8,128)(2,1)S(1)} collective-permute-done((bf16[576,256]{1,0:T(8,128)(2,1)}, bf16[576,256]{1,0:T(8,128)(2,1)S(1)}, u32[]{:S(2)}, u32[]{:S(2)}) %collective-permute-start.19) | collective-permute-done | bytes 294944 | tf_op jit(solution)/shard_map/ppermute | solution.py:48
  160.5 2.5 collective-permute-start.9
  163.0 2.5 collective-permute-start.10
  165.4 1.0 pad_maximum_fusion.2.pair
  166.5 1.7 broadcast_select_fusion.rest_1_
  168.3 2.1 collective-permute-start.26
  172.8 9.9 %project.2.queries = bf16[512,896]{1,0:T(8,128)(2,1)} custom-call(s32[9]{0:T(128)} %stack.47.info, bf16[512,3584]{1,0:T(8,128)(2,1)} %get-tuple-element.8.normed, f32[1,896]{1,0:T(1,128)} %reshape.30.bias, bf16[896,896]{1,0:T(8,128)(2,1)} %constant_dynamic-update-slice_fusion.rest_0_, bf16[896,896]{1,0:T(8,128)(2,1)} %collective-permute-done.4.rest_1_, ...), custom_call_target="tpu_custom_call" | custom-call | flops 3288334336 | bytes 10092544 | tf_op jit(solution)/shard_map/project/pallas_call | solution.py:169
  183.3 7.4 %attend.3 = bf16[256,896]{1,0:T(8,128)(2,1)} custom-call(s32[9]{0:T(128)} %stack.47.info, s32[2]{0:T(128)} %ratios.3, bf16[512,896]{1,0:T(8,128)(2,1)} %project.2.queries, bf16[1152,256]{1,0:T(8,128)(2,1)} %copy-done.14, bf16[1152,256]{1,0:T(8,128)(2,1)} %copy-done.21, bf16[256,256]{1,0:T(8,128)(2,1)} %copy-done.24), custom_call_target="tpu_custom_call" | custom-call | flops 2113929216 | bytes 1835008 | tf_op jit(solution)/shard_map/attend/pallas_call | solution.py:255
  191.6 6.8 %attend.2 = bf16[256,896]{1,0:T(8,128)(2,1)} custom-call(s32[9]{0:T(128)} %stack.47.info, s32[2]{0:T(128)} %ratios.3, bf16[512,896]{1,0:T(8,128)(2,1)} %project.2.queries, bf16[1152,256]{1,0:T(8,128)(2,1)} %copy-done.14, bf16[1152,256]{1,0:T(8,128)(2,1)} %copy-done.21, bf16[256,256]{1,0:T(8,128)(2,1)} %copy-done.24), custom_call_target="tpu_custom_call" | custom-call | flops 2113929216 | bytes 1835008 | tf_op jit(solution)/shard_map/attend/pallas_call | solution.py:255
  200.1 6.2 %collective-permute-done.26.rest_2_ = bf16[896,896]{1,0:T(8,128)(2,1)S(1)} collective-permute-done((bf16[896,896]{1,0:T(8,128)(2,1)S(1)}, bf16[896,896]{1,0:T(8,128)(2,1)S(1)}, u32[]{:S(2)}, u32[]{:S(2)}) %collective-permute-start.26) | collective-permute-done | bytes 1605664 | tf_op jit(solution)/shard_map/ppermute | solution.py:48
  206.3 34.1 %collective-permute-done.27.rest_3_ = bf16[896,896]{1,0:T(8,128)(2,1)S(1)} collective-permute-done((bf16[896,896]{1,0:T(8,128)(2,1)S(1)}, bf16[896,896]{1,0:T(8,128)(2,1)S(1)}, u32[]{:S(2)}, u32[]{:S(2)}) %collective-permute-start.27) | collective-permute-done | bytes 1605664 | tf_op jit(solution)/shard_map/ppermute | solution.py:48
  240.4 1.2 copy-done.5
  241.6 7.6 %out_project.3 = bf16[2,2,256,896]{3,2,1,0:T(8,128)(2,1)} custom-call(s32[9]{0:T(128)} %stack.47.info, bf16[256,896]{1,0:T(8,128)(2,1)} %broadcast_select_fusion.1.attention, bf16[896,896]{1,0:T(8,128)(2,1)} %copy-done.1, bf16[896,896]{1,0:T(8,128)(2,1)} %copy-done, bf16[896,896]{1,0:T(8,128)(2,1)} %copy-done.4, bf16[896,896]{1,0:T(8,128)(2,1)} %copy-done.5), custom_call_target="tpu_custom_call" | custom-call | flops 1644167168 | bytes 6422528 | tf_op jit(solution)/shard_map/out_project/pallas_call | solution.py:295
  249.2 1.3 slice_bitcast_fusion.1
  251.4 7.5 %out_project.2 = bf16[2,2,256,896]{3,2,1,0:T(8,128)(2,1)} custom-call(s32[9]{0:T(128)} %stack.47.info, bf16[256,896]{1,0:T(8,128)(2,1)} %broadcast_select_fusion.2.attention, bf16[896,896]{1,0:T(8,128)(2,1)} %copy-done.1, bf16[896,896]{1,0:T(8,128)(2,1)} %copy-done, bf16[896,896]{1,0:T(8,128)(2,1)} %copy-done.4, bf16[896,896]{1,0:T(8,128)(2,1)} %copy-done.5), custom_call_target="tpu_custom_call" | custom-call | flops 1644167168 | bytes 6422528 | tf_op jit(solution)/shard_map/out_project/pallas_call | solution.py:295
  259.0 1.4 slice_bitcast_fusion.4
  261.2 1.8 collective-permute-start.32
  263.3 1.8 collective-permute-start.29
  265.1 9.5 %collective-permute-done.32 = bf16[256,896]{1,0:T(8,128)(2,1)S(1)} collective-permute-done((bf16[256,896]{1,0:T(8,128)(2,1)S(1)}, bf16[256,896]{1,0:T(8,128)(2,1)S(1)}, u32[]{:S(2)}, u32[]{:S(2)}) %collective-permute-start.32) | collective-permute-done | bytes 458784 | tf_op jit(solution)/shard_map/ppermute | solution.py:48
  274.7 9.1 %collective-permute-done.29 = bf16[256,896]{1,0:T(8,128)(2,1)S(1)} collective-permute-done((bf16[256,896]{1,0:T(8,128)(2,1)S(1)}, bf16[256,896]{1,0:T(8,128)(2,1)S(1)}, u32[]{:S(2)}, u32[]{:S(2)}) %collective-permute-start.29) | collective-permute-done | bytes 458784 | tf_op jit(solution)/shard_map/ppermute | solution.py:48
  (110 shorter events, 13.8 us)
Async XLA Ops:
  0.0 14.6 %collective-permute-start.3 = (bf16[448,896]{1,0:T(8,128)(2,1)}, bf16[448,896]{1,0:T(8,128)(2,1)S(1)}, u32[]{:S(2)}, u32[]{:S(2)}) collective-permute-start(bf16[448,896]{1,0:T(8,128)(2,1)} %param.12), channel_id=1, source_target_pairs={{1,9},{3,11},{5,13},{7,15},{8,0},{10,2},{12,4},{14,6},{17,25},{19,... | collective-permute-start | bytes 2408456 | tf_op jit(solution)/shard_map/ppermute | solution.py:48
  15.6 8.2 %copy-start.18 = (bf16[448,2,128]{2,1,0:T(2,128)(2,1)S(1)}, bf16[448,2,128]{2,1,0:T(2,128)(2,1)}, u32[]{:S(2)}) copy-start(bf16[448,2,128]{2,1,0:T(2,128)(2,1)} %param.16) | copy-start | bytes 688132
  15.6 41.5 %copy-start.13 = (bf16[896,448]{0,1:T(8,128)(2,1)S(1)}, bf16[896,448]{0,1:T(8,128)(2,1)}, u32[]{:S(2)}) copy-start(bf16[896,448]{0,1:T(8,128)(2,1)} %param.18) | copy-start | bytes 2408452
  15.6 41.5 %collective-permute-start.4 = (bf16[896,896]{1,0:T(8,128)(2,1)}, bf16[896,896]{1,0:T(8,128)(2,1)}, u32[]{:S(2)}, u32[]{:S(2)}) collective-permute-start(bf16[896,896]{1,0:T(8,128)(2,1)} %constant_dynamic-update-slice_fusion.rest_0_), channel_id=1, source_target_pairs={{0,16},{2,18},{4,20},{6,22},{9,25},{11,27},{13,29},{15,31},{16,0},... | collective-permute-start | bytes 4816904 | tf_op jit(solution)/shard_map/ppermute | solution.py:48
  23.0 56.5 %collective-permute-start = (bf16[256,3584]{1,0:T(8,128)(2,1)S(1)}, bf16[256,3584]{1,0:T(8,128)(2,1)S(1)}, u32[]{:S(2)}, u32[]{:S(2)}) collective-permute-start(bf16[256,3584]{1,0:T(8,128)(2,1)S(1)} %constant_dynamic-slice_fusion), channel_id=1, source_target_pairs={{1,8},{3,10},{5,12},{7,14},{8,1},{10,3},{12,5},{14,7},{17,24},{19,... | collective-permute-start | bytes 5505032 | tf_op jit(solution)/shard_map/ppermute | solution.py:48
  23.8 50.0 %collective-permute-start.11 = (bf16[448,512]{1,0:T(8,128)(2,1)S(1)}, bf16[448,512]{1,0:T(8,128)(2,1)S(1)}, u32[]{:S(2)}, u32[]{:S(2)}) collective-permute-start(bf16[448,512]{1,0:T(8,128)(2,1)S(1)} %bitcast_dynamic-update-slice_fusion), channel_id=1, source_target_pairs={{1,9},{3,11},{5,13},{7,15},{8,0},{10,2},{12,4},{14,6},{17,25},{19,... | collective-permute-start | bytes 1376264 | tf_op jit(solution)/shard_map/ppermute | solution.py:48
  57.2 27.3 %collective-permute-start.23 = (bf16[448,896]{1,0:T(8,128)(2,1)S(1)}, bf16[448,896]{1,0:T(8,128)(2,1)S(1)}, u32[]{:S(2)}, u32[]{:S(2)}) collective-permute-start(bf16[448,896]{1,0:T(8,128)(2,1)S(1)} %bitcast.49), channel_id=1, source_target_pairs={{0,8},{1,9},{2,10},{3,11},{4,12},{5,13},{6,14},{7,15},{8,0},{9,1},... | collective-permute-start | bytes 2408456 | tf_op jit(solution)/shard_map/ppermute | solution.py:48
  73.9 66.5 %copy-start.6 = (bf16[896,512]{1,0:T(8,128)(2,1)}, bf16[896,512]{1,0:T(8,128)(2,1)S(1)}, u32[]{:S(2)}) copy-start(bf16[896,512]{1,0:T(8,128)(2,1)S(1)} %pad_maximum_fusion.rest_0_) | copy-start | bytes 2752516
  73.9 12.6 %copy-start.19 = (f32[896]{0:T(1024)S(1)}, f32[896]{0:T(1024)}, u32[]{:S(2)}) copy-start(f32[896]{0:T(1024)} %param.13) | copy-start | bytes 10756
  73.9 12.6 %copy-start.22 = (f32[2,128]{1,0:T(2,128)S(1)}, f32[2,128]{1,0:T(2,128)}, u32[]{:S(2)}) copy-start(f32[2,128]{1,0:T(2,128)} %param.17) | copy-start | bytes 3076
  73.9 12.5 %copy-start.23 = (f32[2,128]{1,0:T(2,128)S(1)}, f32[2,128]{1,0:T(2,128)}, u32[]{:S(2)}) copy-start(f32[2,128]{1,0:T(2,128)} %param.15) | copy-start | bytes 3076
  73.9 55.8 %copy-start.25 = (s32[2]{0:T(128)S(1)}, s32[2]{0:T(128)}, u32[]{:S(2)}) copy-start(s32[2]{0:T(128)} %ratios.3) | copy-start | bytes 28
  73.9 58.4 %copy-start.20 = (f32[3584]{0:T(1024)S(1)}, f32[3584]{0:T(1024)}, u32[]{:S(2)}) copy-start(f32[3584]{0:T(1024)} %param.11) | copy-start | bytes 43012
  74.0 27.7 %collective-permute-start.12 = (bf16[896,512]{1,0:T(8,128)(2,1)S(1)}, bf16[896,512]{1,0:T(8,128)(2,1)S(1)}, u32[]{:S(2)}, u32[]{:S(2)}) collective-permute-start(bf16[896,512]{1,0:T(8,128)(2,1)S(1)} %pad_maximum_fusion.rest_0_), channel_id=1, source_target_pairs={{0,16},{2,18},{4,20},{6,22},{9,25},{11,27},{13,29},{15,31},{16,0},... | collective-permute-start | bytes 2752520 | tf_op jit(solution)/shard_map/ppermute | solution.py:48
  76.0 32.4 %collective-permute-start.13 = (bf16[896,512]{1,0:T(8,128)(2,1)S(1)}, bf16[896,512]{1,0:T(8,128)(2,1)}, u32[]{:S(2)}, u32[]{:S(2)}) collective-permute-start(bf16[896,512]{1,0:T(8,128)(2,1)S(1)} %pad_maximum_fusion.rest_0_), channel_id=1, source_target_pairs={{0,4},{2,6},{4,0},{6,2},{9,13},{11,15},{13,9},{15,11},{16,20},{18,... | collective-permute-start | bytes 2752520 | tf_op jit(solution)/shard_map/ppermute | solution.py:48
  79.5 48.9 %copy-start.7 = (bf16[256,3584]{1,0:T(8,128)(2,1)}, bf16[256,3584]{1,0:T(8,128)(2,1)S(1)}, u32[]{:S(2)}) copy-start(bf16[256,3584]{1,0:T(8,128)(2,1)S(1)} %collective-permute-done.first) | copy-start | bytes 5505028
  79.5 46.6 %collective-permute-start.1 = (bf16[256,3584]{1,0:T(8,128)(2,1)S(1)}, bf16[256,3584]{1,0:T(8,128)(2,1)S(1)}, u32[]{:S(2)}, u32[]{:S(2)}) collective-permute-start(bf16[256,3584]{1,0:T(8,128)(2,1)S(1)} %collective-permute-done.first), channel_id=1, source_target_pairs={{1,3},{3,1},{5,7},{7,5},{8,10},{10,8},{12,14},{14,12},{17,19},{19,... | collective-permute-start | bytes 5505032 | tf_op jit(solution)/shard_map/ppermute | solution.py:48
  84.6 83.7 %copy-start.1 = (bf16[896,896]{1,0:T(8,128)(2,1)}, bf16[896,896]{1,0:T(8,128)(2,1)S(1)}, u32[]{:S(2)}) copy-start(bf16[896,896]{1,0:T(8,128)(2,1)S(1)} %constant_dynamic-update-slice_fusion.2.rest_0_) | copy-start | bytes 4816900
  84.6 43.8 %collective-permute-start.24 = (bf16[896,896]{1,0:T(8,128)(2,1)S(1)}, bf16[896,896]{1,0:T(8,128)(2,1)}, u32[]{:S(2)}, u32[]{:S(2)}) collective-permute-start(bf16[896,896]{1,0:T(8,128)(2,1)S(1)} %constant_dynamic-update-slice_fusion.2.rest_0_), channel_id=1, source_target_pairs={{8,16},{9,17},{10,18},{11,19},{12,20},{13,21},{14,22},{15,23},{16,... | collective-permute-start | bytes 4816904 | tf_op jit(solution)/shard_map/ppermute | solution.py:48
  86.5 1.2 collective-permute-start.2
  87.7 22.0 %collective-permute-start.15 = (bf16[896,512]{1,0:T(8,128)(2,1)S(1)}, bf16[896,512]{1,0:T(8,128)(2,1)S(1)}, u32[]{:S(2)}, u32[]{:S(2)}) collective-permute-start(bf16[896,512]{1,0:T(8,128)(2,1)S(1)} %pad_maximum_fusion.rest_0_), channel_id=1, source_target_pairs={{0,1},{2,3},{4,5},{6,7},{9,8},{11,10},{13,12},{15,14},{16,17},{18,... | collective-permute-start | bytes 2752520 | tf_op jit(solution)/shard_map/ppermute | solution.py:48
  101.6 40.2 %copy-start.10 = (bf16[896,512]{1,0:T(8,128)(2,1)}, bf16[896,512]{1,0:T(8,128)(2,1)S(1)}, u32[]{:S(2)}) copy-start(bf16[896,512]{1,0:T(8,128)(2,1)S(1)} %collective-permute-done.12.rest_1_) | copy-start | bytes 2752516
  101.6 18.2 %collective-permute-start.14 = (bf16[896,512]{1,0:T(8,128)(2,1)S(1)}, bf16[896,512]{1,0:T(8,128)(2,1)}, u32[]{:S(2)}, u32[]{:S(2)}) collective-permute-start(bf16[896,512]{1,0:T(8,128)(2,1)S(1)} %collective-permute-done.12.rest_1_), channel_id=1, source_target_pairs={{0,4},{2,6},{4,0},{6,2},{9,13},{11,15},{13,9},{15,11},{16,20},{18,... | collective-permute-start | bytes 2752520 | tf_op jit(solution)/shard_map/ppermute | solution.py:48
  108.4 15.4 %collective-permute-start.16 = (bf16[896,512]{1,0:T(8,128)(2,1)S(1)}, bf16[896,512]{1,0:T(8,128)(2,1)S(1)}, u32[]{:S(2)}, u32[]{:S(2)}) collective-permute-start(bf16[896,512]{1,0:T(8,128)(2,1)S(1)} %collective-permute-done.12.rest_1_), channel_id=1, source_target_pairs={{0,1},{2,3},{4,5},{6,7},{9,8},{11,10},{13,12},{15,14},{16,17},{18,... | collective-permute-start | bytes 2752520 | tf_op jit(solution)/shard_map/ppermute | solution.py:48
  109.8 18.6 %copy-start.11 = (bf16[896,512]{1,0:T(8,128)(2,1)}, bf16[896,512]{1,0:T(8,128)(2,1)S(1)}, u32[]{:S(2)}) copy-start(bf16[896,512]{1,0:T(8,128)(2,1)S(1)} %collective-permute-done.15.rest_4_) | copy-start | bytes 2752516
  109.8 38.5 %collective-permute-start.5 = (bf16[896,896]{1,0:T(8,128)(2,1)}, bf16[896,896]{1,0:T(8,128)(2,1)}, u32[]{:S(2)}, u32[]{:S(2)}) collective-permute-start(bf16[896,896]{1,0:T(8,128)(2,1)} %constant_dynamic-update-slice_fusion.rest_0_), channel_id=1, source_target_pairs={{0,4},{2,6},{4,0},{6,2},{9,13},{11,15},{13,9},{15,11},{16,20},{18,... | collective-permute-start | bytes 4816904 | tf_op jit(solution)/shard_map/ppermute | solution.py:48
  119.8 43.1 %collective-permute-start.6 = (bf16[896,896]{1,0:T(8,128)(2,1)}, bf16[896,896]{1,0:T(8,128)(2,1)}, u32[]{:S(2)}, u32[]{:S(2)}) collective-permute-start(bf16[896,896]{1,0:T(8,128)(2,1)} %collective-permute-done.4.rest_1_), channel_id=1, source_target_pairs={{0,4},{2,6},{4,0},{6,2},{9,13},{11,15},{13,9},{15,11},{16,20},{18,... | collective-permute-start | bytes 4816904 | tf_op jit(solution)/shard_map/ppermute | solution.py:48
  123.8 16.6 %collective-permute-start.17 = (bf16[896,512]{1,0:T(8,128)(2,1)}, bf16[896,512]{1,0:T(8,128)(2,1)}, u32[]{:S(2)}, u32[]{:S(2)}) collective-permute-start(bf16[896,512]{1,0:T(8,128)(2,1)} %collective-permute-done.13.rest_2_), channel_id=1, source_target_pairs={{0,1},{2,3},{4,5},{6,7},{9,8},{11,10},{13,12},{15,14},{16,17},{18,... | collective-permute-start | bytes 2752520 | tf_op jit(solution)/shard_map/ppermute | solution.py:48
  126.1 15.7 %collective-permute-start.18 = (bf16[896,512]{1,0:T(8,128)(2,1)}, bf16[896,512]{1,0:T(8,128)(2,1)}, u32[]{:S(2)}, u32[]{:S(2)}) collective-permute-start(bf16[896,512]{1,0:T(8,128)(2,1)} %collective-permute-done.14.rest_3_), channel_id=1, source_target_pairs={{0,1},{2,3},{4,5},{6,7},{9,8},{11,10},{13,12},{15,14},{16,17},{18,... | collective-permute-start | bytes 2752520 | tf_op jit(solution)/shard_map/ppermute | solution.py:48
  128.4 38.0 %collective-permute-start.25 = (bf16[896,896]{1,0:T(8,128)(2,1)}, bf16[896,896]{1,0:T(8,128)(2,1)}, u32[]{:S(2)}, u32[]{:S(2)}) collective-permute-start(bf16[896,896]{1,0:T(8,128)(2,1)} %collective-permute-done.24), channel_id=1, source_target_pairs={{8,0},{9,1},{10,2},{11,3},{12,4},{13,5},{14,6},{15,7},{16,24},{17,... | collective-permute-start | bytes 4816904 | tf_op jit(solution)/shard_map/ppermute | solution.py:48
  140.4 27.9 %collective-permute-start.7 = (bf16[896,896]{1,0:T(8,128)(2,1)}, bf16[896,896]{1,0:T(8,128)(2,1)S(1)}, u32[]{:S(2)}, u32[]{:S(2)}) collective-permute-start(bf16[896,896]{1,0:T(8,128)(2,1)} %constant_dynamic-update-slice_fusion.rest_0_), channel_id=1, source_target_pairs={{0,1},{2,3},{4,5},{6,7},{9,8},{11,10},{13,12},{15,14},{16,17},{18,... | collective-permute-start | bytes 4816904 | tf_op jit(solution)/shard_map/ppermute | solution.py:48
  148.2 12.2 %collective-permute-start.19 = (bf16[576,256]{1,0:T(8,128)(2,1)}, bf16[576,256]{1,0:T(8,128)(2,1)S(1)}, u32[]{:S(2)}, u32[]{:S(2)}) collective-permute-start(bf16[576,256]{1,0:T(8,128)(2,1)} %project.3), channel_id=1, source_target_pairs={{0,4},{1,5},{2,6},{3,7},{4,0},{5,1},{6,2},{7,3},{8,12},{9,13},{10,... | collective-permute-start | bytes 884744 | tf_op jit(solution)/shard_map/ppermute | solution.py:48
  148.3 23.7 %collective-permute-start.8 = (bf16[896,896]{1,0:T(8,128)(2,1)}, bf16[896,896]{1,0:T(8,128)(2,1)}, u32[]{:S(2)}, u32[]{:S(2)}) collective-permute-start(bf16[896,896]{1,0:T(8,128)(2,1)} %collective-permute-done.4.rest_1_), channel_id=1, source_target_pairs={{0,1},{2,3},{4,5},{6,7},{9,8},{11,10},{13,12},{15,14},{16,17},{18,... | collective-permute-start | bytes 4816904 | tf_op jit(solution)/shard_map/ppermute | solution.py:48
  160.5 12.3 %collective-permute-start.9 = (bf16[896,896]{1,0:T(8,128)(2,1)}, bf16[896,896]{1,0:T(8,128)(2,1)}, u32[]{:S(2)}, u32[]{:S(2)}) collective-permute-start(bf16[896,896]{1,0:T(8,128)(2,1)} %collective-permute-done.5.rest_2_), channel_id=1, source_target_pairs={{0,1},{2,3},{4,5},{6,7},{9,8},{11,10},{13,12},{15,14},{16,17},{18,... | collective-permute-start | bytes 4816904 | tf_op jit(solution)/shard_map/ppermute | solution.py:48
  163.0 9.8 %collective-permute-start.10 = (bf16[896,896]{1,0:T(8,128)(2,1)}, bf16[896,896]{1,0:T(8,128)(2,1)}, u32[]{:S(2)}, u32[]{:S(2)}) collective-permute-start(bf16[896,896]{1,0:T(8,128)(2,1)} %collective-permute-done.6.rest_3_), channel_id=1, source_target_pairs={{0,1},{2,3},{4,5},{6,7},{9,8},{11,10},{13,12},{15,14},{16,17},{18,... | collective-permute-start | bytes 4816904 | tf_op jit(solution)/shard_map/ppermute | solution.py:48
  166.4 3.9 %collective-permute-start.20 = (bf16[1152,256]{1,0:T(8,128)(2,1)S(1)}, bf16[1152,256]{1,0:T(8,128)(2,1)S(1)}, u32[]{:S(2)}, u32[]{:S(2)}) collective-permute-start(bf16[1152,256]{1,0:T(8,128)(2,1)S(1)} %pad_maximum_fusion.2.pair), channel_id=1, source_target_pairs={{0,1},{1,0},{2,3},{3,2},{4,5},{5,4},{6,7},{7,6},{8,9},{9,8},{10,11... | collective-permute-start | bytes 1769480 | tf_op jit(solution)/shard_map/ppermute | solution.py:48
  168.2 14.4 %copy-start = (bf16[896,896]{1,0:T(8,128)(2,1)}, bf16[896,896]{1,0:T(8,128)(2,1)S(1)}, u32[]{:S(2)}) copy-start(bf16[896,896]{1,0:T(8,128)(2,1)S(1)} %broadcast_select_fusion.rest_1_) | copy-start | bytes 4816900
  168.3 38.0 %collective-permute-start.26 = (bf16[896,896]{1,0:T(8,128)(2,1)S(1)}, bf16[896,896]{1,0:T(8,128)(2,1)S(1)}, u32[]{:S(2)}, u32[]{:S(2)}) collective-permute-start(bf16[896,896]{1,0:T(8,128)(2,1)S(1)} %constant_dynamic-update-slice_fusion.2.rest_0_), channel_id=1, source_target_pairs={{0,4},{1,5},{2,6},{3,7},{4,0},{5,1},{6,2},{7,3},{8,12},{9,13},{10,... | collective-permute-start | bytes 4816904 | tf_op jit(solution)/shard_map/ppermute | solution.py:48
  170.4 70.0 %collective-permute-start.27 = (bf16[896,896]{1,0:T(8,128)(2,1)S(1)}, bf16[896,896]{1,0:T(8,128)(2,1)S(1)}, u32[]{:S(2)}, u32[]{:S(2)}) collective-permute-start(bf16[896,896]{1,0:T(8,128)(2,1)S(1)} %broadcast_select_fusion.rest_1_), channel_id=1, source_target_pairs={{0,4},{1,5},{2,6},{3,7},{4,0},{5,1},{6,2},{7,3},{8,12},{9,13},{10,... | collective-permute-start | bytes 4816904 | tf_op jit(solution)/shard_map/ppermute | solution.py:48
  172.0 10.7 %collective-permute-start.21 = (bf16[256,256]{1,0:T(8,128)(2,1)S(1)}, bf16[256,256]{1,0:T(8,128)(2,1)S(1)}, u32[]{:S(2)}, u32[]{:S(2)}) collective-permute-start(bf16[256,256]{1,0:T(8,128)(2,1)S(1)} %pad_maximum_fusion.3), channel_id=1, source_target_pairs={{0,16},{1,17},{2,18},{3,19},{4,20},{5,21},{6,22},{7,23},{8,24},{9,... | collective-permute-start | bytes 393224 | tf_op jit(solution)/shard_map/ppermute | solution.py:48
  190.7 8.6 %copy-start.16 = (bf16[256,896]{1,0:T(8,128)(2,1)S(1)}, bf16[256,896]{1,0:T(8,128)(2,1)}, u32[]{:S(2)}) copy-start(bf16[256,896]{1,0:T(8,128)(2,1)} %attend.3) | copy-start | bytes 1376260
  190.7 8.6 %collective-permute-start.30 = (bf16[256,896]{1,0:T(8,128)(2,1)}, bf16[256,896]{1,0:T(8,128)(2,1)S(1)}, u32[]{:S(2)}, u32[]{:S(2)}) collective-permute-start(bf16[256,896]{1,0:T(8,128)(2,1)} %attend.3), channel_id=1, source_target_pairs={{1,8},{3,10},{5,12},{7,14},{8,1},{10,3},{12,5},{14,7},{17,24},{19,... | collective-permute-start | bytes 1376264 | tf_op jit(solution)/shard_map/ppermute | solution.py:48
  198.4 52.2 %collective-permute-start.22 = (bf16[256,896]{1,0:T(8,128)(2,1)}, bf16[256,896]{1,0:T(8,128)(2,1)S(1)}, u32[]{:S(2)}, u32[]{:S(2)}) collective-permute-start(bf16[256,896]{1,0:T(8,128)(2,1)} %attend.2), channel_id=1, source_target_pairs={{1,8},{3,10},{5,12},{7,14},{8,1},{10,3},{12,5},{14,7},{17,24},{19,... | collective-permute-start | bytes 1376264 | tf_op jit(solution)/shard_map/ppermute | solution.py:48
  206.3 34.1 %copy-start.4 = (bf16[896,896]{1,0:T(8,128)(2,1)}, bf16[896,896]{1,0:T(8,128)(2,1)S(1)}, u32[]{:S(2)}) copy-start(bf16[896,896]{1,0:T(8,128)(2,1)S(1)} %collective-permute-done.26.rest_2_) | copy-start | bytes 4816900
  250.5 10.4 %collective-permute-start.31 = (bf16[2,256,896]{2,1,0:T(8,128)(2,1)S(1)}, bf16[2,256,896]{2,1,0:T(8,128)(2,1)S(1)}, u32[]{:S(2)}, u32[]{:S(2)}) collective-permute-start(bf16[2,256,896]{2,1,0:T(8,128)(2,1)S(1)} %slice_bitcast_fusion.1), channel_id=1, source_target_pairs={{0,1},{1,0},{2,3},{3,2},{4,5},{5,4},{6,7},{7,6},{8,9},{9,8},{10,11... | collective-permute-start | bytes 2752520 | tf_op jit(solution)/shard_map/ppermute | solution.py:48
  260.4 2.6 collective-permute-start.28
  261.2 13.4 %collective-permute-start.32 = (bf16[256,896]{1,0:T(8,128)(2,1)S(1)}, bf16[256,896]{1,0:T(8,128)(2,1)S(1)}, u32[]{:S(2)}, u32[]{:S(2)}) collective-permute-start(bf16[256,896]{1,0:T(8,128)(2,1)S(1)} %fusion.5), channel_id=1, source_target_pairs={{0,2},{1,3},{2,0},{3,1},{4,6},{5,7},{6,4},{7,5},{8,10},{9,11},{10,... | collective-permute-start | bytes 1376264 | tf_op jit(solution)/shard_map/ppermute | solution.py:48
  263.3 20.5 %collective-permute-start.29 = (bf16[256,896]{1,0:T(8,128)(2,1)S(1)}, bf16[256,896]{1,0:T(8,128)(2,1)S(1)}, u32[]{:S(2)}, u32[]{:S(2)}) collective-permute-start(bf16[256,896]{1,0:T(8,128)(2,1)S(1)} %fusion.4), channel_id=1, source_target_pairs={{0,2},{1,3},{2,0},{3,1},{4,6},{5,7},{6,4},{7,5},{8,10},{9,11},{10,... | collective-permute-start | bytes 1376264 | tf_op jit(solution)/shard_map/ppermute | solution.py:48
  (11 other events, 31.6 us)

commit v3 on v2

--- a/solution.py
+++ b/solution.py
@@ -113,37 +113,33 @@
     )(info, hidden, first, second, gain.reshape(1, width))
 
 
-def fetch_weights(info, refs, weights, sems, count):
-    matched, big, l, x, swap = info[0], info[4], info[5], info[6], info[8]
-    rows = refs[0].shape[0] // 2
-    own, copied = refs[:count], refs[count:]
-    half = count // 2
-
-    def copy(source, i, j):
-        flip, m = i // half, i % half
-        place = j if (copied or m == 0) else j ^ swap
-        block = 4 * (big ^ m) + 2 * (l ^ place) + (x ^ flip)
+def fetch_weights(info, keys, refs, weights, sems, first_col=0):
+    matched, big, l, x = info[0], info[4], info[5], info[6]
+    count = len(keys)
+    rows, cols = refs[0].shape[0], weights.shape[1]
+
+    def copy(ref, i):
+        flip_big, flip_l, flip_x = keys[i]
+        block = 4 * (big ^ flip_big) + 2 * (l ^ flip_l) + (x ^ flip_x)
         return pltpu.make_async_copy(
-            source[i].at[pl.ds(j * rows, rows), :],
+            ref.at[:, pl.ds(first_col, cols)],
             weights.at[pl.ds(pl.multiple_of(block * rows, 16), rows), :],
-            sems.at[2 * i + j],
+            sems.at[i],
         )
 
     for i in range(count):
-        for j in range(2):
-            if copied:
-                pl.when(matched == 1)(copy(own, i, j).start)
-                pl.when(matched == 0)(copy(copied, i, j).start)
-            else:
-                copy(own, i, j).start()
+        if len(refs) > count:
+            pl.when(matched == 1)(copy(refs[i], i).start)
+            pl.when(matched == 0)(copy(refs[count + i], i).start)
+        else:
+            copy(refs[i], i).start()
     for i in range(count):
-        for j in range(2):
-            copy(own, i, j).wait()
-
-
-def query_kernel(count, info, normed, bias, *rest):
-    refs, (out, weights, sems) = rest[: 2 * count], rest[2 * count :]
-    fetch_weights(info, refs, weights, sems, count)
+        copy(refs[i], i).wait()
+
+
+def query_kernel(keys, info, normed, bias, *rest):
+    refs, (out, weights, sems) = rest[:-3], rest[-3:]
+    fetch_weights(info, keys, refs, weights, sems)
     tile = 256
     for i in range(out.shape[0] // tile):
         rows = slice(i * tile, (i + 1) * tile)
@@ -151,9 +147,9 @@
         out[rows, :] = (product + bias[...]).astype(jnp.bfloat16)
 
 
-def keyval_kernel(count, info, normed, pooled, bias, *rest):
-    refs, (out, weights, sems) = rest[: 2 * count], rest[2 * count :]
-    fetch_weights(info, refs, weights, sems, count)
+def keyval_kernel(first_col, keys, info, normed, pooled, bias, *rest):
+    refs, (out, weights, sems) = rest[:-3], rest[-3:]
+    fetch_weights(info, keys, refs, weights, sems, first_col)
     rows = normed.shape[0]
     cols = out.shape[1]
     product = jnp.dot(normed[...], weights[:, :cols], preferred_element_type=jnp.float32)
@@ -163,17 +159,17 @@
 
 
 def project(kernel, out_rows, out_cols, info, left, bias, own, copied):
-    count = len(own)
+    keys = tuple(own)
     width = left[0].shape[1]
-    cols = own[0].shape[1]
+    cols = bias.shape[0]
     return pl.pallas_call(
-        functools.partial(kernel, count),
+        functools.partial(kernel, keys),
         out_shape=jax.ShapeDtypeStruct((out_rows, out_cols), jnp.bfloat16),
-        in_specs=[smem()] + [vmem()] * (len(left) + 1) + [hbm()] * (2 * count),
+        in_specs=[smem()] + [vmem()] * (len(left) + 1) + [hbm()] * (2 * len(keys)),
         out_specs=vmem(),
         scratch_shapes=[
             pltpu.VMEM((width, cols), jnp.bfloat16),
-            pltpu.SemaphoreType.DMA((2 * count,)),
+            pltpu.SemaphoreType.DMA((len(keys),)),
         ],
         compiler_params=params(),
         cost_estimate=pl.CostEstimate(
@@ -182,7 +178,7 @@
             transcendentals=0,
         ),
         name="project",
-    )(info, *left, bias.reshape(1, -1), *own, *copied)
+    )(info, *left, bias.reshape(1, -1), *[own[k] for k in keys], *[copied[k] for k in keys])
 
 
 def attend_kernel(tokens, beacons, first_row, info, ratios, queries, pair, far_pair, *rest):
@@ -275,9 +271,9 @@
     )(info, ratios, queries, pair, far_pair, *beacons)
 
 
-def out_kernel(count, info, attention, *rest):
-    refs, (out, weights, sems) = rest[:count], rest[count:]
-    fetch_weights(info, refs, weights, sems, count)
+def out_kernel(keys, info, attention, *rest):
+    refs, (out, weights, sems) = rest[:-3], rest[-3:]
+    fetch_weights(info, keys, refs, weights, sems)
     width = out.shape[3]
     for i in (1, 0):
         for j in (1, 0):
@@ -290,73 +286,27 @@
 
 def out_project(info, attention, pieces):
     tokens, depth = attention.shape
-    count = len(pieces)
-    width = count * pieces[0].shape[0] // KVH
+    keys = tuple(pieces)
+    width = len(keys) * pieces[keys[0]].shape[0] // KVH
     return pl.pallas_call(
-        functools.partial(out_kernel, count),
+        functools.partial(out_kernel, keys),
         out_shape=jax.ShapeDtypeStruct((2, 2, tokens, width), jnp.bfloat16),
-        in_specs=[smem(), vmem()] + [hbm()] * count,
+        in_specs=[smem(), vmem()] + [hbm()] * len(keys),
         out_specs=vmem(),
         scratch_shapes=[
             pltpu.VMEM((KVH * width, depth), jnp.bfloat16),
-            pltpu.SemaphoreType.DMA((2 * count,)),
+            pltpu.SemaphoreType.DMA((len(keys),)),
         ],
         compiler_params=params(),
         cost_estimate=pl.CostEstimate(
             flops=8 * tokens * width * depth, bytes_accessed=8 * width * depth, transcendentals=0
         ),
         name="out_project",
-    )(info, attention, *pieces)
-
-
-def gather_pieces(shard, n_seq):
-    other = send(
-        shard, n_seq, lambda big, l, x, y, c: (big, 1 - l, x, y, c) if c != l else None
-    )
-    near = [jnp.concatenate([shard, other], axis=0)]
-    bit = 1
-    while bit < n_seq // SPLIT:
-        near += [
-            send(
-                piece,
-                n_seq,
-                lambda big, l, x, y, c: (big ^ bit, l, x, y, c) if c == l else None,
-            )
-            for piece in near
-        ]
-        bit *= 2
-    across = [
-        send(piece, n_seq, lambda big, l, x, y, c: (big, l, 1 - x, y, c) if c == l else None)
-        for piece in near
-    ]
-    own = near + across
-    copied = [
-        send(piece, n_seq, lambda big, l, x, y, c: (big, l, x, y, 1 - c) if c == l else None)
-        for piece in own
-    ]
-    return own, copied
-
-
-def gather_output_pieces(shard, inner, n_seq):
-    other = send(shard, n_seq, lambda big, l, x, y, c: (big, 1 - l, x, y, c))
-    near = [jnp.concatenate([shard, other], axis=0)]
-    if n_seq == 2 * SPLIT:
-        middle = send(
-            near[0], n_seq, lambda big, l, x, y, c: (1 - big, 1 - l, x, y, c) if big != l else None
-        )
-        outer = send(
-            middle, n_seq, lambda big, l, x, y, c: (big, 1 - l, x, y, c) if big != l else None
-        )
-        near.append(jnp.where(inner, middle, outer))
-    else:
-        bit = 1
-        while bit < n_seq // SPLIT:
-            near += [
-                send(piece, n_seq, lambda big, l, x, y, c: (big ^ bit, l, x, y, c))
-                for piece in near
-            ]
-            bit *= 2
-    return near + [send(p, n_seq, lambda big, l, x, y, c: (big, l, 1 - x, y, c)) for p in near]
+    )(info, attention, *[pieces[k] for k in keys])
+
+
+def together(*values):
+    return lax.optimization_barrier(values)
 
 
 def on_device(
@@ -381,7 +331,7 @@
     matched = c == l
     segment_ids = jnp.arange(ratios.shape[0], dtype=jnp.int32)
     own_ratio = jnp.sum(jnp.where(segment_ids == big, ratios, 0))
-    inner = (big != l) & (n_seq == 2 * SPLIT)
+    inner = big != l
     info = jnp.stack(
         [
             matched.astype(jnp.int32),
@@ -392,42 +342,124 @@
             l,
             x,
             c,
-            inner.astype(jnp.int32),
         ]
     ).astype(jnp.int32)
 
+    kv_cols = 2 * keyval_weight.shape[2]
+    depth = keyval_weight.shape[0]
+    query_cols = query_weight.shape[1]
+    biases = jnp.concatenate([query_bias, keyval_bias.reshape(-1), beacon_bias.reshape(-1)])
+    shard = jnp.concatenate(
+        [
+            query_weight,
+            keyval_weight.reshape(depth, kv_cols),
+            beacon_weight.reshape(depth, kv_cols),
+        ],
+        axis=1,
+    )
+    out_shard = out_weight.T
+
+    def to_other_l(value):
+        return send(value, n_seq, lambda big, l, x, y, c: (big, 1 - l, x, y, c) if c != l else None)
+
+    def to_other_big(value, bit):
+        return send(value, n_seq, lambda big, l, x, y, c: (big ^ bit, l, x, y, c) if c == l else None)
+
+    def to_other_x(value):
+        return send(value, n_seq, lambda big, l, x, y, c: (big, l, 1 - x, y, c) if c == l else None)
+
+    def to_other_core(value):
+        return send(value, n_seq, lambda big, l, x, y, c: (big, l, x, y, 1 - c) if c == l else None)
+
+    own, copied = {(0, 0, 0): shard}, {}
+    own[0, 1, 0] = to_other_l(shard)
+    own[1, 0, 0] = to_other_big(shard, 1)
+    own[0, 0, 1] = to_other_x(shard)
     own_half = lax.dynamic_slice_in_dim(hidden, y * half, half, 0)
     first = send(
         own_half, n_seq, lambda big, l, x, y, c: (big, 1 - l, x, y, 1 - c) if c != l else None
     )
-    second = send(first, n_seq, lambda big, l, x, y, c: (big, l, x, 1 - y, c) if c != l else None)
-
-    kv_cols = 2 * keyval_weight.shape[2]
-    depth = keyval_weight.shape[0]
-    small = jnp.concatenate(
-        [keyval_weight.reshape(depth, kv_cols), beacon_weight.reshape(depth, kv_cols)], axis=1
-    )
-    biases = jnp.concatenate([query_bias, keyval_bias.reshape(-1), beacon_bias.reshape(-1)])
     other_biases = send(biases, n_seq, lambda big, l, x, y, c: (big, l, x, y, 1 - c))
     biases = jnp.where(matched, biases, other_biases)
-    query_cols = query_weight.shape[1]
-
-    small_own, small_copied = gather_pieces(small, n_seq)
-    query_own, query_copied = gather_pieces(query_weight, n_seq)
-    out_shard, _ = lax.optimization_barrier((out_weight.T, query_own[1]))
-    out_pieces = gather_output_pieces(out_shard, inner, n_seq)
+    copied[0, 0, 0] = to_other_core(shard)
+
+    own[0, 1, 0], own[1, 0, 0], own[0, 0, 1] = together(own[0, 1, 0], own[1, 0, 0], own[0, 0, 1])
+    own[1, 1, 0] = to_other_big(own[0, 1, 0], 1)
+    own[0, 1, 1] = to_other_x(own[0, 1, 0])
+    own[1, 0, 1] = to_other_x(own[1, 0, 0])
+    for key in ((0, 1, 0), (1, 0, 0), (0, 0, 1)):
+        copied[key] = to_other_core(own[key])
+
+    own[1, 1, 0], own[0, 1, 1], own[1, 0, 1], first, out_shard = together(
+        own[1, 1, 0], own[0, 1, 1], own[1, 0, 1], first, out_shard
+    )
+    second = send(first, n_seq, lambda big, l, x, y, c: (big, l, x, 1 - y, c) if c != l else None)
+    own[1, 1, 1] = to_other_x(own[1, 1, 0])
+    for key in ((1, 1, 0), (0, 1, 1), (1, 0, 1)):
+        copied[key] = to_other_core(own[key])
+    bit = 2
+    while bit < n_seq // SPLIT:
+        for key in list(own):
+            new = (key[0] ^ bit, key[1], key[2])
+            own[new] = to_other_big(own[key], bit)
+            copied[new] = to_other_core(own[new])
+        bit *= 2
+
+    def swap_l(value):
+        return send(value, n_seq, lambda big, l, x, y, c: (big, 1 - l, x, y, c))
+
+    def swap_inner(value):
+        return send(
+            value, n_seq, lambda big, l, x, y, c: (1 - big, 1 - l, x, y, c) if big != l else None
+        )
+
+    def to_outer(value):
+        return send(value, n_seq, lambda big, l, x, y, c: (big, 1 - l, x, y, c) if big != l else None)
+
+    def swap_x(value):
+        return send(value, n_seq, lambda big, l, x, y, c: (big, l, 1 - x, y, c))
+
+    out_pieces = {(0, 0, 0): out_shard, (0, 1, 0): swap_l(out_shard)}
+    if n_seq == 2 * SPLIT:
+        middle_own = swap_inner(out_shard)
+        own[1, 1, 1], out_pieces[0, 1, 0], middle_own = together(
+            own[1, 1, 1], out_pieces[0, 1, 0], middle_own
+        )
+        middle_other = swap_inner(out_pieces[0, 1, 0])
+        outer_own = to_outer(middle_own)
+        out_pieces[0, 0, 1] = swap_x(out_shard)
+        middle_other, outer_own, out_pieces[0, 0, 1] = together(
+            middle_other, outer_own, out_pieces[0, 0, 1]
+        )
+        outer_other = to_outer(middle_other)
+        out_pieces[1, 1, 0] = jnp.where(inner, middle_own, outer_other)
+        out_pieces[1, 0, 0] = jnp.where(inner, middle_other, outer_own)
+    else:
+        bit = 1
+        while bit < n_seq // SPLIT:
+            for key in list(out_pieces):
+                out_pieces[key[0] ^ bit, key[1], 0] = send(
+                    out_pieces[key], n_seq, lambda big, l, x, y, c: (big ^ bit, l, x, y, c)
+                )
+            bit *= 2
+    for key in list(out_pieces):
+        if (key[0], key[1], 1) not in out_pieces:
+            out_pieces[key[0], key[1], 1] = swap_x(out_pieces[key])
+    copied[1, 1, 1] = to_other_core(own[1, 1, 1])
+    if n_seq > 2 * SPLIT:
+        copied = {key: copied[key] for key in own}
 
     normed, pooled = norm_and_pool(info, hidden, first, second, norm_gain)
     slots_dev = rows_dev // R_MIN
     keyval = project(
-        keyval_kernel,
+        functools.partial(keyval_kernel, query_cols),
         rows_dev + slots_dev,
         kv_cols,
         info,
         [normed, pooled],
         biases[query_cols:],
-        small_own,
-        small_copied,
+        own,
+        copied,
     )
     beside = send(keyval, n_seq, lambda big, l, x, y, c: (big, l, 1 - x, y, c))
     pair = jnp.concatenate([keyval, beside], axis=0)
@@ -457,8 +489,8 @@
         info,
         [normed],
         biases[:query_cols],
-        query_own,
-        query_copied,
+        own,
+        copied,
     )
     parts = 2
     part = rows_dev // parts

time: 288 us -> 243 us (0.84)
  waiting for transfers between devices: 154 us -> 76.3 us
  starting transfers between devices: 57.1 us -> 89.9 us
    ppermute x33 -> x36, waiting for transfers between devices: 154 us -> 76.3 us  [send(): return lax.ppermute(value, AXES, moves(n_seq, rule))]
    ppermute x33 -> x36, starting transfers between devices: 57.1 us -> 89.9 us  [send(): return lax.ppermute(value, AXES, moves(n_seq, rule))]
    unnamed x55 -> x64, local copies, waits for them, and re-layouts: 4.11 us -> 6.52 us
  transfers between devices with their start and end apart: 33 -> 36, of which waited for: 12 -> 12; matrix products, arithmetic and copies ran while one was open for 6% -> 6% of each run, Pallas kernels for 18% -> 21%
where the time goes in v3:
time: 243 us; the launch traced here: 241 us
  starting transfers between devices  89.9 us (37%)
  waiting for transfers between devices  76.3 us (31%)
  Pallas kernels  51.2 us (21%)
  local copies, waits for them, and re-layouts  14.7 us (6%)
  other arithmetic  6.29 us (3%)
  between operations  2.71 us (1%)
    ppermute x36, starting transfers between devices, send(): return lax.ppermute(value, AXES, moves(n_seq, rule))  89.9 us
    ppermute x36, waiting for transfers between devices, send(): return lax.ppermute(value, AXES, moves(n_seq, rule))  76.3 us
    pallas_call x2, Pallas kernels, project(): pl.pallas_call(functools.partial(kernel, keys), out_shape=jax.ShapeDtypeS...  16.3 us
    pallas_call x2, Pallas kernels, out_project(): pl.pallas_call(functools.partial(out_kernel, keys), out_shape=jax.ShapeDt...  15.1 us
    pallas_call x2, Pallas kernels, attend(): pl.pallas_call(functools.partial(attend_kernel, tokens, len(beacons), fir...  14.2 us
    unnamed x64, local copies, waits for them, and re-layouts  6.52 us
    pallas_call x1, Pallas kernels, norm_and_pool(): pl.pallas_call(norm_kernel, out_shape=(jax.ShapeDtypeStruct((rows, width)...  5.49 us
  transfers between devices with their start and end apart: 36, of which 12 were waited for; matrix products, arithmetic and copies ran while one was open for 6% of the time, Pallas kernels for 21%

profile of v3, /device:TPU:0, one launch (start us, length us, event | category | flops | bytes accessed | tf_op | source)
XLA Modules:
  0.0 241.2 jit_solution(9886785900942197334)
XLA Ops:
  0.0 1.2 constant_dynamic-update-slice_fusion
  2.3 1.3 collective-permute-start
  3.6 5.9 %collective-permute-start.1 = (bf16[448,1408]{1,0:T(8,128)(2,1)S(1)}, bf16[448,1408]{1,0:T(8,128)(2,1)}, u32[]{:S(2)}, u32[]{:S(2)}) collective-permute-start(bf16[448,1408]{1,0:T(8,128)(2,1)S(1)} %bitcast_dynamic-update-slice_fusion.rest_0_), channel_id=1, source_target_pairs={{0,16},{2,18},{4,20},{6,22},{9,25},{11,27},{13,29},{15,31},{16,0},... | collective-permute-start | bytes 3784712 | tf_op jit(solution)/shard_map/ppermute | solution.py:48
  9.5 3.4 %collective-permute-start.2 = (bf16[448,1408]{1,0:T(8,128)(2,1)S(1)}, bf16[448,1408]{1,0:T(8,128)(2,1)}, u32[]{:S(2)}, u32[]{:S(2)}) collective-permute-start(bf16[448,1408]{1,0:T(8,128)(2,1)S(1)} %bitcast_dynamic-update-slice_fusion.rest_0_), channel_id=1, source_target_pairs={{0,4},{2,6},{4,0},{6,2},{9,13},{11,15},{13,9},{15,11},{16,20},{18,... | collective-permute-start | bytes 3784712 | tf_op jit(solution)/shard_map/ppermute | solution.py:48
  13.0 1.7 constant_dynamic-slice_fusion
  15.5 16.9 %collective-permute-done.rest_1_ = bf16[448,1408]{1,0:T(8,128)(2,1)S(1)} collective-permute-done((bf16[448,1408]{1,0:T(8,128)(2,1)S(1)}, bf16[448,1408]{1,0:T(8,128)(2,1)S(1)}, u32[]{:S(2)}, u32[]{:S(2)}) %collective-permute-start) | collective-permute-done | bytes 1261600 | tf_op jit(solution)/shard_map/ppermute | solution.py:48
  32.4 5.6 %collective-permute-done.1.rest_2_ = bf16[448,1408]{1,0:T(8,128)(2,1)} collective-permute-done((bf16[448,1408]{1,0:T(8,128)(2,1)S(1)}, bf16[448,1408]{1,0:T(8,128)(2,1)}, u32[]{:S(2)}, u32[]{:S(2)}) %collective-permute-start.1) | collective-permute-done | bytes 1261600 | tf_op jit(solution)/shard_map/ppermute | solution.py:48
  38.0 5.1 %collective-permute-start.3 = (bf16[448,1408]{1,0:T(8,128)(2,1)S(1)}, bf16[448,1408]{1,0:T(8,128)(2,1)S(1)}, u32[]{:S(2)}, u32[]{:S(2)}) collective-permute-start(bf16[448,1408]{1,0:T(8,128)(2,1)S(1)} %collective-permute-done.rest_1_), channel_id=1, source_target_pairs={{0,16},{2,18},{4,20},{6,22},{9,25},{11,27},{13,29},{15,31},{16,0},... | collective-permute-start | bytes 3784712 | tf_op jit(solution)/shard_map/ppermute | solution.py:48
  43.1 3.4 %collective-permute-start.4 = (bf16[448,1408]{1,0:T(8,128)(2,1)S(1)}, bf16[448,1408]{1,0:T(8,128)(2,1)S(1)}, u32[]{:S(2)}, u32[]{:S(2)}) collective-permute-start(bf16[448,1408]{1,0:T(8,128)(2,1)S(1)} %collective-permute-done.rest_1_), channel_id=1, source_target_pairs={{0,4},{2,6},{4,0},{6,2},{9,13},{11,15},{13,9},{15,11},{16,20},{18,... | collective-permute-start | bytes 3784712 | tf_op jit(solution)/shard_map/ppermute | solution.py:48
  46.5 2.4 %collective-permute-start.5 = (bf16[448,1408]{1,0:T(8,128)(2,1)}, bf16[448,1408]{1,0:T(8,128)(2,1)}, u32[]{:S(2)}, u32[]{:S(2)}) collective-permute-start(bf16[448,1408]{1,0:T(8,128)(2,1)} %collective-permute-done.1.rest_2_), channel_id=1, source_target_pairs={{0,4},{2,6},{4,0},{6,2},{9,13},{11,15},{13,9},{15,11},{16,20},{18,... | collective-permute-start | bytes 3784712 | tf_op jit(solution)/shard_map/ppermute | solution.py:48
  48.9 1.4 collective-permute-start.12
  50.3 16.9 %collective-permute-start.13 = (bf16[448,1408]{1,0:T(8,128)(2,1)S(1)}, bf16[448,1408]{1,0:T(8,128)(2,1)S(1)}, u32[]{:S(2)}, u32[]{:S(2)}) collective-permute-start(bf16[448,1408]{1,0:T(8,128)(2,1)S(1)} %collective-permute-done.rest_1_), channel_id=1, source_target_pairs={{0,1},{2,3},{4,5},{6,7},{9,8},{11,10},{13,12},{15,14},{16,17},{18,... | collective-permute-start | bytes 3784712 | tf_op jit(solution)/shard_map/ppermute | solution.py:48
  67.2 4.0 %collective-permute-done.3.rest_4_ = bf16[448,1408]{1,0:T(8,128)(2,1)S(1)} collective-permute-done((bf16[448,1408]{1,0:T(8,128)(2,1)S(1)}, bf16[448,1408]{1,0:T(8,128)(2,1)S(1)}, u32[]{:S(2)}, u32[]{:S(2)}) %collective-permute-start.3) | collective-permute-done | bytes 1261600 | tf_op jit(solution)/shard_map/ppermute | solution.py:48
  71.2 4.5 %collective-permute-done.5.rest_6_ = bf16[448,1408]{1,0:T(8,128)(2,1)} collective-permute-done((bf16[448,1408]{1,0:T(8,128)(2,1)}, bf16[448,1408]{1,0:T(8,128)(2,1)}, u32[]{:S(2)}, u32[]{:S(2)}) %collective-permute-start.5) | collective-permute-done | bytes 1261600 | tf_op jit(solution)/shard_map/ppermute | solution.py:48
  75.7 3.4 %collective-permute-start.9 = (bf16[448,1408]{1,0:T(8,128)(2,1)S(1)}, bf16[448,1408]{1,0:T(8,128)(2,1)}, u32[]{:S(2)}, u32[]{:S(2)}) collective-permute-start(bf16[448,1408]{1,0:T(8,128)(2,1)S(1)} %collective-permute-done.3.rest_4_), channel_id=1, source_target_pairs={{0,4},{2,6},{4,0},{6,2},{9,13},{11,15},{13,9},{15,11},{16,20},{18,... | collective-permute-start | bytes 3784712 | tf_op jit(solution)/shard_map/ppermute | solution.py:48
  80.4 2.1 collective-permute-start.14
  82.5 1.4 collective-permute-start.15
  83.9 1.5 collective-permute-start.11
  85.5 6.1 %collective-permute-done.10.rest_1_ = bf16[448,896]{1,0:T(8,128)(2,1)} collective-permute-done((bf16[448,896]{1,0:T(8,128)(2,1)S(1)}, bf16[448,896]{1,0:T(8,128)(2,1)}, u32[]{:S(2)}, u32[]{:S(2)}) %collective-permute-start.10) | collective-permute-done | bytes 802848 | tf_op jit(solution)/shard_map/ppermute | solution.py:48
  92.4 1.4 collective-permute-start.16
  94.8 1.4 collective-permute-start.17
  96.1 2.4 %collective-permute-start.18 = (bf16[448,1408]{1,0:T(8,128)(2,1)}, bf16[448,1408]{1,0:T(8,128)(2,1)}, u32[]{:S(2)}, u32[]{:S(2)}) collective-permute-start(bf16[448,1408]{1,0:T(8,128)(2,1)} %collective-permute-done.5.rest_6_), channel_id=1, source_target_pairs={{0,1},{2,3},{4,5},{6,7},{9,8},{11,10},{13,12},{15,14},{16,17},{18,... | collective-permute-start | bytes 3784712 | tf_op jit(solution)/shard_map/ppermute | solution.py:48
  98.6 2.3 collective-permute-start.19
  100.9 1.5 collective-permute-start.26
  102.4 1.6 collective-permute-start.24
  104.0 1.2 copy-done.19
  105.2 1.3 collective-permute-start.25
  111.6 5.5 %norm_pool.1 = (bf16[512,3584]{1,0:T(8,128)(2,1)}, bf16[64,3584]{1,0:T(8,128)(2,1)}) custom-call(s32[8]{0:T(128)} %stack.39.info, bf16[512,3584]{1,0:T(8,128)(2,1)} %hidden.1, bf16[256,3584]{1,0:T(8,128)(2,1)} %copy-done.18, bf16[256,3584]{1,0:T(8,128)(2,1)} %copy-done.19, f32[1,3584]{1,0:T(1,128)} %reshape.29.gain), custom_call_target="tpu_custom_call" | custom-call | flops 234881024 | bytes 7340032 | tf_op jit(solution)/shard_map/norm_pool/pallas_call | solution.py:99
  117.1 6.5 %project.3 = bf16[576,256]{1,0:T(8,128)(2,1)} custom-call(s32[8]{0:T(128)} %stack.39.info, bf16[512,3584]{1,0:T(8,128)(2,1)} %get-tuple-element.24.normed, bf16[64,3584]{1,0:T(8,128)(2,1)} %get-tuple-element.31.pooled, f32[1,512]{1,0:T(1,128)} %bitcast.55, bf16[448,1408]{1,0:T(8,128)(2,1)} %copy-done, bf16[448,1408]{1,0:T(8,128)(2,1)} %copy-done.5, ...), custom_call_target="tpu_custom_call" | custom-call | flops 1056964608 | bytes 7798784 | tf_op jit(solution)/shard_map/project/pallas_call | solution.py:165
  124.8 1.5 collective-permute-start.28
  126.3 12.2 %collective-permute-done.25 = bf16[448,896]{1,0:T(8,128)(2,1)} collective-permute-done((bf16[448,896]{1,0:T(8,128)(2,1)}, bf16[448,896]{1,0:T(8,128)(2,1)}, u32[]{:S(2)}, u32[]{:S(2)}) %collective-permute-start.25) | collective-permute-done | bytes 802848 | tf_op jit(solution)/shard_map/ppermute | solution.py:48
  138.5 1.5 collective-permute-start.27
  142.1 1.2 broadcast_select_fusion.rest_4_
  143.3 1.6 collective-permute-start.30
  145.6 9.8 %project.2.queries = bf16[512,896]{1,0:T(8,128)(2,1)} custom-call(s32[8]{0:T(128)} %stack.39.info, bf16[512,3584]{1,0:T(8,128)(2,1)} %get-tuple-element.24.normed, f32[1,896]{1,0:T(1,128)} %reshape.32.bias, bf16[448,1408]{1,0:T(8,128)(2,1)} %copy-done, bf16[448,1408]{1,0:T(8,128)(2,1)} %copy-done.5, bf16[448,1408]{1,0:T(8,128)(2,1)} %collective-permute-done.1.rest_2_, ...), custom_call_target="tpu_custom_call" | custom-call | flops 3288334336 | bytes 10092544 | tf_op jit(solution)/shard_map/project/pallas_call | solution.py:165
  155.6 10.4 %collective-permute-start.22 = (bf16[256,256]{1,0:T(8,128)(2,1)S(1)}, bf16[256,256]{1,0:T(8,128)(2,1)S(1)}, u32[]{:S(2)}, u32[]{:S(2)}) collective-permute-start(bf16[256,256]{1,0:T(8,128)(2,1)S(1)} %pad_maximum_fusion.2), channel_id=1, source_target_pairs={{0,16},{1,17},{2,18},{3,19},{4,20},{5,21},{6,22},{7,23},{8,24},{9,... | collective-permute-start | bytes 393224 | tf_op jit(solution)/shard_map/ppermute | solution.py:48
  166.7 5.8 %collective-permute-done.22.rest_0_ = bf16[256,256]{1,0:T(8,128)(2,1)S(1)} collective-permute-done((bf16[256,256]{1,0:T(8,128)(2,1)S(1)}, bf16[256,256]{1,0:T(8,128)(2,1)S(1)}, u32[]{:S(2)}, u32[]{:S(2)}) %collective-permute-start.22) | collective-permute-done | bytes 131104 | tf_op jit(solution)/shard_map/ppermute | solution.py:48
  173.2 7.4 %attend.3 = bf16[256,896]{1,0:T(8,128)(2,1)} custom-call(s32[8]{0:T(128)} %stack.39.info, s32[2]{0:T(128)} %ratios.3, bf16[512,896]{1,0:T(8,128)(2,1)} %project.2.queries, bf16[1152,256]{1,0:T(8,128)(2,1)} %copy-done.20, bf16[1152,256]{1,0:T(8,128)(2,1)} %copy-done.26, bf16[256,256]{1,0:T(8,128)(2,1)} %copy-done.29), custom_call_target="tpu_custom_call" | custom-call | flops 2113929216 | bytes 1835008 | tf_op jit(solution)/shard_map/attend/pallas_call | solution.py:251
  181.4 6.8 %attend.2 = bf16[256,896]{1,0:T(8,128)(2,1)} custom-call(s32[8]{0:T(128)} %stack.39.info, s32[2]{0:T(128)} %ratios.3, bf16[512,896]{1,0:T(8,128)(2,1)} %project.2.queries, bf16[1152,256]{1,0:T(8,128)(2,1)} %copy-done.20, bf16[1152,256]{1,0:T(8,128)(2,1)} %copy-done.26, bf16[256,256]{1,0:T(8,128)(2,1)} %copy-done.29), custom_call_target="tpu_custom_call" | custom-call | flops 2113929216 | bytes 1835008 | tf_op jit(solution)/shard_map/attend/pallas_call | solution.py:251
  192.0 7.6 %out_project.3 = bf16[2,2,256,896]{3,2,1,0:T(8,128)(2,1)} custom-call(s32[8]{0:T(128)} %stack.39.info, bf16[256,896]{1,0:T(8,128)(2,1)} %broadcast_select_fusion.2.attention, bf16[448,896]{1,0:T(8,128)(2,1)} %bitcast.48, bf16[448,896]{1,0:T(8,128)(2,1)} %collective-permute-done.10.rest_1_, bf16[448,896]{1,0:T(8,128)(2,1)} %collective-permute-done.26.rest_2_, ...), custom_call_target="tpu_custom_call" | custom-call | flops 1644167168 | bytes 6422528 | tf_op jit(solution)/shard_map/out_project/pallas_call | solution.py:291
  199.6 1.3 slice_bitcast_fusion.1
  200.9 6.2 %collective-permute-start.34 = (bf16[2,256,896]{2,1,0:T(8,128)(2,1)S(1)}, bf16[2,256,896]{2,1,0:T(8,128)(2,1)S(1)}, u32[]{:S(2)}, u32[]{:S(2)}) collective-permute-start(bf16[2,256,896]{2,1,0:T(8,128)(2,1)S(1)} %slice_bitcast_fusion.1), channel_id=1, source_target_pairs={{0,1},{1,0},{2,3},{3,2},{4,5},{5,4},{6,7},{7,6},{8,9},{9,8},{10,11... | collective-permute-start | bytes 2752520 | tf_op jit(solution)/shard_map/ppermute | solution.py:48
  208.0 7.6 %out_project.2 = bf16[2,2,256,896]{3,2,1,0:T(8,128)(2,1)} custom-call(s32[8]{0:T(128)} %stack.39.info, bf16[256,896]{1,0:T(8,128)(2,1)} %broadcast_select_fusion.3.attention, bf16[448,896]{1,0:T(8,128)(2,1)} %bitcast.49, bf16[448,896]{1,0:T(8,128)(2,1)} %collective-permute-done.10.rest_1_, bf16[448,896]{1,0:T(8,128)(2,1)} %collective-permute-done.26.rest_2_, ...), custom_call_target="tpu_custom_call" | custom-call | flops 1644167168 | bytes 6422528 | tf_op jit(solution)/shard_map/out_project/pallas_call | solution.py:291
  215.6 1.4 slice_bitcast_fusion.4
  217.6 1.6 collective-permute-start.35
  219.8 1.6 collective-permute-start.32
  221.3 9.7 %collective-permute-done.35 = bf16[256,896]{1,0:T(8,128)(2,1)S(1)} collective-permute-done((bf16[256,896]{1,0:T(8,128)(2,1)S(1)}, bf16[256,896]{1,0:T(8,128)(2,1)S(1)}, u32[]{:S(2)}, u32[]{:S(2)}) %collective-permute-start.35) | collective-permute-done | bytes 458784 | tf_op jit(solution)/shard_map/ppermute | solution.py:48
  231.1 9.0 %collective-permute-done.32 = bf16[256,896]{1,0:T(8,128)(2,1)S(1)} collective-permute-done((bf16[256,896]{1,0:T(8,128)(2,1)S(1)}, bf16[256,896]{1,0:T(8,128)(2,1)S(1)}, u32[]{:S(2)}, u32[]{:S(2)}) %collective-permute-start.32) | collective-permute-done | bytes 458784 | tf_op jit(solution)/shard_map/ppermute | solution.py:48
  (123 shorter events, 21.2 us)
Async XLA Ops:
  2.3 46.7 %copy-start = (bf16[448,1408]{1,0:T(8,128)(2,1)}, bf16[448,1408]{1,0:T(8,128)(2,1)S(1)}, u32[]{:S(2)}) copy-start(bf16[448,1408]{1,0:T(8,128)(2,1)S(1)} %bitcast_dynamic-update-slice_fusion.rest_0_) | copy-start | bytes 3784708
  2.3 30.1 %collective-permute-start = (bf16[448,1408]{1,0:T(8,128)(2,1)S(1)}, bf16[448,1408]{1,0:T(8,128)(2,1)S(1)}, u32[]{:S(2)}, u32[]{:S(2)}) collective-permute-start(bf16[448,1408]{1,0:T(8,128)(2,1)S(1)} %bitcast_dynamic-update-slice_fusion.rest_0_), channel_id=1, source_target_pairs={{1,9},{3,11},{5,13},{7,15},{8,0},{10,2},{12,4},{14,6},{17,25},{19,... | collective-permute-start | bytes 3784712 | tf_op jit(solution)/shard_map/ppermute | solution.py:48
  3.6 34.4 %collective-permute-start.1 = (bf16[448,1408]{1,0:T(8,128)(2,1)S(1)}, bf16[448,1408]{1,0:T(8,128)(2,1)}, u32[]{:S(2)}, u32[]{:S(2)}) collective-permute-start(bf16[448,1408]{1,0:T(8,128)(2,1)S(1)} %bitcast_dynamic-update-slice_fusion.rest_0_), channel_id=1, source_target_pairs={{0,16},{2,18},{4,20},{6,22},{9,25},{11,27},{13,29},{15,31},{16,0},... | collective-permute-start | bytes 3784712 | tf_op jit(solution)/shard_map/ppermute | solution.py:48
  9.5 28.5 %collective-permute-start.2 = (bf16[448,1408]{1,0:T(8,128)(2,1)S(1)}, bf16[448,1408]{1,0:T(8,128)(2,1)}, u32[]{:S(2)}, u32[]{:S(2)}) collective-permute-start(bf16[448,1408]{1,0:T(8,128)(2,1)S(1)} %bitcast_dynamic-update-slice_fusion.rest_0_), channel_id=1, source_target_pairs={{0,4},{2,6},{4,0},{6,2},{9,13},{11,15},{13,9},{15,11},{16,20},{18,... | collective-permute-start | bytes 3784712 | tf_op jit(solution)/shard_map/ppermute | solution.py:48
  13.0 62.7 %copy-start.14 = (bf16[896,448]{0,1:T(8,128)(2,1)S(1)}, bf16[896,448]{0,1:T(8,128)(2,1)}, u32[]{:S(2)}) copy-start(bf16[896,448]{0,1:T(8,128)(2,1)} %param.18) | copy-start | bytes 2408452
  13.0 66.1 %copy-start.24 = (f32[896]{0:T(1024)S(1)}, f32[896]{0:T(1024)}, u32[]{:S(2)}) copy-start(f32[896]{0:T(1024)} %param.13) | copy-start | bytes 10756
  13.0 66.1 %copy-start.27 = (f32[2,128]{1,0:T(2,128)S(1)}, f32[2,128]{1,0:T(2,128)}, u32[]{:S(2)}) copy-start(f32[2,128]{1,0:T(2,128)} %param.17) | copy-start | bytes 3076
  13.0 66.1 %copy-start.28 = (f32[2,128]{1,0:T(2,128)S(1)}, f32[2,128]{1,0:T(2,128)}, u32[]{:S(2)}) copy-start(f32[2,128]{1,0:T(2,128)} %param.15) | copy-start | bytes 3076
  13.0 93.6 %copy-start.30 = (s32[2]{0:T(128)S(1)}, s32[2]{0:T(128)}, u32[]{:S(2)}) copy-start(s32[2]{0:T(128)} %ratios.3) | copy-start | bytes 28
  13.0 96.2 %copy-start.25 = (f32[3584]{0:T(1024)S(1)}, f32[3584]{0:T(1024)}, u32[]{:S(2)}) copy-start(f32[3584]{0:T(1024)} %param.11) | copy-start | bytes 43012
  14.7 35.6 %collective-permute-start.6 = (bf16[256,3584]{1,0:T(8,128)(2,1)S(1)}, bf16[256,3584]{1,0:T(8,128)(2,1)S(1)}, u32[]{:S(2)}, u32[]{:S(2)}) collective-permute-start(bf16[256,3584]{1,0:T(8,128)(2,1)S(1)} %constant_dynamic-slice_fusion), channel_id=1, source_target_pairs={{1,8},{3,10},{5,12},{7,14},{8,1},{10,3},{12,5},{14,7},{17,24},{19,... | collective-permute-start | bytes 5505032 | tf_op jit(solution)/shard_map/ppermute | solution.py:48
  32.4 84.7 %copy-start.5 = (bf16[448,1408]{1,0:T(8,128)(2,1)}, bf16[448,1408]{1,0:T(8,128)(2,1)S(1)}, u32[]{:S(2)}) copy-start(bf16[448,1408]{1,0:T(8,128)(2,1)S(1)} %collective-permute-done.rest_1_) | copy-start | bytes 3784708
  38.0 33.2 %collective-permute-start.3 = (bf16[448,1408]{1,0:T(8,128)(2,1)S(1)}, bf16[448,1408]{1,0:T(8,128)(2,1)S(1)}, u32[]{:S(2)}, u32[]{:S(2)}) collective-permute-start(bf16[448,1408]{1,0:T(8,128)(2,1)S(1)} %collective-permute-done.rest_1_), channel_id=1, source_target_pairs={{0,16},{2,18},{4,20},{6,22},{9,25},{11,27},{13,29},{15,31},{16,0},... | collective-permute-start | bytes 3784712 | tf_op jit(solution)/shard_map/ppermute | solution.py:48
  43.1 28.1 %collective-permute-start.4 = (bf16[448,1408]{1,0:T(8,128)(2,1)S(1)}, bf16[448,1408]{1,0:T(8,128)(2,1)S(1)}, u32[]{:S(2)}, u32[]{:S(2)}) collective-permute-start(bf16[448,1408]{1,0:T(8,128)(2,1)S(1)} %collective-permute-done.rest_1_), channel_id=1, source_target_pairs={{0,4},{2,6},{4,0},{6,2},{9,13},{11,15},{13,9},{15,11},{16,20},{18,... | collective-permute-start | bytes 3784712 | tf_op jit(solution)/shard_map/ppermute | solution.py:48
  46.5 29.2 %collective-permute-start.5 = (bf16[448,1408]{1,0:T(8,128)(2,1)}, bf16[448,1408]{1,0:T(8,128)(2,1)}, u32[]{:S(2)}, u32[]{:S(2)}) collective-permute-start(bf16[448,1408]{1,0:T(8,128)(2,1)} %collective-permute-done.1.rest_2_), channel_id=1, source_target_pairs={{0,4},{2,6},{4,0},{6,2},{9,13},{11,15},{13,9},{15,11},{16,20},{18,... | collective-permute-start | bytes 3784712 | tf_op jit(solution)/shard_map/ppermute | solution.py:48
  48.9 33.6 %collective-permute-start.12 = (bf16[448,1408]{1,0:T(8,128)(2,1)S(1)}, bf16[448,1408]{1,0:T(8,128)(2,1)S(1)}, u32[]{:S(2)}, u32[]{:S(2)}) collective-permute-start(bf16[448,1408]{1,0:T(8,128)(2,1)S(1)} %bitcast_dynamic-update-slice_fusion.rest_0_), channel_id=1, source_target_pairs={{0,1},{2,3},{4,5},{6,7},{9,8},{11,10},{13,12},{15,14},{16,17},{18,... | collective-permute-start | bytes 3784712 | tf_op jit(solution)/shard_map/ppermute | solution.py:48
  50.3 53.6 %copy-start.18 = (bf16[256,3584]{1,0:T(8,128)(2,1)}, bf16[256,3584]{1,0:T(8,128)(2,1)S(1)}, u32[]{:S(2)}) copy-start(bf16[256,3584]{1,0:T(8,128)(2,1)S(1)} %collective-permute-done.6.first) | copy-start | bytes 5505028
  50.3 33.6 %collective-permute-start.13 = (bf16[448,1408]{1,0:T(8,128)(2,1)S(1)}, bf16[448,1408]{1,0:T(8,128)(2,1)S(1)}, u32[]{:S(2)}, u32[]{:S(2)}) collective-permute-start(bf16[448,1408]{1,0:T(8,128)(2,1)S(1)} %collective-permute-done.rest_1_), channel_id=1, source_target_pairs={{0,1},{2,3},{4,5},{6,7},{9,8},{11,10},{13,12},{15,14},{16,17},{18,... | collective-permute-start | bytes 3784712 | tf_op jit(solution)/shard_map/ppermute | solution.py:48
  71.2 21.2 %copy-start.6 = (bf16[448,1408]{1,0:T(8,128)(2,1)}, bf16[448,1408]{1,0:T(8,128)(2,1)S(1)}, u32[]{:S(2)}) copy-start(bf16[448,1408]{1,0:T(8,128)(2,1)S(1)} %collective-permute-done.3.rest_4_) | copy-start | bytes 3784708
  71.2 29.7 %copy-start.7 = (bf16[448,1408]{1,0:T(8,128)(2,1)}, bf16[448,1408]{1,0:T(8,128)(2,1)S(1)}, u32[]{:S(2)}) copy-start(bf16[448,1408]{1,0:T(8,128)(2,1)S(1)} %collective-permute-done.4.rest_5_) | copy-start | bytes 3784708
  75.7 15.9 %collective-permute-start.10 = (bf16[448,896]{1,0:T(8,128)(2,1)S(1)}, bf16[448,896]{1,0:T(8,128)(2,1)}, u32[]{:S(2)}, u32[]{:S(2)}) collective-permute-start(bf16[448,896]{1,0:T(8,128)(2,1)S(1)} %bitcast.50), channel_id=1, source_target_pairs={{0,8},{1,9},{2,10},{3,11},{4,12},{5,13},{6,14},{7,15},{8,0},{9,1},... | collective-permute-start | bytes 2408456 | tf_op jit(solution)/shard_map/ppermute | solution.py:48
  75.7 19.1 %collective-permute-start.9 = (bf16[448,1408]{1,0:T(8,128)(2,1)S(1)}, bf16[448,1408]{1,0:T(8,128)(2,1)}, u32[]{:S(2)}, u32[]{:S(2)}) collective-permute-start(bf16[448,1408]{1,0:T(8,128)(2,1)S(1)} %collective-permute-done.3.rest_4_), channel_id=1, source_target_pairs={{0,4},{2,6},{4,0},{6,2},{9,13},{11,15},{13,9},{15,11},{16,20},{18,... | collective-permute-start | bytes 3784712 | tf_op jit(solution)/shard_map/ppermute | solution.py:48
  79.1 1.2 collective-permute-start.8
  80.4 15.8 %collective-permute-start.14 = (bf16[448,1408]{1,0:T(8,128)(2,1)}, bf16[448,1408]{1,0:T(8,128)(2,1)S(1)}, u32[]{:S(2)}, u32[]{:S(2)}) collective-permute-start(bf16[448,1408]{1,0:T(8,128)(2,1)} %collective-permute-done.1.rest_2_), channel_id=1, source_target_pairs={{0,1},{2,3},{4,5},{6,7},{9,8},{11,10},{13,12},{15,14},{16,17},{18,... | collective-permute-start | bytes 3784712 | tf_op jit(solution)/shard_map/ppermute | solution.py:48
  82.5 16.0 %collective-permute-start.15 = (bf16[448,1408]{1,0:T(8,128)(2,1)}, bf16[448,1408]{1,0:T(8,128)(2,1)S(1)}, u32[]{:S(2)}, u32[]{:S(2)}) collective-permute-start(bf16[448,1408]{1,0:T(8,128)(2,1)} %collective-permute-done.2.rest_3_), channel_id=1, source_target_pairs={{0,1},{2,3},{4,5},{6,7},{9,8},{11,10},{13,12},{15,14},{16,17},{18,... | collective-permute-start | bytes 3784712 | tf_op jit(solution)/shard_map/ppermute | solution.py:48
  83.9 20.0 %copy-start.9 = (bf16[448,1408]{1,0:T(8,128)(2,1)}, bf16[448,1408]{1,0:T(8,128)(2,1)S(1)}, u32[]{:S(2)}) copy-start(bf16[448,1408]{1,0:T(8,128)(2,1)S(1)} %collective-permute-done.13.rest_9_) | copy-start | bytes 3784708
  83.9 8.5 %collective-permute-start.11 = (bf16[448,896]{1,0:T(8,128)(2,1)S(1)}, bf16[448,896]{1,0:T(8,128)(2,1)}, u32[]{:S(2)}, u32[]{:S(2)}) collective-permute-start(bf16[448,896]{1,0:T(8,128)(2,1)S(1)} %bitcast.51), channel_id=1, source_target_pairs={{8,16},{9,17},{10,18},{11,19},{12,20},{13,21},{14,22},{15,23},{16,... | collective-permute-start | bytes 2408456 | tf_op jit(solution)/shard_map/ppermute | solution.py:48
  91.6 12.3 %collective-permute-start.7 = (bf16[256,3584]{1,0:T(8,128)(2,1)S(1)}, bf16[256,3584]{1,0:T(8,128)(2,1)S(1)}, u32[]{:S(2)}, u32[]{:S(2)}) collective-permute-start(bf16[256,3584]{1,0:T(8,128)(2,1)S(1)} %collective-permute-done.6.first), channel_id=1, source_target_pairs={{1,3},{3,1},{5,7},{7,5},{8,10},{10,8},{12,14},{14,12},{17,19},{19,... | collective-permute-start | bytes 5505032 | tf_op jit(solution)/shard_map/ppermute | solution.py:48
  92.4 8.5 %collective-permute-start.16 = (bf16[448,1408]{1,0:T(8,128)(2,1)S(1)}, bf16[448,1408]{1,0:T(8,128)(2,1)S(1)}, u32[]{:S(2)}, u32[]{:S(2)}) collective-permute-start(bf16[448,1408]{1,0:T(8,128)(2,1)S(1)} %collective-permute-done.3.rest_4_), channel_id=1, source_target_pairs={{0,1},{2,3},{4,5},{6,7},{9,8},{11,10},{13,12},{15,14},{16,17},{18,... | collective-permute-start | bytes 3784712 | tf_op jit(solution)/shard_map/ppermute | solution.py:48
  94.8 7.6 %collective-permute-start.17 = (bf16[448,1408]{1,0:T(8,128)(2,1)S(1)}, bf16[448,1408]{1,0:T(8,128)(2,1)S(1)}, u32[]{:S(2)}, u32[]{:S(2)}) collective-permute-start(bf16[448,1408]{1,0:T(8,128)(2,1)S(1)} %collective-permute-done.4.rest_5_), channel_id=1, source_target_pairs={{0,1},{2,3},{4,5},{6,7},{9,8},{11,10},{13,12},{15,14},{16,17},{18,... | collective-permute-start | bytes 3784712 | tf_op jit(solution)/shard_map/ppermute | solution.py:48
  96.1 21.0 %collective-permute-start.18 = (bf16[448,1408]{1,0:T(8,128)(2,1)}, bf16[448,1408]{1,0:T(8,128)(2,1)}, u32[]{:S(2)}, u32[]{:S(2)}) collective-permute-start(bf16[448,1408]{1,0:T(8,128)(2,1)} %collective-permute-done.5.rest_6_), channel_id=1, source_target_pairs={{0,1},{2,3},{4,5},{6,7},{9,8},{11,10},{13,12},{15,14},{16,17},{18,... | collective-permute-start | bytes 3784712 | tf_op jit(solution)/shard_map/ppermute | solution.py:48
  98.6 18.6 %collective-permute-start.19 = (bf16[448,1408]{1,0:T(8,128)(2,1)}, bf16[448,1408]{1,0:T(8,128)(2,1)}, u32[]{:S(2)}, u32[]{:S(2)}) collective-permute-start(bf16[448,1408]{1,0:T(8,128)(2,1)} %collective-permute-done.9.rest_7_), channel_id=1, source_target_pairs={{0,1},{2,3},{4,5},{6,7},{9,8},{11,10},{13,12},{15,14},{16,17},{18,... | collective-permute-start | bytes 3784712 | tf_op jit(solution)/shard_map/ppermute | solution.py:48
  100.9 25.4 %collective-permute-start.26 = (bf16[448,896]{1,0:T(8,128)(2,1)S(1)}, bf16[448,896]{1,0:T(8,128)(2,1)}, u32[]{:S(2)}, u32[]{:S(2)}) collective-permute-start(bf16[448,896]{1,0:T(8,128)(2,1)S(1)} %bitcast.52), channel_id=1, source_target_pairs={{0,4},{1,5},{2,6},{3,7},{4,0},{5,1},{6,2},{7,3},{8,12},{9,13},{10,... | collective-permute-start | bytes 2408456 | tf_op jit(solution)/shard_map/ppermute | solution.py:48
  102.4 23.9 %collective-permute-start.24 = (bf16[448,896]{1,0:T(8,128)(2,1)}, bf16[448,896]{1,0:T(8,128)(2,1)}, u32[]{:S(2)}, u32[]{:S(2)}) collective-permute-start(bf16[448,896]{1,0:T(8,128)(2,1)} %collective-permute-done.10.rest_1_), channel_id=1, source_target_pairs={{8,16},{9,17},{10,18},{11,19},{12,20},{13,21},{14,22},{15,23},{16,... | collective-permute-start | bytes 2408456 | tf_op jit(solution)/shard_map/ppermute | solution.py:48
  105.2 33.3 %collective-permute-start.25 = (bf16[448,896]{1,0:T(8,128)(2,1)}, bf16[448,896]{1,0:T(8,128)(2,1)}, u32[]{:S(2)}, u32[]{:S(2)}) collective-permute-start(bf16[448,896]{1,0:T(8,128)(2,1)} %collective-permute-done.11), channel_id=1, source_target_pairs={{8,0},{9,1},{10,2},{11,3},{12,4},{13,5},{14,6},{15,7},{16,24},{17,... | collective-permute-start | bytes 2408456 | tf_op jit(solution)/shard_map/ppermute | solution.py:48
  123.6 16.4 %collective-permute-start.20 = (bf16[576,256]{1,0:T(8,128)(2,1)}, bf16[576,256]{1,0:T(8,128)(2,1)S(1)}, u32[]{:S(2)}, u32[]{:S(2)}) collective-permute-start(bf16[576,256]{1,0:T(8,128)(2,1)} %project.3), channel_id=1, source_target_pairs={{0,4},{1,5},{2,6},{3,7},{4,0},{5,1},{6,2},{7,3},{8,12},{9,13},{10,... | collective-permute-start | bytes 884744 | tf_op jit(solution)/shard_map/ppermute | solution.py:48
  124.8 65.2 %collective-permute-start.28 = (bf16[448,896]{1,0:T(8,128)(2,1)}, bf16[448,896]{1,0:T(8,128)(2,1)S(1)}, u32[]{:S(2)}, u32[]{:S(2)}) collective-permute-start(bf16[448,896]{1,0:T(8,128)(2,1)} %collective-permute-done.10.rest_1_), channel_id=1, source_target_pairs={{0,4},{1,5},{2,6},{3,7},{4,0},{5,1},{6,2},{7,3},{8,12},{9,13},{10,... | collective-permute-start | bytes 2408456 | tf_op jit(solution)/shard_map/ppermute | solution.py:48
  138.5 27.4 %collective-permute-start.27 = (bf16[448,896]{1,0:T(8,128)(2,1)}, bf16[448,896]{1,0:T(8,128)(2,1)S(1)}, u32[]{:S(2)}, u32[]{:S(2)}) collective-permute-start(bf16[448,896]{1,0:T(8,128)(2,1)} %collective-permute-done.24), channel_id=1, source_target_pairs={{8,0},{9,1},{10,2},{11,3},{12,4},{13,5},{14,6},{15,7},{16,24},{17,... | collective-permute-start | bytes 2408456 | tf_op jit(solution)/shard_map/ppermute | solution.py:48
  141.0 14.5 %collective-permute-start.21 = (bf16[1152,256]{1,0:T(8,128)(2,1)S(1)}, bf16[1152,256]{1,0:T(8,128)(2,1)S(1)}, u32[]{:S(2)}, u32[]{:S(2)}) collective-permute-start(bf16[1152,256]{1,0:T(8,128)(2,1)S(1)} %pad_maximum_fusion.1.pair), channel_id=1, source_target_pairs={{0,1},{1,0},{2,3},{3,2},{4,5},{5,4},{6,7},{7,6},{8,9},{9,8},{10,11... | collective-permute-start | bytes 1769480 | tf_op jit(solution)/shard_map/ppermute | solution.py:48
  143.3 46.7 %collective-permute-start.30 = (bf16[448,896]{1,0:T(8,128)(2,1)S(1)}, bf16[448,896]{1,0:T(8,128)(2,1)S(1)}, u32[]{:S(2)}, u32[]{:S(2)}) collective-permute-start(bf16[448,896]{1,0:T(8,128)(2,1)S(1)} %broadcast_select_fusion.rest_4_), channel_id=1, source_target_pairs={{0,4},{1,5},{2,6},{3,7},{4,0},{5,1},{6,2},{7,3},{8,12},{9,13},{10,... | collective-permute-start | bytes 2408456 | tf_op jit(solution)/shard_map/ppermute | solution.py:48
  155.6 16.9 %collective-permute-start.22 = (bf16[256,256]{1,0:T(8,128)(2,1)S(1)}, bf16[256,256]{1,0:T(8,128)(2,1)S(1)}, u32[]{:S(2)}, u32[]{:S(2)}) collective-permute-start(bf16[256,256]{1,0:T(8,128)(2,1)S(1)} %pad_maximum_fusion.2), channel_id=1, source_target_pairs={{0,16},{1,17},{2,18},{3,19},{4,20},{5,21},{6,22},{7,23},{8,24},{9,... | collective-permute-start | bytes 393224 | tf_op jit(solution)/shard_map/ppermute | solution.py:48
  166.1 24.0 %collective-permute-start.29 = (bf16[448,896]{1,0:T(8,128)(2,1)S(1)}, bf16[448,896]{1,0:T(8,128)(2,1)S(1)}, u32[]{:S(2)}, u32[]{:S(2)}) collective-permute-start(bf16[448,896]{1,0:T(8,128)(2,1)S(1)} %broadcast_select_fusion.1.rest_3_), channel_id=1, source_target_pairs={{0,4},{1,5},{2,6},{3,7},{4,0},{5,1},{6,2},{7,3},{8,12},{9,13},{10,... | collective-permute-start | bytes 2408456 | tf_op jit(solution)/shard_map/ppermute | solution.py:48
  180.6 8.5 %collective-permute-start.33 = (bf16[256,896]{1,0:T(8,128)(2,1)}, bf16[256,896]{1,0:T(8,128)(2,1)S(1)}, u32[]{:S(2)}, u32[]{:S(2)}) collective-permute-start(bf16[256,896]{1,0:T(8,128)(2,1)} %attend.3), channel_id=1, source_target_pairs={{1,8},{3,10},{5,12},{7,14},{8,1},{10,3},{12,5},{14,7},{17,24},{19,... | collective-permute-start | bytes 1376264 | tf_op jit(solution)/shard_map/ppermute | solution.py:48
  188.2 18.9 %collective-permute-start.23 = (bf16[256,896]{1,0:T(8,128)(2,1)}, bf16[256,896]{1,0:T(8,128)(2,1)S(1)}, u32[]{:S(2)}, u32[]{:S(2)}) collective-permute-start(bf16[256,896]{1,0:T(8,128)(2,1)} %attend.2), channel_id=1, source_target_pairs={{1,8},{3,10},{5,12},{7,14},{8,1},{10,3},{12,5},{14,7},{17,24},{19,... | collective-permute-start | bytes 1376264 | tf_op jit(solution)/shard_map/ppermute | solution.py:48
  200.9 16.1 %collective-permute-start.34 = (bf16[2,256,896]{2,1,0:T(8,128)(2,1)S(1)}, bf16[2,256,896]{2,1,0:T(8,128)(2,1)S(1)}, u32[]{:S(2)}, u32[]{:S(2)}) collective-permute-start(bf16[2,256,896]{2,1,0:T(8,128)(2,1)S(1)} %slice_bitcast_fusion.1), channel_id=1, source_target_pairs={{0,1},{1,0},{2,3},{3,2},{4,5},{5,4},{6,7},{7,6},{8,9},{9,8},{10,11... | collective-permute-start | bytes 2752520 | tf_op jit(solution)/shard_map/ppermute | solution.py:48
  217.0 2.5 %collective-permute-start.31 = (bf16[2,256,896]{2,1,0:T(8,128)(2,1)S(1)}, bf16[2,256,896]{2,1,0:T(8,128)(2,1)S(1)}, u32[]{:S(2)}, u32[]{:S(2)}) collective-permute-start(bf16[2,256,896]{2,1,0:T(8,128)(2,1)S(1)} %slice_bitcast_fusion.4), channel_id=1, source_target_pairs={{0,1},{1,0},{2,3},{3,2},{4,5},{5,4},{6,7},{7,6},{8,9},{9,8},{10,11... | collective-permute-start | bytes 2752520 | tf_op jit(solution)/shard_map/ppermute | solution.py:48
  217.6 13.4 %collective-permute-start.35 = (bf16[256,896]{1,0:T(8,128)(2,1)S(1)}, bf16[256,896]{1,0:T(8,128)(2,1)S(1)}, u32[]{:S(2)}, u32[]{:S(2)}) collective-permute-start(bf16[256,896]{1,0:T(8,128)(2,1)S(1)} %fusion.5), channel_id=1, source_target_pairs={{0,2},{1,3},{2,0},{3,1},{4,6},{5,7},{6,4},{7,5},{8,10},{9,11},{10,... | collective-permute-start | bytes 1376264 | tf_op jit(solution)/shard_map/ppermute | solution.py:48
  219.8 20.4 %collective-permute-start.32 = (bf16[256,896]{1,0:T(8,128)(2,1)S(1)}, bf16[256,896]{1,0:T(8,128)(2,1)S(1)}, u32[]{:S(2)}, u32[]{:S(2)}) collective-permute-start(bf16[256,896]{1,0:T(8,128)(2,1)S(1)} %fusion.4), channel_id=1, source_target_pairs={{0,2},{1,3},{2,0},{3,1},{4,6},{5,7},{6,4},{7,5},{8,10},{9,11},{10,... | collective-permute-start | bytes 1376264 | tf_op jit(solution)/shard_map/ppermute | solution.py:48
  (19 other events, 136.6 us)

commit v4 on v3

v4 whole, which is shorter than its diff:
```python
import functools
import math

import jax
import jax.numpy as jnp
from jax import lax
from jax.experimental import pallas as pl
from jax.experimental.pallas import tpu as pltpu
from jax.sharding import PartitionSpec as P

QH = 28
KVH = 4
HEAD_DIM = 128
SPLIT = 4
R_MIN = 8
AXES = ("seq", "head")
VMEM_LIMIT = 56 * 1024 * 1024


def params():
    return pltpu.CompilerParams(vmem_limit_bytes=VMEM_LIMIT)


def vmem():
    return pl.BlockSpec(memory_space=pltpu.VMEM)


def smem():
    return pl.BlockSpec(memory_space=pltpu.SMEM)


def hbm():
    return pl.BlockSpec(memory_space=pl.ANY)


def moves(n_seq, rule):
    pairs = []
    for s in range(n_seq):
        for h in range(KVH):
            target = rule(s >> 2, (s >> 1) & 1, s & 1, h >> 1, h & 1)
            if target is not None:
                big, l, x, y, c = target
                pairs.append((s * KVH + h, (4 * big + 2 * l + x) * KVH + 2 * y + c))
    return pairs


def send(value, n_seq, rule):
    return lax.ppermute(value, AXES, moves(n_seq, rule))


def norm_kernel(info, hidden, first, second, gain, normed, pooled, buf, sems):
    rows = hidden.shape[0]
    half = rows // 2
    tiles = sems.shape[0]
    tile = rows // tiles
    matched, y_bit, ratio = info[0], info[1], info[2]

    def land(i):
        return buf.at[pl.ds(i * tile, tile), :]

    for i in range(tiles):

        @pl.when(matched == 1)
        def _():
            pltpu.make_async_copy(hidden.at[pl.ds(i * tile, tile), :], land(i), sems.at[i]).start()

        upper = (i * tile) // half
        local = pl.ds(i * tile - upper * half, tile)

        @pl.when((matched == 0) & (y_bit == upper))
        def _():
            pltpu.make_async_copy(first.at[local, :], land(i), sems.at[i]).start()

        @pl.when((matched == 0) & (y_bit != upper))
        def _():
            pltpu.make_async_copy(second.at[local, :], land(i), sems.at[i]).start()

    scale = gain[...]
    for i in range(tiles):
        pltpu.make_async_copy(hidden.at[pl.ds(i * tile, tile), :], land(i), sems.at[i]).wait()
        floats = buf[i * tile : (i + 1) * tile, :].astype(jnp.float32)
        mean = jnp.mean(floats * floats, axis=1, keepdims=True)
        normed[i * tile : (i + 1) * tile, :] = (floats * lax.rsqrt(mean + 1e-06) * scale).astype(
            jnp.bfloat16
        )
    slots = pooled.shape[0]
    token = lax.broadcasted_iota(jnp.int32, (slots, rows), 1)
    slot = lax.broadcasted_iota(jnp.int32, (slots, rows), 0)
    member = (
        (token >= slot * ratio) & (token < (slot + 1) * ratio) & (slot < info[3])
    ).astype(jnp.float32).astype(jnp.bfloat16)
    total = jnp.dot(member, normed[...], preferred_element_type=jnp.float32)
    pooled[...] = (total / ratio.astype(jnp.float32)).astype(jnp.bfloat16)


def norm_and_pool(info, hidden, first, second, gain):
    rows, width = hidden.shape
    tiles = 8
    return pl.pallas_call(
        norm_kernel,
        out_shape=(
            jax.ShapeDtypeStruct((rows, width), jnp.bfloat16),
            jax.ShapeDtypeStruct((rows // R_MIN, width), jnp.bfloat16),
        ),
        in_specs=[smem(), hbm(), hbm(), hbm(), vmem()],
        out_specs=(vmem(), vmem()),
        scratch_shapes=[pltpu.VMEM((rows, width), jnp.bfloat16), pltpu.SemaphoreType.DMA((tiles,))],
        compiler_params=params(),
        cost_estimate=pl.CostEstimate(
            flops=2 * rows * rows // R_MIN * width, bytes_accessed=4 * rows * width, transcendentals=0
        ),
        name="norm_pool",
    )(info, hidden, first, second, gain)


def block_of(info, key):
    return 4 * (info[4] ^ key[0]) + 2 * (info[5] ^ key[1]) + (info[6] ^ key[2])


def chunk_blocks(rows):
    blocks = 2
    while blocks * rows % 128:
        blocks *= 2
    return blocks


def load_chunks(info, keys, refs, weights, sems, normed, left, left_sems, first_col):
    count = len(keys)
    rows, cols = refs[0].shape[0], weights.shape[2]
    blocks = chunk_blocks(rows)
    chunks = count // blocks
    flips = [4 * key[0] + 2 * key[1] + key[2] for key in keys]

    def chunk_of(k):
        return block_of(info, (0, 0, 0)) // blocks ^ k

    def members(k):
        return [i for i in range(count) if flips[i] // blocks == k]

    def piece(ref, i, k):
        spot = block_of(info, keys[i]) % blocks * rows
        return pltpu.make_async_copy(
            ref.at[:, pl.ds(first_col, cols)],
            weights.at[k, pl.ds(pl.multiple_of(spot, 16), rows), :],
            sems.at[i],
        )

    def columns(k):
        start = pl.multiple_of(chunk_of(k) * (blocks * rows), 128)
        return pltpu.make_async_copy(
            normed.at[:, pl.ds(start, blocks * rows)], left.at[k], left_sems.at[k]
        )

    for k in range(chunks):
        columns(k).start()
        for i in members(k):
            pl.when(info[0] == 1)(piece(refs[i], i, k).start)
            pl.when(info[0] == 0)(piece(refs[count + i], i, k).start)

    def wait(k):
        columns(k).wait()
        for i in members(k):
            piece(refs[i], i, k).wait()

    return chunks, wait, chunk_of


def query_kernel(first_col, keys, info, normed, bias, *rest):
    refs, (out, weights, sems, left, left_sems, total) = rest[:-6], rest[-6:]
    chunks, wait, _ = load_chunks(
        info, keys, refs, weights, sems, normed, left, left_sems, first_col
    )
    for k in range(chunks):
        wait(k)
        product = jnp.dot(left[k], weights[k], preferred_element_type=jnp.float32)
        if k == 0:
            total[...] = product + bias[...]
        elif k < chunks - 1:
            total[...] += product
        else:
            out[...] = (total[...] + product).astype(jnp.bfloat16)


def keyval_kernel(first_col, keys, info, normed, pooled, bias, *rest):
    refs, (out, weights, sems, left, left_sems, total) = rest[:-6], rest[-6:]
    chunks, wait, chunk_of = load_chunks(
        info, keys, refs, weights, sems, normed, left, left_sems, first_col
    )
    tokens, depth = normed.shape[0], weights.shape[1]
    cols = out.shape[1]
    for k in range(chunks):
        wait(k)
        slots = pooled[:, pl.ds(pl.multiple_of(chunk_of(k) * depth, 128), depth)]
        product = jnp.dot(left[k], weights[k, :, :cols], preferred_element_type=jnp.float32)
        beacon = jnp.dot(slots, weights[k, :, cols:], preferred_element_type=jnp.float32)
        if k == 0:
            total[:tokens, :] = product + bias[:, :cols]
            total[tokens:, :] = beacon + bias[:, cols:]
        elif k < chunks - 1:
            total[:tokens, :] += product
            total[tokens:, :] += beacon
        else:
            out[:tokens, :] = (total[:tokens, :] + product).astype(jnp.bfloat16)
            out[tokens:, :] = (total[tokens:, :] + beacon).astype(jnp.bfloat16)


def project(kernel, out_rows, out_cols, info, left, bias, own, copied):
    keys = tuple(own)
    rows = own[keys[0]].shape[0]
    blocks = chunk_blocks(rows)
    tokens, width = left[0].shape
    cols = bias.shape[0]
    chunks = len(keys) // blocks
    return pl.pallas_call(
        functools.partial(kernel, keys),
        out_shape=jax.ShapeDtypeStruct((out_rows, out_cols), jnp.bfloat16),
        in_specs=[smem(), hbm()] + [vmem()] * len(left) + [hbm()] * (2 * len(keys)),
        out_specs=vmem(),
        scratch_shapes=[
            pltpu.VMEM((chunks, blocks * rows, cols), jnp.bfloat16),
            pltpu.SemaphoreType.DMA((len(keys),)),
            pltpu.VMEM((chunks, tokens, blocks * rows), jnp.bfloat16),
            pltpu.SemaphoreType.DMA((chunks,)),
            pltpu.VMEM((out_rows, out_cols), jnp.float32),
        ],
        compiler_params=params(),
        cost_estimate=pl.CostEstimate(
            flops=2 * out_rows * out_cols * width,
            bytes_accessed=2 * width * (out_rows + cols),
            transcendentals=0,
        ),
        name="project",
    )(info, *left, bias.reshape(1, -1), *[own[k] for k in keys], *[copied[k] for k in keys])


def attend_kernel(tokens, slots, beacons, first_row, info, ratios, queries, *rest):
    pair, beside, across, corner = rest[:4]
    beacon_refs, out = rest[4 : 4 + beacons], rest[4 + beacons]
    place = 2 * info[7] + info[6]
    big = info[4]
    scale = 1.0 / math.sqrt(HEAD_DIM)
    tile = min(256, tokens)

    def pieces(variant):
        full = []
        if variant in (1, 3):
            full.append(beside)
        if variant in (2, 3):
            full += [across, corner]
        return full

    def score(rows, keys):
        return lax.dot_general(
            rows, keys, (((1,), (1,)), ((), ())), preferred_element_type=jnp.float32
        ) * scale

    def run(variant):
        for local_start in range(0, out.shape[0], tile):
            start = first_row + local_start
            rows = queries[start : start + tile, :]
            parts = []
            seen = start + tile
            scores = score(rows, pair[:seen, :HEAD_DIM])
            q_pos = start + lax.broadcasted_iota(jnp.int32, (tile, seen), 0)
            k_pos = lax.broadcasted_iota(jnp.int32, (tile, seen), 1)
            parts.append((jnp.where(k_pos <= q_pos, scores, -1e30), pair[:seen, HEAD_DIM:]))
            for ref in pieces(variant):
                parts.append((score(rows, ref[:tokens, :HEAD_DIM]), ref[:tokens, HEAD_DIM:]))
            for m in range(beacons):
                source = big ^ (m + 1)
                count = beacon_refs[m].shape[0]
                live = jnp.where(source < big, tokens // ratios[source], 0)
                local = lax.broadcasted_iota(jnp.int32, (tile, count), 1) % slots
                scores = score(rows, beacon_refs[m][:, :HEAD_DIM])
                parts.append((jnp.where(local < live, scores, -1e30), beacon_refs[m][:, HEAD_DIM:]))
            top = functools.reduce(
                jnp.maximum, [jnp.max(s, axis=1, keepdims=True) for s, _ in parts]
            )
            total = jnp.zeros((tile, 1), jnp.float32)
            mixed = jnp.zeros((tile, HEAD_DIM), jnp.float32)
            for scores, values in parts:
                weights = jnp.exp(scores - top)
                total += jnp.sum(weights, axis=1, keepdims=True)
                mixed += jnp.dot(
                    weights.astype(jnp.bfloat16), values, preferred_element_type=jnp.float32
                )
            out[local_start : local_start + tile, :] = (mixed / total).astype(jnp.bfloat16)

    for variant in range(SPLIT):
        pl.when(place == variant)(functools.partial(run, variant))


def attend(first_row, row_count, info, ratios, queries, keyvals, beacons):
    tokens, cols = queries.shape
    slots = keyvals[0].shape[0] - tokens
    heads = cols // HEAD_DIM
    keys = 4 * tokens + sum(b.shape[0] for b in beacons)
    return pl.pallas_call(
        functools.partial(attend_kernel, tokens, slots, len(beacons), first_row),
        grid=(heads,),
        out_shape=jax.ShapeDtypeStruct((row_count, cols), jnp.bfloat16),
        in_specs=[smem(), smem(), pl.BlockSpec((tokens, HEAD_DIM), lambda i: (0, i))]
        + [vmem()] * (len(keyvals) + len(beacons)),
        out_specs=pl.BlockSpec((row_count, HEAD_DIM), lambda i: (0, i)),
        compiler_params=params(),
        cost_estimate=pl.CostEstimate(
            flops=4 * row_count * keys * cols,
            bytes_accessed=4 * tokens * cols,
            transcendentals=row_count * keys * heads,
        ),
        name="attend",
    )(info, ratios, queries, *keyvals, *beacons)


def out_kernel(keys, info, attention, *rest):
    refs, (away, kept, weights, sems) = rest[:-4], rest[-4:]
    rows = refs[0].shape[0]
    width = kept.shape[2]
    per_group = width // rows

    for i, key in enumerate(keys):
        block = block_of(info, key)
        group = (block // per_group) ^ (2 * info[1] + info[7])
        spot = pl.multiple_of((block % per_group) * rows, 16)
        pltpu.make_async_copy(
            refs[i], weights.at[group, pl.ds(spot, rows), :], sems.at[group]
        ).start()
    for out, j, group in ((away, 1, 3), (away, 0, 1), (kept, 1, 2), (kept, 0, 0)):
        pltpu.make_async_copy(weights.at[group], weights.at[group], sems.at[group]).wait()
        out[j] = lax.dot_general(
            attention[...],
            weights[group],
            (((1,), (1,)), ((), ())),
            preferred_element_type=jnp.float32,
        ).astype(jnp.bfloat16)


def out_project(info, attention, pieces):
    tokens, depth = attention.shape
    keys = tuple(pieces)
    width = len(keys) * pieces[keys[0]].shape[0] // KVH
    shape = jax.ShapeDtypeStruct((2, tokens, width), jnp.bfloat16)
    return pl.pallas_call(
        functools.partial(out_kernel, keys),
        out_shape=(shape, shape),
        in_specs=[smem(), vmem()] + [hbm()] * len(keys),
        out_specs=(vmem(), vmem()),
        scratch_shapes=[
            pltpu.VMEM((KVH, width, depth), jnp.bfloat16),
            pltpu.SemaphoreType.DMA((KVH,)),
        ],
        compiler_params=params(),
        cost_estimate=pl.CostEstimate(
            flops=8 * tokens * width * depth, bytes_accessed=8 * width * depth, transcendentals=0
        ),
        name="out_project",
    )(info, attention, *[pieces[k] for k in keys])


def together(*values):
    return lax.optimization_barrier(values)


def on_device(
    hidden,
    norm_gain,
    query_weight,
    query_bias,
    keyval_weight,
    keyval_bias,
    beacon_weight,
    beacon_bias,
    out_weight,
    ratios,
):
    n_seq = lax.axis_size("seq")
    rows_dev = hidden.shape[0]
    half = rows_dev // 2
    seq_index = lax.axis_index("seq")
    head_index = lax.axis_index("head")
    big, l, x = seq_index // 4, (seq_index // 2) % 2, seq_index % 2
    y, c = head_index // 2, head_index % 2
    matched = c == l
    segment_ids = jnp.arange(ratios.shape[0], dtype=jnp.int32)
    own_ratio = jnp.sum(jnp.where(segment_ids == big, ratios, 0))
    inner = big != l
    info = jnp.stack(
        [
            matched.astype(jnp.int32),
            y,
            own_ratio,
            rows_dev // own_ratio,
            big,
            l,
            x,
            c,
        ]
    ).astype(jnp.int32)

    kv_cols = 2 * keyval_weight.shape[2]
    depth = keyval_weight.shape[0]
    query_cols = query_weight.shape[1]
    biases = jnp.concatenate([query_bias, keyval_bias.reshape(-1), beacon_bias.reshape(-1)])
    shard = jnp.concatenate(
        [
            query_weight,
            keyval_weight.reshape(depth, kv_cols),
            beacon_weight.reshape(depth, kv_cols),
        ],
        axis=1,
    )
    out_shard = out_weight.T

    def to_other_l(value):
        return send(value, n_seq, lambda big, l, x, y, c: (big, 1 - l, x, y, c) if c != l else None)

    def to_other_big(value, bit):
        return send(value, n_seq, lambda big, l, x, y, c: (big ^ bit, l, x, y, c) if c == l else None)

    def to_other_x(value):
        return send(value, n_seq, lambda big, l, x, y, c: (big, l, 1 - x, y, c) if c == l else None)

    def to_other_core(value):
        return send(value, n_seq, lambda big, l, x, y, c: (big, l, x, y, 1 - c) if c == l else None)

    def swap_l(value):
        return send(value, n_seq, lambda big, l, x, y, c: (big, 1 - l, x, y, c))

    def swap_big(value, bit):
        return send(value, n_seq, lambda big, l, x, y, c: (big ^ bit, l, x, y, c))

    def swap_inner(value):
        return send(
            value, n_seq, lambda big, l, x, y, c: (1 - big, 1 - l, x, y, c) if big != l else None
        )

    def to_outer(value):
        return send(value, n_seq, lambda big, l, x, y, c: (big, 1 - l, x, y, c) if big != l else None)

    def swap_x(value):
        return send(value, n_seq, lambda big, l, x, y, c: (big, l, 1 - x, y, c))

    own, copied = {(0, 0, 0): shard}, {}
    own_half = lax.dynamic_slice_in_dim(hidden, y * half, half, 0)
    first = send(
        own_half, n_seq, lambda big, l, x, y, c: (big, 1 - l, x, y, 1 - c) if c != l else None
    )
    own[0, 1, 0] = to_other_l(shard)
    own[1, 0, 0] = to_other_big(shard, 1)
    own[0, 0, 1] = to_other_x(shard)
    other_biases = send(biases, n_seq, lambda big, l, x, y, c: (big, l, x, y, 1 - c))
    biases = jnp.where(matched, biases, other_biases)
    gain = norm_gain.reshape(1, -1)
    own[0, 1, 0], own[1, 0, 0], own[0, 0, 1], biases, gain, info = together(
        own[0, 1, 0], own[1, 0, 0], own[0, 0, 1], biases, gain, info
    )
    own[1, 1, 0] = to_other_big(own[0, 1, 0], 1)
    own[0, 1, 1] = to_other_x(own[0, 1, 0])
    own[1, 0, 1] = to_other_x(own[1, 0, 0])
    keys = ((0, 0, 0), (0, 1, 0), (1, 0, 0), (0, 0, 1))
    for key in keys:
        copied[key] = to_other_core(own[key])
    (
        own[1, 1, 0],
        own[0, 1, 1],
        own[1, 0, 1],
        first,
        copied[0, 0, 0],
        copied[0, 1, 0],
        copied[1, 0, 0],
        copied[0, 0, 1],
    ) = together(
        own[1, 1, 0], own[0, 1, 1], own[1, 0, 1], first, *[copied[key] for key in keys]
    )
    own[1, 1, 1] = to_other_x(own[1, 1, 0])
    second = send(first, n_seq, lambda big, l, x, y, c: (big, l, x, 1 - y, c) if c != l else None)
    keys = ((1, 1, 0), (0, 1, 1), (1, 0, 1))
    for key in keys:
        copied[key] = to_other_core(own[key])
    copied[1, 1, 0], copied[0, 1, 1], copied[1, 0, 1], out_shard = together(
        *[copied[key] for key in keys], out_shard
    )
    outs = {(0, 0, 0): out_shard, (0, 1, 0): swap_l(out_shard)}
    two_segments = n_seq == 2 * SPLIT
    middle_own = swap_inner(out_shard) if two_segments else out_shard
    outs[0, 0, 1] = swap_x(out_shard)
    bit = 2
    while bit < n_seq // SPLIT:
        for key in list(own):
            new = (key[0] ^ bit, key[1], key[2])
            own[new] = to_other_big(own[key], bit)
            copied[new] = to_other_core(own[new])
        bit *= 2

    normed, pooled = norm_and_pool(info, hidden, first, second, gain)
    if two_segments:
        normed, middle_own, outs[0, 1, 0], outs[0, 0, 1], own[1, 1, 1] = together(
            normed, middle_own, outs[0, 1, 0], outs[0, 0, 1], own[1, 1, 1]
        )
        middle_other = swap_inner(outs[0, 1, 0])
        outer_own = to_outer(middle_own)
        outs[0, 1, 1] = swap_x(outs[0, 1, 0])
    copied[1, 1, 1] = to_other_core(own[1, 1, 1])
    slots_dev = rows_dev // R_MIN
    copied = {key: copied[key] for key in own}
    keyval = project(
        functools.partial(keyval_kernel, query_cols),
        rows_dev + slots_dev,
        kv_cols,
        info,
        [normed, pooled],
        biases[query_cols:],
        own,
        copied,
    )
    beside = send(keyval, n_seq, lambda big, l, x, y, c: (big, l, 1 - x, y, c))
    across = send(keyval, n_seq, lambda big, l, x, y, c: (big, l, x, y, 1 - c))
    normed, keyval = together(normed, keyval)
    query = project(
        functools.partial(query_kernel, 0),
        rows_dev,
        query_cols,
        info,
        [normed],
        biases[:query_cols],
        own,
        copied,
    )
    query, beside, across = together(query, beside, across)
    corner = send(beside, n_seq, lambda big, l, x, y, c: (big, l, x, y, 1 - c))
    beacons = [
        jnp.concatenate([piece[rows_dev:] for piece in (keyval, beside, across, corner)], axis=0)
    ]
    bit = 1
    while bit < n_seq // SPLIT:
        beacons += [swap_big(piece, bit) for piece in beacons]
        bit *= 2
    beacons = beacons[1:]
    if two_segments:
        query, middle_other, outer_own, outs[0, 1, 1] = together(
            query, middle_other, outer_own, outs[0, 1, 1]
        )
        outer_other = to_outer(middle_other)
        outs[1, 0, 0] = jnp.where(inner, middle_other, outer_own)
        outs[1, 0, 1] = swap_x(outs[1, 0, 0])
    else:
        bit = 1
        while bit < n_seq // SPLIT:
            for key in list(outs):
                if key[2] == 0:
                    outs[key[0] ^ bit, key[1], 0] = swap_big(outs[key], bit)
            bit *= 2
        for key in list(outs):
            if (key[0], key[1], 1) not in outs:
                outs[key[0], key[1], 1] = swap_x(outs[key])

    def attend_rows(first_row, row_count):
        return attend(
            first_row, row_count, info, ratios, query, [keyval, beside, across, corner], beacons
        )

    def swap_back(value):
        return send(
            value, n_seq, lambda big, l, x, y, c: (big, 1 - l, x, y, 1 - c) if c != l else None
        )

    def swap_core(value):
        return send(value, n_seq, lambda big, l, x, y, c: (big, l, x, y, 1 - c))

    def swap_y(value):
        return send(value, n_seq, lambda big, l, x, y, c: (big, l, x, 1 - y, c))

    def add(kept, from_core):
        sums = kept.astype(jnp.float32) + from_core.astype(jnp.float32)
        return sums[0], sums[1].astype(jnp.bfloat16)

    part = rows_dev // 2
    early = attend_rows(0, part)
    if two_segments:
        early, outer_other, outs[1, 0, 1] = together(early, outer_other, outs[1, 0, 1])
        outs[1, 1, 0] = jnp.where(inner, middle_own, outer_other)
        outs[1, 1, 1] = swap_x(outs[1, 1, 0])
    early_swapped = swap_back(early)
    query, early = together(query, early)
    late = attend_rows(part, part)
    late, early, early_swapped = together(late, early, early_swapped)
    late_swapped = swap_back(late)
    early_away, early_kept = out_project(info, jnp.where(matched, early, early_swapped), outs)
    early_away, early_kept, late, late_swapped = together(
        early_away, early_kept, late, late_swapped
    )
    early_near, early_far = add(early_kept, swap_core(early_away))
    late = jnp.where(matched, late, late_swapped)
    late, early_near, early_far = together(late, early_near, early_far)
    early_from_y = swap_y(early_far)
    late_away, late_kept = out_project(info, late, outs)
    late_away, late_kept, early_from_y = together(late_away, late_kept, early_from_y)
    late_near, late_far = add(late_kept, swap_core(late_away))
    results = [(early_near, early_from_y), (late_near, swap_y(late_far))]
    return jnp.concatenate(
        [(near + from_y.astype(jnp.float32)).astype(jnp.bfloat16) for near, from_y in results], axis=0
    )


def solution(mesh):
    return jax.shard_map(
        on_device,
        mesh=mesh,
        in_specs=(
            P("seq", None),
            P(),
            P("seq", "head"),
            P("head"),
            P("seq", None, "head"),
            P(None, "head"),
            P("seq", None, "head"),
            P(None, "head"),
            P("head", "seq"),
            P(),
        ),
        out_specs=P("seq", "head"),
        check_vma=False,
    )
```

time: 243 us -> 235 us (0.967)
  starting transfers between devices: 89.9 us -> 83.2 us
  local copies, waits for them, and re-layouts: 14.7 us -> 12 us
    ppermute x36 -> x37, starting transfers between devices: 89.9 us -> 83.2 us  [send(): return lax.ppermute(value, AXES, moves(n_seq, rule))]
    squeeze x2 -> x1, local copies, waits for them, and re-layouts: 2.69 us -> 0.06 us  [add(): return (sums[0], sums[1].astype(jnp.bfloat16))]
    ppermute x36 -> x37, waiting for transfers between devices: 76.3 us -> 77.9 us  [send(): return lax.ppermute(value, AXES, moves(n_seq, rule))]
    unnamed x64 -> x70, local copies, waits for them, and re-layouts: 6.52 us -> 5.01 us
  transfers between devices with their start and end apart: 36 -> 37, of which waited for: 12 -> 14; matrix products, arithmetic and copies ran while one was open for 6% -> 4% of each run, Pallas kernels for 21% -> 22%
where the time goes in v4:
time: 235 us; the launch traced here: 233 us
  starting transfers between devices  83.2 us (35%)
  waiting for transfers between devices  77.9 us (33%)
  Pallas kernels  51.1 us (22%)
  local copies, waits for them, and re-layouts  12 us (5%)
  other arithmetic  6.43 us (3%)
  between operations  2.69 us (1%)
    ppermute x37, starting transfers between devices, send(): return lax.ppermute(value, AXES, moves(n_seq, rule))  83.2 us
    ppermute x37, waiting for transfers between devices, send(): return lax.ppermute(value, AXES, moves(n_seq, rule))  77.9 us
    pallas_call x2, Pallas kernels, out_project(): pl.pallas_call(functools.partial(out_kernel, keys), out_shape=(shape, sha...  15.8 us
    pallas_call x2, Pallas kernels, project(): pl.pallas_call(functools.partial(kernel, keys), out_shape=jax.ShapeDtypeS...  15.6 us
    pallas_call x2, Pallas kernels, attend(): pl.pallas_call(functools.partial(attend_kernel, tokens, slots, len(beacon...  14.3 us
    pallas_call x1, Pallas kernels, norm_and_pool(): pl.pallas_call(norm_kernel, out_shape=(jax.ShapeDtypeStruct((rows, width)...  5.49 us
    unnamed x70, local copies, waits for them, and re-layouts  5.01 us
  transfers between devices with their start and end apart: 37, of which 14 were waited for; matrix products, arithmetic and copies ran while one was open for 4% of the time, Pallas kernels for 22%

profile of v4, /device:TPU:0, one launch (start us, length us, event | category | flops | bytes accessed | tf_op | source)
XLA Modules:
  0.0 233.3 jit_solution(15836354952059906013)
XLA Ops:
  0.0 1.3 constant_dynamic-update-slice_fusion
  1.4 1.3 collective-permute-start
  2.7 5.9 %collective-permute-start.1 = (bf16[448,1408]{1,0:T(8,128)(2,1)S(1)}, bf16[448,1408]{1,0:T(8,128)(2,1)}, u32[]{:S(2)}, u32[]{:S(2)}) collective-permute-start(bf16[448,1408]{1,0:T(8,128)(2,1)S(1)} %bitcast_dynamic-update-slice_fusion.rest_0_), channel_id=1, source_target_pairs={{0,16},{2,18},{4,20},{6,22},{9,25},{11,27},{13,29},{15,31},{16,0},... | collective-permute-start | bytes 3784712 | tf_op jit(solution)/shard_map/ppermute | solution.py:48
  8.6 3.4 %collective-permute-start.2 = (bf16[448,1408]{1,0:T(8,128)(2,1)S(1)}, bf16[448,1408]{1,0:T(8,128)(2,1)}, u32[]{:S(2)}, u32[]{:S(2)}) collective-permute-start(bf16[448,1408]{1,0:T(8,128)(2,1)S(1)} %bitcast_dynamic-update-slice_fusion.rest_0_), channel_id=1, source_target_pairs={{0,4},{2,6},{4,0},{6,2},{9,13},{11,15},{13,9},{15,11},{16,20},{18,... | collective-permute-start | bytes 3784712 | tf_op jit(solution)/shard_map/ppermute | solution.py:48
  12.1 3.0 %constant_dynamic-slice_fusion = bf16[256,3584]{1,0:T(8,128)(2,1)} fusion(bf16[512,3584]{1,0:T(8,128)(2,1)} %hidden.1, s32[]{:T(128)S(6)} %select_n.79), kind=kLoop, calls=%fused_computation.24 | loop fusion | bytes 3670020 | tf_op jit(solution)/shard_map/dynamic_slice | solution.py:444
  15.1 1.9 collective-permute-start.7
  20.3 1.2 stack.39.info
  21.5 2.4 %collective-permute-start.8 = (bf16[448,1408]{1,0:T(8,128)(2,1)S(1)}, bf16[448,1408]{1,0:T(8,128)(2,1)S(1)}, u32[]{:S(2)}, u32[]{:S(2)}) collective-permute-start(bf16[448,1408]{1,0:T(8,128)(2,1)S(1)} %bitcast_dynamic-update-slice_fusion.rest_0_), channel_id=1, source_target_pairs={{0,1},{2,3},{4,5},{6,7},{9,8},{11,10},{13,12},{15,14},{16,17},{18,... | collective-permute-start | bytes 3784712 | tf_op jit(solution)/shard_map/ppermute | solution.py:48
  24.0 7.5 %collective-permute-done.rest_1_ = bf16[448,1408]{1,0:T(8,128)(2,1)S(1)} collective-permute-done((bf16[448,1408]{1,0:T(8,128)(2,1)S(1)}, bf16[448,1408]{1,0:T(8,128)(2,1)S(1)}, u32[]{:S(2)}, u32[]{:S(2)}) %collective-permute-start) | collective-permute-done | bytes 1261600 | tf_op jit(solution)/shard_map/ppermute | solution.py:48
  31.5 5.6 %collective-permute-done.1.rest_2_ = bf16[448,1408]{1,0:T(8,128)(2,1)} collective-permute-done((bf16[448,1408]{1,0:T(8,128)(2,1)S(1)}, bf16[448,1408]{1,0:T(8,128)(2,1)}, u32[]{:S(2)}, u32[]{:S(2)}) %collective-permute-start.1) | collective-permute-done | bytes 1261600 | tf_op jit(solution)/shard_map/ppermute | solution.py:48
  37.1 5.1 %collective-permute-start.4 = (bf16[448,1408]{1,0:T(8,128)(2,1)S(1)}, bf16[448,1408]{1,0:T(8,128)(2,1)S(1)}, u32[]{:S(2)}, u32[]{:S(2)}) collective-permute-start(bf16[448,1408]{1,0:T(8,128)(2,1)S(1)} %collective-permute-done.rest_1_), channel_id=1, source_target_pairs={{0,16},{2,18},{4,20},{6,22},{9,25},{11,27},{13,29},{15,31},{16,0},... | collective-permute-start | bytes 3784712 | tf_op jit(solution)/shard_map/ppermute | solution.py:48
  42.2 3.4 %collective-permute-start.5 = (bf16[448,1408]{1,0:T(8,128)(2,1)S(1)}, bf16[448,1408]{1,0:T(8,128)(2,1)S(1)}, u32[]{:S(2)}, u32[]{:S(2)}) collective-permute-start(bf16[448,1408]{1,0:T(8,128)(2,1)S(1)} %collective-permute-done.rest_1_), channel_id=1, source_target_pairs={{0,4},{2,6},{4,0},{6,2},{9,13},{11,15},{13,9},{15,11},{16,20},{18,... | collective-permute-start | bytes 3784712 | tf_op jit(solution)/shard_map/ppermute | solution.py:48
  45.6 1.4 collective-permute-start.9
  47.0 2.4 %collective-permute-start.6 = (bf16[448,1408]{1,0:T(8,128)(2,1)}, bf16[448,1408]{1,0:T(8,128)(2,1)S(1)}, u32[]{:S(2)}, u32[]{:S(2)}) collective-permute-start(bf16[448,1408]{1,0:T(8,128)(2,1)} %collective-permute-done.1.rest_2_), channel_id=1, source_target_pairs={{0,4},{2,6},{4,0},{6,2},{9,13},{11,15},{13,9},{15,11},{16,20},{18,... | collective-permute-start | bytes 3784712 | tf_op jit(solution)/shard_map/ppermute | solution.py:48
  49.4 16.8 %collective-permute-start.10 = (bf16[448,1408]{1,0:T(8,128)(2,1)}, bf16[448,1408]{1,0:T(8,128)(2,1)S(1)}, u32[]{:S(2)}, u32[]{:S(2)}) collective-permute-start(bf16[448,1408]{1,0:T(8,128)(2,1)} %collective-permute-done.1.rest_2_), channel_id=1, source_target_pairs={{0,1},{2,3},{4,5},{6,7},{9,8},{11,10},{13,12},{15,14},{16,17},{18,... | collective-permute-start | bytes 3784712 | tf_op jit(solution)/shard_map/ppermute | solution.py:48
  66.2 4.1 %collective-permute-done.4.rest_4_ = bf16[448,1408]{1,0:T(8,128)(2,1)S(1)} collective-permute-done((bf16[448,1408]{1,0:T(8,128)(2,1)S(1)}, bf16[448,1408]{1,0:T(8,128)(2,1)S(1)}, u32[]{:S(2)}, u32[]{:S(2)}) %collective-permute-start.4) | collective-permute-done | bytes 1261600 | tf_op jit(solution)/shard_map/ppermute | solution.py:48
  70.3 1.4 collective-permute-start.11
  71.6 3.0 %collective-permute-done.6.rest_6_ = bf16[448,1408]{1,0:T(8,128)(2,1)S(1)} collective-permute-done((bf16[448,1408]{1,0:T(8,128)(2,1)}, bf16[448,1408]{1,0:T(8,128)(2,1)S(1)}, u32[]{:S(2)}, u32[]{:S(2)}) %collective-permute-start.6) | collective-permute-done | bytes 1261600 | tf_op jit(solution)/shard_map/ppermute | solution.py:48
  74.7 2.0 collective-permute-start.13
  76.7 1.4 collective-permute-start.14
  78.1 1.4 collective-permute-start.15
  79.4 1.9 collective-permute-start.12
  81.4 3.5 %collective-permute-start.19 = (bf16[448,1408]{1,0:T(8,128)(2,1)S(1)}, bf16[448,1408]{1,0:T(8,128)(2,1)}, u32[]{:S(2)}, u32[]{:S(2)}) collective-permute-start(bf16[448,1408]{1,0:T(8,128)(2,1)S(1)} %collective-permute-done.4.rest_4_), channel_id=1, source_target_pairs={{0,4},{2,6},{4,0},{6,2},{9,13},{11,15},{13,9},{15,11},{16,20},{18,... | collective-permute-start | bytes 3784712 | tf_op jit(solution)/shard_map/ppermute | solution.py:48
  85.0 2.0 collective-permute-start.16
  87.0 3.7 %collective-permute-start.17 = (bf16[448,896]{1,0:T(8,128)(2,1)S(1)}, bf16[448,896]{1,0:T(8,128)(2,1)}, u32[]{:S(2)}, u32[]{:S(2)}) collective-permute-start(bf16[448,896]{1,0:T(8,128)(2,1)S(1)} %bitcast.33), channel_id=1, source_target_pairs={{0,8},{1,9},{2,10},{3,11},{4,12},{5,13},{6,14},{7,15},{8,0},{9,1},... | collective-permute-start | bytes 2408456 | tf_op jit(solution)/shard_map/ppermute | solution.py:48
  91.3 5.5 %norm_pool.1 = (bf16[512,3584]{1,0:T(8,128)(2,1)}, bf16[64,3584]{1,0:T(8,128)(2,1)}) custom-call(s32[8]{0:T(128)} %stack.39.info, bf16[512,3584]{1,0:T(8,128)(2,1)} %hidden.1, bf16[256,3584]{1,0:T(8,128)(2,1)} %collective-permute-done.7.first, bf16[256,3584]{1,0:T(8,128)(2,1)} %collective-permute-done.12.second, f32[1,3584]{1,0:T(1,128)} %reshape.27.gain), custom_call_target="tpu_custom_call" | custom-call | flops 234881024 | bytes 7340032 | tf_op jit(solution)/shard_map/norm_pool/pallas_call | solution.py:99
  96.8 12.2 %collective-permute-done.19.rest_7_ = bf16[448,1408]{1,0:T(8,128)(2,1)} collective-permute-done((bf16[448,1408]{1,0:T(8,128)(2,1)S(1)}, bf16[448,1408]{1,0:T(8,128)(2,1)}, u32[]{:S(2)}, u32[]{:S(2)}) %collective-permute-start.19) | collective-permute-done | bytes 1261600 | tf_op jit(solution)/shard_map/ppermute | solution.py:48
  109.0 9.9 %collective-permute-done.18.rest_2_ = bf16[448,896]{1,0:T(8,128)(2,1)S(1)} collective-permute-done((bf16[448,896]{1,0:T(8,128)(2,1)S(1)}, bf16[448,896]{1,0:T(8,128)(2,1)S(1)}, u32[]{:S(2)}, u32[]{:S(2)}) %collective-permute-start.18) | collective-permute-done | bytes 802848 | tf_op jit(solution)/shard_map/ppermute | solution.py:48
  119.8 1.4 collective-permute-start.20
  121.9 1.3 collective-permute-start.24
  123.2 1.9 collective-permute-start.25
  127.4 6.3 %project.2.rest_0_ = bf16[576,256]{1,0:T(8,128)(2,1)} custom-call(s32[8]{0:T(128)} %stack.39.info, bf16[512,3584]{1,0:T(8,128)(2,1)} %get-tuple-element.83.normed, bf16[64,3584]{1,0:T(8,128)(2,1)} %get-tuple-element.73.pooled, f32[1,512]{1,0:T(1,128)} %bitcast.37, bf16[448,1408]{1,0:T(8,128)(2,1)} %copy-done, bf16[448,1408]{1,0:T(8,128)(2,1)} %copy-done.3, ...), custom_call_target="tpu_custom_call" | custom-call | flops 1056964608 | bytes 7798784 | tf_op jit(solution)/shard_map/project/pallas_call | solution.py:214
  133.9 9.3 %project.3.queries = bf16[512,896]{1,0:T(8,128)(2,1)} custom-call(s32[8]{0:T(128)} %stack.39.info, bf16[512,3584]{1,0:T(8,128)(2,1)} %get-tuple-element.83.normed, f32[1,896]{1,0:T(1,128)} %reshape.29.bias, bf16[448,1408]{1,0:T(8,128)(2,1)} %copy-done, bf16[448,1408]{1,0:T(8,128)(2,1)} %copy-done.3, bf16[448,1408]{1,0:T(8,128)(2,1)} %collective-permute-done.1.rest_2_, ...), custom_call_target="tpu_custom_call" | custom-call | flops 3288334336 | bytes 10092544 | tf_op jit(solution)/shard_map/project/pallas_call | solution.py:214
  143.3 1.5 collective-permute-start.28
  146.1 1.9 collective-permute-start.29
  149.5 7.4 %collective-permute-start.27 = (bf16[256,256]{1,0:T(8,128)(2,1)S(1)}, bf16[256,256]{1,0:T(8,128)(2,1)S(1)}, u32[]{:S(2)}, u32[]{:S(2)}) collective-permute-start(bf16[256,256]{1,0:T(8,128)(2,1)S(1)} %pad_maximum_fusion.1), channel_id=1, source_target_pairs={{0,16},{1,17},{2,18},{3,19},{4,20},{5,21},{6,22},{7,23},{8,24},{9,... | collective-permute-start | bytes 393224 | tf_op jit(solution)/shard_map/ppermute | solution.py:48
  156.9 5.8 %collective-permute-done.27.rest_4_ = bf16[256,256]{1,0:T(8,128)(2,1)S(1)} collective-permute-done((bf16[256,256]{1,0:T(8,128)(2,1)S(1)}, bf16[256,256]{1,0:T(8,128)(2,1)S(1)}, u32[]{:S(2)}, u32[]{:S(2)}) %collective-permute-start.27) | collective-permute-done | bytes 131104 | tf_op jit(solution)/shard_map/ppermute | solution.py:48
  163.4 6.8 %attend.2 = bf16[256,896]{1,0:T(8,128)(2,1)} custom-call(s32[8]{0:T(128)} %stack.39.info, s32[2]{0:T(128)} %ratios.3, bf16[512,896]{1,0:T(8,128)(2,1)} %project.3.queries, bf16[576,256]{1,0:T(8,128)(2,1)} %project.2.rest_0_, bf16[576,256]{1,0:T(8,128)(2,1)} %copy-done.29, bf16[576,256]{1,0:T(8,128)(2,1)} %copy-done.30, bf16[576,256]{1,0:T(8,128)(2,1)} %copy-done.31, ...), custom_call_target="tpu_custom_call" | custom-call | flops 2113929216 | bytes 1835008 | tf_op jit(solution)/shard_map/attend/pallas_call | solution.py:298
  170.6 1.6 collective-permute-start.31
  172.9 7.5 %attend.3 = bf16[256,896]{1,0:T(8,128)(2,1)} custom-call(s32[8]{0:T(128)} %stack.39.info, s32[2]{0:T(128)} %ratios.3, bf16[512,896]{1,0:T(8,128)(2,1)} %project.3.queries, bf16[576,256]{1,0:T(8,128)(2,1)} %project.2.rest_0_, bf16[576,256]{1,0:T(8,128)(2,1)} %copy-done.29, bf16[576,256]{1,0:T(8,128)(2,1)} %copy-done.30, bf16[576,256]{1,0:T(8,128)(2,1)} %copy-done.31, ...), custom_call_target="tpu_custom_call" | custom-call | flops 2113929216 | bytes 1835008 | tf_op jit(solution)/shard_map/attend/pallas_call | solution.py:298
  182.1 8.8 %collective-permute-done.31.rest_7_ = bf16[448,896]{1,0:T(8,128)(2,1)S(1)} collective-permute-done((bf16[448,896]{1,0:T(8,128)(2,1)S(1)}, bf16[448,896]{1,0:T(8,128)(2,1)S(1)}, u32[]{:S(2)}, u32[]{:S(2)}) %collective-permute-start.31) | collective-permute-done | bytes 802848 | tf_op jit(solution)/shard_map/ppermute | solution.py:48
  191.8 7.9 %out_project.2 = (bf16[2,256,896]{2,1,0:T(8,128)(2,1)}, bf16[2,256,896]{2,1,0:T(8,128)(2,1)}) custom-call(s32[8]{0:T(128)} %stack.39.info, bf16[256,896]{1,0:T(8,128)(2,1)} %broadcast_select_fusion.3.attention, bf16[448,896]{1,0:T(8,128)(2,1)} %bitcast.30, bf16[448,896]{1,0:T(8,128)(2,1)} %collective-permute-done.17.rest_1_, bf16[448,896]{1,0:T(8,128)(2,1)} %copy-done.16, ...), custom_call_target="tpu_custom_call" | custom-call | flops 1644167168 | bytes 6422528 | tf_op jit(solution)/shard_map/out_project/pallas_call | solution.py:343
  200.7 1.8 collective-permute-done.33
  203.6 7.9 %out_project.3 = (bf16[2,256,896]{2,1,0:T(8,128)(2,1)}, bf16[2,256,896]{2,1,0:T(8,128)(2,1)}) custom-call(s32[8]{0:T(128)} %stack.39.info, bf16[256,896]{1,0:T(8,128)(2,1)} %broadcast_select_fusion.2.attention, bf16[448,896]{1,0:T(8,128)(2,1)} %bitcast.31, bf16[448,896]{1,0:T(8,128)(2,1)} %collective-permute-done.17.rest_1_, bf16[448,896]{1,0:T(8,128)(2,1)} %copy-done.16, ...), custom_call_target="tpu_custom_call" | custom-call | flops 1644167168 | bytes 6422528 | tf_op jit(solution)/shard_map/out_project/pallas_call | solution.py:343
  211.5 3.9 %collective-permute-done.34 = bf16[256,896]{1,0:T(8,128)(2,1)S(1)} collective-permute-done((bf16[256,896]{1,0:T(8,128)(2,1)S(1)}, bf16[256,896]{1,0:T(8,128)(2,1)S(1)}, u32[]{:S(2)}, u32[]{:S(2)}) %collective-permute-start.34) | collective-permute-done | bytes 458784 | tf_op jit(solution)/shard_map/ppermute | solution.py:48
  215.4 2.7 %collective-permute-done.35 = bf16[2,256,896]{2,1,0:T(8,128)(2,1)S(1)} collective-permute-done((bf16[2,256,896]{2,1,0:T(8,128)(2,1)}, bf16[2,256,896]{2,1,0:T(8,128)(2,1)S(1)}, u32[]{:S(2)}, u32[]{:S(2)}) %collective-permute-start.35) | collective-permute-done | bytes 917536 | tf_op jit(solution)/shard_map/ppermute | solution.py:48
  218.1 1.4 convert_add_fusion
  220.5 11.7 %collective-permute-done.36 = bf16[256,896]{1,0:T(8,128)(2,1)S(1)} collective-permute-done((bf16[256,896]{1,0:T(8,128)(2,1)S(1)}, bf16[256,896]{1,0:T(8,128)(2,1)S(1)}, u32[]{:S(2)}, u32[]{:S(2)}) %collective-permute-start.36) | collective-permute-done | bytes 458784 | tf_op jit(solution)/shard_map/ppermute | solution.py:48
  (130 shorter events, 17.6 us)
Async XLA Ops:
  1.4 20.2 %copy-start = (bf16[448,1408]{1,0:T(8,128)(2,1)}, bf16[448,1408]{1,0:T(8,128)(2,1)S(1)}, u32[]{:S(2)}) copy-start(bf16[448,1408]{1,0:T(8,128)(2,1)S(1)} %bitcast_dynamic-update-slice_fusion.rest_0_) | copy-start | bytes 3784708
  1.4 30.1 %collective-permute-start = (bf16[448,1408]{1,0:T(8,128)(2,1)S(1)}, bf16[448,1408]{1,0:T(8,128)(2,1)S(1)}, u32[]{:S(2)}, u32[]{:S(2)}) collective-permute-start(bf16[448,1408]{1,0:T(8,128)(2,1)S(1)} %bitcast_dynamic-update-slice_fusion.rest_0_), channel_id=1, source_target_pairs={{1,9},{3,11},{5,13},{7,15},{8,0},{10,2},{12,4},{14,6},{17,25},{19,... | collective-permute-start | bytes 3784712 | tf_op jit(solution)/shard_map/ppermute | solution.py:48
  2.7 34.4 %collective-permute-start.1 = (bf16[448,1408]{1,0:T(8,128)(2,1)S(1)}, bf16[448,1408]{1,0:T(8,128)(2,1)}, u32[]{:S(2)}, u32[]{:S(2)}) collective-permute-start(bf16[448,1408]{1,0:T(8,128)(2,1)S(1)} %bitcast_dynamic-update-slice_fusion.rest_0_), channel_id=1, source_target_pairs={{0,16},{2,18},{4,20},{6,22},{9,25},{11,27},{13,29},{15,31},{16,0},... | collective-permute-start | bytes 3784712 | tf_op jit(solution)/shard_map/ppermute | solution.py:48
  8.6 28.5 %collective-permute-start.2 = (bf16[448,1408]{1,0:T(8,128)(2,1)S(1)}, bf16[448,1408]{1,0:T(8,128)(2,1)}, u32[]{:S(2)}, u32[]{:S(2)}) collective-permute-start(bf16[448,1408]{1,0:T(8,128)(2,1)S(1)} %bitcast_dynamic-update-slice_fusion.rest_0_), channel_id=1, source_target_pairs={{0,4},{2,6},{4,0},{6,2},{9,13},{11,15},{13,9},{15,11},{16,20},{18,... | collective-permute-start | bytes 3784712 | tf_op jit(solution)/shard_map/ppermute | solution.py:48
  12.1 72.9 %copy-start.15 = (bf16[896,448]{0,1:T(8,128)(2,1)S(1)}, bf16[896,448]{0,1:T(8,128)(2,1)}, u32[]{:S(2)}) copy-start(bf16[896,448]{0,1:T(8,128)(2,1)} %param.18) | copy-start | bytes 2408452
  15.1 34.4 %collective-permute-start.7 = (bf16[256,3584]{1,0:T(8,128)(2,1)}, bf16[256,3584]{1,0:T(8,128)(2,1)}, u32[]{:S(2)}, u32[]{:S(2)}) collective-permute-start(bf16[256,3584]{1,0:T(8,128)(2,1)} %constant_dynamic-slice_fusion), channel_id=1, source_target_pairs={{1,8},{3,10},{5,12},{7,14},{8,1},{10,3},{12,5},{14,7},{17,24},{19,... | collective-permute-start | bytes 5505032 | tf_op jit(solution)/shard_map/ppermute | solution.py:48
  17.0 4.5 %collective-permute-start.3 = (f32[1408]{0:T(1024)S(1)}, f32[1408]{0:T(1024)S(1)}, u32[]{:S(2)}, u32[]{:S(2)}) collective-permute-start(f32[1408]{0:T(1024)S(1)} %pad_maximum_fusion.2), channel_id=1, source_target_pairs={{0,1},{1,0},{2,3},{3,2},{4,5},{5,4},{6,7},{7,6},{8,9},{9,8},{10,11... | collective-permute-start | bytes 16904 | tf_op jit(solution)/shard_map/ppermute | solution.py:48
  21.5 25.4 %collective-permute-start.8 = (bf16[448,1408]{1,0:T(8,128)(2,1)S(1)}, bf16[448,1408]{1,0:T(8,128)(2,1)S(1)}, u32[]{:S(2)}, u32[]{:S(2)}) collective-permute-start(bf16[448,1408]{1,0:T(8,128)(2,1)S(1)} %bitcast_dynamic-update-slice_fusion.rest_0_), channel_id=1, source_target_pairs={{0,1},{2,3},{4,5},{6,7},{9,8},{11,10},{13,12},{15,14},{16,17},{18,... | collective-permute-start | bytes 3784712 | tf_op jit(solution)/shard_map/ppermute | solution.py:48
  31.5 65.3 %copy-start.3 = (bf16[448,1408]{1,0:T(8,128)(2,1)}, bf16[448,1408]{1,0:T(8,128)(2,1)S(1)}, u32[]{:S(2)}) copy-start(bf16[448,1408]{1,0:T(8,128)(2,1)S(1)} %collective-permute-done.rest_1_) | copy-start | bytes 3784708
  37.1 33.2 %collective-permute-start.4 = (bf16[448,1408]{1,0:T(8,128)(2,1)S(1)}, bf16[448,1408]{1,0:T(8,128)(2,1)S(1)}, u32[]{:S(2)}, u32[]{:S(2)}) collective-permute-start(bf16[448,1408]{1,0:T(8,128)(2,1)S(1)} %collective-permute-done.rest_1_), channel_id=1, source_target_pairs={{0,16},{2,18},{4,20},{6,22},{9,25},{11,27},{13,29},{15,31},{16,0},... | collective-permute-start | bytes 3784712 | tf_op jit(solution)/shard_map/ppermute | solution.py:48
  42.2 29.5 %collective-permute-start.5 = (bf16[448,1408]{1,0:T(8,128)(2,1)S(1)}, bf16[448,1408]{1,0:T(8,128)(2,1)S(1)}, u32[]{:S(2)}, u32[]{:S(2)}) collective-permute-start(bf16[448,1408]{1,0:T(8,128)(2,1)S(1)} %collective-permute-done.rest_1_), channel_id=1, source_target_pairs={{0,4},{2,6},{4,0},{6,2},{9,13},{11,15},{13,9},{15,11},{16,20},{18,... | collective-permute-start | bytes 3784712 | tf_op jit(solution)/shard_map/ppermute | solution.py:48
  45.6 29.1 %collective-permute-start.9 = (bf16[448,1408]{1,0:T(8,128)(2,1)S(1)}, bf16[448,1408]{1,0:T(8,128)(2,1)S(1)}, u32[]{:S(2)}, u32[]{:S(2)}) collective-permute-start(bf16[448,1408]{1,0:T(8,128)(2,1)S(1)} %collective-permute-done.rest_1_), channel_id=1, source_target_pairs={{0,1},{2,3},{4,5},{6,7},{9,8},{11,10},{13,12},{15,14},{16,17},{18,... | collective-permute-start | bytes 3784712 | tf_op jit(solution)/shard_map/ppermute | solution.py:48
  47.0 27.7 %copy-start.4 = (bf16[448,1408]{1,0:T(8,128)(2,1)}, bf16[448,1408]{1,0:T(8,128)(2,1)S(1)}, u32[]{:S(2)}) copy-start(bf16[448,1408]{1,0:T(8,128)(2,1)S(1)} %collective-permute-done.8.rest_8_) | copy-start | bytes 3784708
  47.0 27.7 %collective-permute-start.6 = (bf16[448,1408]{1,0:T(8,128)(2,1)}, bf16[448,1408]{1,0:T(8,128)(2,1)S(1)}, u32[]{:S(2)}, u32[]{:S(2)}) collective-permute-start(bf16[448,1408]{1,0:T(8,128)(2,1)} %collective-permute-done.1.rest_2_), channel_id=1, source_target_pairs={{0,4},{2,6},{4,0},{6,2},{9,13},{11,15},{13,9},{15,11},{16,20},{18,... | collective-permute-start | bytes 3784712 | tf_op jit(solution)/shard_map/ppermute | solution.py:48
  49.4 25.2 %collective-permute-start.10 = (bf16[448,1408]{1,0:T(8,128)(2,1)}, bf16[448,1408]{1,0:T(8,128)(2,1)S(1)}, u32[]{:S(2)}, u32[]{:S(2)}) collective-permute-start(bf16[448,1408]{1,0:T(8,128)(2,1)} %collective-permute-done.1.rest_2_), channel_id=1, source_target_pairs={{0,1},{2,3},{4,5},{6,7},{9,8},{11,10},{13,12},{15,14},{16,17},{18,... | collective-permute-start | bytes 3784712 | tf_op jit(solution)/shard_map/ppermute | solution.py:48
  70.3 26.6 %copy-start.5 = (bf16[448,1408]{1,0:T(8,128)(2,1)}, bf16[448,1408]{1,0:T(8,128)(2,1)S(1)}, u32[]{:S(2)}) copy-start(bf16[448,1408]{1,0:T(8,128)(2,1)S(1)} %collective-permute-done.4.rest_4_) | copy-start | bytes 3784708
  70.3 4.4 %collective-permute-start.11 = (bf16[448,1408]{1,0:T(8,128)(2,1)}, bf16[448,1408]{1,0:T(8,128)(2,1)S(1)}, u32[]{:S(2)}, u32[]{:S(2)}) collective-permute-start(bf16[448,1408]{1,0:T(8,128)(2,1)} %collective-permute-done.2.rest_3_), channel_id=1, source_target_pairs={{0,1},{2,3},{4,5},{6,7},{9,8},{11,10},{13,12},{15,14},{16,17},{18,... | collective-permute-start | bytes 3784712 | tf_op jit(solution)/shard_map/ppermute | solution.py:48
  71.6 25.2 %copy-start.6 = (bf16[448,1408]{1,0:T(8,128)(2,1)}, bf16[448,1408]{1,0:T(8,128)(2,1)S(1)}, u32[]{:S(2)}) copy-start(bf16[448,1408]{1,0:T(8,128)(2,1)S(1)} %collective-permute-done.5.rest_5_) | copy-start | bytes 3784708
  74.7 22.2 %copy-start.8 = (bf16[448,1408]{1,0:T(8,128)(2,1)}, bf16[448,1408]{1,0:T(8,128)(2,1)S(1)}, u32[]{:S(2)}) copy-start(bf16[448,1408]{1,0:T(8,128)(2,1)S(1)} %collective-permute-done.6.rest_6_) | copy-start | bytes 3784708
  74.7 22.2 %copy-start.7 = (bf16[448,1408]{1,0:T(8,128)(2,1)}, bf16[448,1408]{1,0:T(8,128)(2,1)S(1)}, u32[]{:S(2)}) copy-start(bf16[448,1408]{1,0:T(8,128)(2,1)S(1)} %collective-permute-done.9.rest_9_) | copy-start | bytes 3784708
  74.7 10.2 %collective-permute-start.13 = (bf16[448,1408]{1,0:T(8,128)(2,1)S(1)}, bf16[448,1408]{1,0:T(8,128)(2,1)S(1)}, u32[]{:S(2)}, u32[]{:S(2)}) collective-permute-start(bf16[448,1408]{1,0:T(8,128)(2,1)S(1)} %collective-permute-done.4.rest_4_), channel_id=1, source_target_pairs={{0,1},{2,3},{4,5},{6,7},{9,8},{11,10},{13,12},{15,14},{16,17},{18,... | collective-permute-start | bytes 3784712 | tf_op jit(solution)/shard_map/ppermute | solution.py:48
  76.7 8.3 %collective-permute-start.14 = (bf16[448,1408]{1,0:T(8,128)(2,1)S(1)}, bf16[448,1408]{1,0:T(8,128)(2,1)S(1)}, u32[]{:S(2)}, u32[]{:S(2)}) collective-permute-start(bf16[448,1408]{1,0:T(8,128)(2,1)S(1)} %collective-permute-done.5.rest_5_), channel_id=1, source_target_pairs={{0,1},{2,3},{4,5},{6,7},{9,8},{11,10},{13,12},{15,14},{16,17},{18,... | collective-permute-start | bytes 3784712 | tf_op jit(solution)/shard_map/ppermute | solution.py:48
  78.1 6.9 %collective-permute-start.15 = (bf16[448,1408]{1,0:T(8,128)(2,1)S(1)}, bf16[448,1408]{1,0:T(8,128)(2,1)S(1)}, u32[]{:S(2)}, u32[]{:S(2)}) collective-permute-start(bf16[448,1408]{1,0:T(8,128)(2,1)S(1)} %collective-permute-done.6.rest_6_), channel_id=1, source_target_pairs={{0,1},{2,3},{4,5},{6,7},{9,8},{11,10},{13,12},{15,14},{16,17},{18,... | collective-permute-start | bytes 3784712 | tf_op jit(solution)/shard_map/ppermute | solution.py:48
  79.4 11.9 %collective-permute-start.12 = (bf16[256,3584]{1,0:T(8,128)(2,1)}, bf16[256,3584]{1,0:T(8,128)(2,1)}, u32[]{:S(2)}, u32[]{:S(2)}) collective-permute-start(bf16[256,3584]{1,0:T(8,128)(2,1)} %collective-permute-done.7.first), channel_id=1, source_target_pairs={{1,3},{3,1},{5,7},{7,5},{8,10},{10,8},{12,14},{14,12},{17,19},{19,... | collective-permute-start | bytes 5505032 | tf_op jit(solution)/shard_map/ppermute | solution.py:48
  81.4 27.7 %collective-permute-start.19 = (bf16[448,1408]{1,0:T(8,128)(2,1)S(1)}, bf16[448,1408]{1,0:T(8,128)(2,1)}, u32[]{:S(2)}, u32[]{:S(2)}) collective-permute-start(bf16[448,1408]{1,0:T(8,128)(2,1)S(1)} %collective-permute-done.4.rest_4_), channel_id=1, source_target_pairs={{0,4},{2,6},{4,0},{6,2},{9,13},{11,15},{13,9},{15,11},{16,20},{18,... | collective-permute-start | bytes 3784712 | tf_op jit(solution)/shard_map/ppermute | solution.py:48
  85.0 24.0 %collective-permute-start.16 = (bf16[448,896]{1,0:T(8,128)(2,1)S(1)}, bf16[448,896]{1,0:T(8,128)(2,1)}, u32[]{:S(2)}, u32[]{:S(2)}) collective-permute-start(bf16[448,896]{1,0:T(8,128)(2,1)S(1)} %bitcast.32), channel_id=1, source_target_pairs={{8,16},{9,17},{10,18},{11,19},{12,20},{13,21},{14,22},{15,23},{16,... | collective-permute-start | bytes 2408456 | tf_op jit(solution)/shard_map/ppermute | solution.py:48
  87.0 22.0 %collective-permute-start.17 = (bf16[448,896]{1,0:T(8,128)(2,1)S(1)}, bf16[448,896]{1,0:T(8,128)(2,1)}, u32[]{:S(2)}, u32[]{:S(2)}) collective-permute-start(bf16[448,896]{1,0:T(8,128)(2,1)S(1)} %bitcast.33), channel_id=1, source_target_pairs={{0,8},{1,9},{2,10},{3,11},{4,12},{5,13},{6,14},{7,15},{8,0},{9,1},... | collective-permute-start | bytes 2408456 | tf_op jit(solution)/shard_map/ppermute | solution.py:48
  90.8 28.2 %collective-permute-start.18 = (bf16[448,896]{1,0:T(8,128)(2,1)S(1)}, bf16[448,896]{1,0:T(8,128)(2,1)S(1)}, u32[]{:S(2)}, u32[]{:S(2)}) collective-permute-start(bf16[448,896]{1,0:T(8,128)(2,1)S(1)} %bitcast.34), channel_id=1, source_target_pairs={{0,4},{1,5},{2,6},{3,7},{4,0},{5,1},{6,2},{7,3},{8,12},{9,13},{10,... | collective-permute-start | bytes 2408456 | tf_op jit(solution)/shard_map/ppermute | solution.py:48
  119.8 6.4 %collective-permute-start.20 = (bf16[448,1408]{1,0:T(8,128)(2,1)}, bf16[448,1408]{1,0:T(8,128)(2,1)S(1)}, u32[]{:S(2)}, u32[]{:S(2)}) collective-permute-start(bf16[448,1408]{1,0:T(8,128)(2,1)} %collective-permute-done.19.rest_7_), channel_id=1, source_target_pairs={{0,1},{2,3},{4,5},{6,7},{9,8},{11,10},{13,12},{15,14},{16,17},{18,... | collective-permute-start | bytes 3784712 | tf_op jit(solution)/shard_map/ppermute | solution.py:48
  121.2 22.1 %collective-permute-start.23 = (bf16[448,896]{1,0:T(8,128)(2,1)}, bf16[448,896]{1,0:T(8,128)(2,1)S(1)}, u32[]{:S(2)}, u32[]{:S(2)}) collective-permute-start(bf16[448,896]{1,0:T(8,128)(2,1)} %collective-permute-done.17.rest_1_), channel_id=1, source_target_pairs={{8,16},{9,17},{10,18},{11,19},{12,20},{13,21},{14,22},{15,23},{16,... | collective-permute-start | bytes 2408456 | tf_op jit(solution)/shard_map/ppermute | solution.py:48
  121.9 21.4 %collective-permute-start.24 = (bf16[448,896]{1,0:T(8,128)(2,1)}, bf16[448,896]{1,0:T(8,128)(2,1)}, u32[]{:S(2)}, u32[]{:S(2)}) collective-permute-start(bf16[448,896]{1,0:T(8,128)(2,1)} %collective-permute-done.16), channel_id=1, source_target_pairs={{8,0},{9,1},{10,2},{11,3},{12,4},{13,5},{14,6},{15,7},{16,24},{17,... | collective-permute-start | bytes 2408456 | tf_op jit(solution)/shard_map/ppermute | solution.py:48
  123.2 20.1 %collective-permute-start.25 = (bf16[448,896]{1,0:T(8,128)(2,1)}, bf16[448,896]{1,0:T(8,128)(2,1)S(1)}, u32[]{:S(2)}, u32[]{:S(2)}) collective-permute-start(bf16[448,896]{1,0:T(8,128)(2,1)} %collective-permute-done.17.rest_1_), channel_id=1, source_target_pairs={{0,4},{1,5},{2,6},{3,7},{4,0},{5,1},{6,2},{7,3},{8,12},{9,13},{10,... | collective-permute-start | bytes 2408456 | tf_op jit(solution)/shard_map/ppermute | solution.py:48
  133.7 9.6 %collective-permute-start.21 = (bf16[576,256]{1,0:T(8,128)(2,1)}, bf16[576,256]{1,0:T(8,128)(2,1)S(1)}, u32[]{:S(2)}, u32[]{:S(2)}) collective-permute-start(bf16[576,256]{1,0:T(8,128)(2,1)} %project.2.rest_0_), channel_id=1, source_target_pairs={{0,4},{1,5},{2,6},{3,7},{4,0},{5,1},{6,2},{7,3},{8,12},{9,13},{10,... | collective-permute-start | bytes 884744 | tf_op jit(solution)/shard_map/ppermute | solution.py:48
  133.9 9.3 %collective-permute-start.22 = (bf16[576,256]{1,0:T(8,128)(2,1)}, bf16[576,256]{1,0:T(8,128)(2,1)S(1)}, u32[]{:S(2)}, u32[]{:S(2)}) collective-permute-start(bf16[576,256]{1,0:T(8,128)(2,1)} %project.2.rest_0_), channel_id=1, source_target_pairs={{0,1},{1,0},{2,3},{3,2},{4,5},{5,4},{6,7},{7,6},{8,9},{9,8},{10,11... | collective-permute-start | bytes 884744 | tf_op jit(solution)/shard_map/ppermute | solution.py:48
  143.3 27.2 %collective-permute-start.28 = (bf16[448,896]{1,0:T(8,128)(2,1)S(1)}, bf16[448,896]{1,0:T(8,128)(2,1)S(1)}, u32[]{:S(2)}, u32[]{:S(2)}) collective-permute-start(bf16[448,896]{1,0:T(8,128)(2,1)S(1)} %collective-permute-done.23), channel_id=1, source_target_pairs={{8,0},{9,1},{10,2},{11,3},{12,4},{13,5},{14,6},{15,7},{16,24},{17,... | collective-permute-start | bytes 2408456 | tf_op jit(solution)/shard_map/ppermute | solution.py:48
  146.0 24.1 %copy-start.1 = (bf16[448,896]{1,0:T(8,128)(2,1)}, bf16[448,896]{1,0:T(8,128)(2,1)S(1)}, u32[]{:S(2)}) copy-start(bf16[448,896]{1,0:T(8,128)(2,1)S(1)} %broadcast_select_fusion.1.rest_4_) | copy-start | bytes 2408452
  146.1 24.5 %collective-permute-start.29 = (bf16[448,896]{1,0:T(8,128)(2,1)S(1)}, bf16[448,896]{1,0:T(8,128)(2,1)S(1)}, u32[]{:S(2)}, u32[]{:S(2)}) collective-permute-start(bf16[448,896]{1,0:T(8,128)(2,1)S(1)} %broadcast_select_fusion.1.rest_4_), channel_id=1, source_target_pairs={{0,4},{1,5},{2,6},{3,7},{4,0},{5,1},{6,2},{7,3},{8,12},{9,13},{10,... | collective-permute-start | bytes 2408456 | tf_op jit(solution)/shard_map/ppermute | solution.py:48
  147.9 1.6 collective-permute-start.26
  149.5 13.2 %copy-start.31 = (bf16[576,256]{1,0:T(8,128)(2,1)}, bf16[576,256]{1,0:T(8,128)(2,1)S(1)}, u32[]{:S(2)}) copy-start(bf16[576,256]{1,0:T(8,128)(2,1)S(1)} %collective-permute-done.26.rest_3_) | copy-start | bytes 884740
  149.5 13.2 %collective-permute-start.27 = (bf16[256,256]{1,0:T(8,128)(2,1)S(1)}, bf16[256,256]{1,0:T(8,128)(2,1)S(1)}, u32[]{:S(2)}, u32[]{:S(2)}) collective-permute-start(bf16[256,256]{1,0:T(8,128)(2,1)S(1)} %pad_maximum_fusion.1), channel_id=1, source_target_pairs={{0,16},{1,17},{2,18},{3,19},{4,20},{5,21},{6,22},{7,23},{8,24},{9,... | collective-permute-start | bytes 393224 | tf_op jit(solution)/shard_map/ppermute | solution.py:48
  170.6 20.3 %collective-permute-start.31 = (bf16[448,896]{1,0:T(8,128)(2,1)S(1)}, bf16[448,896]{1,0:T(8,128)(2,1)S(1)}, u32[]{:S(2)}, u32[]{:S(2)}) collective-permute-start(bf16[448,896]{1,0:T(8,128)(2,1)S(1)} %broadcast_select_fusion.rest_6_), channel_id=1, source_target_pairs={{0,4},{1,5},{2,6},{3,7},{4,0},{5,1},{6,2},{7,3},{8,12},{9,13},{10,... | collective-permute-start | bytes 2408456 | tf_op jit(solution)/shard_map/ppermute | solution.py:48
  172.2 8.2 %collective-permute-start.30 = (bf16[256,896]{1,0:T(8,128)(2,1)S(1)}, bf16[256,896]{1,0:T(8,128)(2,1)S(1)}, u32[]{:S(2)}, u32[]{:S(2)}) collective-permute-start(bf16[256,896]{1,0:T(8,128)(2,1)S(1)} %copy-done.21), channel_id=1, source_target_pairs={{1,8},{3,10},{5,12},{7,14},{8,1},{10,3},{12,5},{14,7},{17,24},{19,... | collective-permute-start | bytes 1376264 | tf_op jit(solution)/shard_map/ppermute | solution.py:48
  180.4 19.4 %collective-permute-start.32 = (bf16[256,896]{1,0:T(8,128)(2,1)}, bf16[256,896]{1,0:T(8,128)(2,1)S(1)}, u32[]{:S(2)}, u32[]{:S(2)}) collective-permute-start(bf16[256,896]{1,0:T(8,128)(2,1)} %attend.3), channel_id=1, source_target_pairs={{1,8},{3,10},{5,12},{7,14},{8,1},{10,3},{12,5},{14,7},{17,24},{19,... | collective-permute-start | bytes 1376264 | tf_op jit(solution)/shard_map/ppermute | solution.py:48
  182.1 17.7 %copy-start.22 = (bf16[256,896]{1,0:T(8,128)(2,1)S(1)}, bf16[256,896]{1,0:T(8,128)(2,1)}, u32[]{:S(2)}) copy-start(bf16[256,896]{1,0:T(8,128)(2,1)} %attend.3) | copy-start | bytes 1376260
  199.7 2.7 %collective-permute-start.33 = (bf16[2,256,896]{2,1,0:T(8,128)(2,1)}, bf16[2,256,896]{2,1,0:T(8,128)(2,1)S(1)}, u32[]{:S(2)}, u32[]{:S(2)}) collective-permute-start(bf16[2,256,896]{2,1,0:T(8,128)(2,1)} %get-tuple-element.108), channel_id=1, source_target_pairs={{0,1},{1,0},{2,3},{3,2},{4,5},{5,4},{6,7},{7,6},{8,9},{9,8},{10,11... | collective-permute-start | bytes 2752520 | tf_op jit(solution)/shard_map/ppermute | solution.py:48
  202.8 12.6 %collective-permute-start.34 = (bf16[256,896]{1,0:T(8,128)(2,1)S(1)}, bf16[256,896]{1,0:T(8,128)(2,1)S(1)}, u32[]{:S(2)}, u32[]{:S(2)}) collective-permute-start(bf16[256,896]{1,0:T(8,128)(2,1)S(1)} %fusion.2), channel_id=1, source_target_pairs={{0,2},{1,3},{2,0},{3,1},{4,6},{5,7},{6,4},{7,5},{8,10},{9,11},{10,... | collective-permute-start | bytes 1376264 | tf_op jit(solution)/shard_map/ppermute | solution.py:48
  215.4 2.7 %collective-permute-start.35 = (bf16[2,256,896]{2,1,0:T(8,128)(2,1)}, bf16[2,256,896]{2,1,0:T(8,128)(2,1)S(1)}, u32[]{:S(2)}, u32[]{:S(2)}) collective-permute-start(bf16[2,256,896]{2,1,0:T(8,128)(2,1)} %get-tuple-element.116), channel_id=1, source_target_pairs={{0,1},{1,0},{2,3},{3,2},{4,5},{5,4},{6,7},{7,6},{8,9},{9,8},{10,11... | collective-permute-start | bytes 2752520 | tf_op jit(solution)/shard_map/ppermute | solution.py:48
  219.6 12.6 %collective-permute-start.36 = (bf16[256,896]{1,0:T(8,128)(2,1)S(1)}, bf16[256,896]{1,0:T(8,128)(2,1)S(1)}, u32[]{:S(2)}, u32[]{:S(2)}) collective-permute-start(bf16[256,896]{1,0:T(8,128)(2,1)S(1)} %fusion.3), channel_id=1, source_target_pairs={{0,2},{1,3},{2,0},{3,1},{4,6},{5,7},{6,4},{7,5},{8,10},{9,11},{10,... | collective-permute-start | bytes 1376264 | tf_op jit(solution)/shard_map/ppermute | solution.py:48
  (23 other events, 109.7 us)

commit v5 on v4

--- a/solution.py
+++ b/solution.py
@@ -448,12 +448,15 @@
     own[0, 1, 0] = to_other_l(shard)
     own[1, 0, 0] = to_other_big(shard, 1)
     own[0, 0, 1] = to_other_x(shard)
+    half_rows = out_shard.shape[0] // 2
+    upper = swap_x(out_shard[:half_rows])
+    gain = norm_gain.reshape(1, -1)
+    own[0, 1, 0], own[1, 0, 0], own[0, 0, 1], upper, out_shard, gain, info = together(
+        own[0, 1, 0], own[1, 0, 0], own[0, 0, 1], upper, out_shard, gain, info
+    )
+    lower = swap_x(out_shard[half_rows:])
     other_biases = send(biases, n_seq, lambda big, l, x, y, c: (big, l, x, y, 1 - c))
     biases = jnp.where(matched, biases, other_biases)
-    gain = norm_gain.reshape(1, -1)
-    own[0, 1, 0], own[1, 0, 0], own[0, 0, 1], biases, gain, info = together(
-        own[0, 1, 0], own[1, 0, 0], own[0, 0, 1], biases, gain, info
-    )
     own[1, 1, 0] = to_other_big(own[0, 1, 0], 1)
     own[0, 1, 1] = to_other_x(own[0, 1, 0])
     own[1, 0, 1] = to_other_x(own[1, 0, 0])
@@ -465,12 +468,20 @@
         own[0, 1, 1],
         own[1, 0, 1],
         first,
+        biases,
+        lower,
         copied[0, 0, 0],
         copied[0, 1, 0],
         copied[1, 0, 0],
         copied[0, 0, 1],
     ) = together(
-        own[1, 1, 0], own[0, 1, 1], own[1, 0, 1], first, *[copied[key] for key in keys]
+        own[1, 1, 0],
+        own[0, 1, 1],
+        own[1, 0, 1],
+        first,
+        biases,
+        lower,
+        *[copied[key] for key in keys],
     )
     own[1, 1, 1] = to_other_x(own[1, 1, 0])
     second = send(first, n_seq, lambda big, l, x, y, c: (big, l, x, 1 - y, c) if c != l else None)
@@ -483,7 +494,7 @@
     outs = {(0, 0, 0): out_shard, (0, 1, 0): swap_l(out_shard)}
     two_segments = n_seq == 2 * SPLIT
     middle_own = swap_inner(out_shard) if two_segments else out_shard
-    outs[0, 0, 1] = swap_x(out_shard)
+    outs[0, 0, 1] = jnp.concatenate([upper, lower], axis=0)
     bit = 2
     while bit < n_seq // SPLIT:
         for key in list(own):
@@ -494,8 +505,8 @@
 
     normed, pooled = norm_and_pool(info, hidden, first, second, gain)
     if two_segments:
-        normed, middle_own, outs[0, 1, 0], outs[0, 0, 1], own[1, 1, 1] = together(
-            normed, middle_own, outs[0, 1, 0], outs[0, 0, 1], own[1, 1, 1]
+        normed, middle_own, outs[0, 1, 0], own[1, 1, 1] = together(
+            normed, middle_own, outs[0, 1, 0], own[1, 1, 1]
         )
         middle_other = swap_inner(outs[0, 1, 0])
         outer_own = to_outer(middle_own)

time: 235 us -> 229 us (0.974)
  starting transfers between devices: 83.2 us -> 71.9 us
  waiting for transfers between devices: 77.9 us -> 81.9 us
    ppermute x37 -> x38, starting transfers between devices: 83.2 us -> 71.9 us  [send(): return lax.ppermute(value, AXES, moves(n_seq, rule))]
    ppermute x37 -> x38, waiting for transfers between devices: 77.9 us -> 81.9 us  [send(): return lax.ppermute(value, AXES, moves(n_seq, rule))]
    unnamed x70 -> x71, local copies, waits for them, and re-layouts: 5.01 us -> 5.12 us
  transfers between devices with their start and end apart: 37 -> 38, of which waited for: 14 -> 16; matrix products, arithmetic and copies ran while one was open for 4% -> 6% of each run, Pallas kernels for 22% -> 22%
where the time goes in v5:
time: 229 us; the launch traced here: 228 us
  waiting for transfers between devices  81.9 us (36%)
  starting transfers between devices  71.9 us (31%)
  Pallas kernels  51.1 us (22%)
  local copies, waits for them, and re-layouts  13.9 us (6%)
  other arithmetic  6.5 us (3%)
  between operations  2.42 us (1%)
    ppermute x38, waiting for transfers between devices, send(): return lax.ppermute(value, AXES, moves(n_seq, rule))  81.9 us
    ppermute x38, starting transfers between devices, send(): return lax.ppermute(value, AXES, moves(n_seq, rule))  71.9 us
    pallas_call x2, Pallas kernels, out_project(): pl.pallas_call(functools.partial(out_kernel, keys), out_shape=(shape, sha...  15.7 us
    pallas_call x2, Pallas kernels, project(): pl.pallas_call(functools.partial(kernel, keys), out_shape=jax.ShapeDtypeS...  15.6 us
    pallas_call x2, Pallas kernels, attend(): pl.pallas_call(functools.partial(attend_kernel, tokens, slots, len(beacon...  14.3 us
    pallas_call x1, Pallas kernels, norm_and_pool(): pl.pallas_call(norm_kernel, out_shape=(jax.ShapeDtypeStruct((rows, width)...  5.49 us
    unnamed x71, local copies, waits for them, and re-layouts  5.12 us
  transfers between devices with their start and end apart: 38, of which 16 were waited for; matrix products, arithmetic and copies ran while one was open for 6% of the time, Pallas kernels for 22%

profile of v5, /device:TPU:0, one launch (start us, length us, event | category | flops | bytes accessed | tf_op | source)
XLA Modules:
  0.0 227.7 jit_solution(18281894069045842161)
XLA Ops:
  1.4 1.3 collective-permute-start
  2.7 5.9 %collective-permute-start.1 = (bf16[448,1408]{1,0:T(8,128)(2,1)S(1)}, bf16[448,1408]{1,0:T(8,128)(2,1)}, u32[]{:S(2)}, u32[]{:S(2)}) collective-permute-start(bf16[448,1408]{1,0:T(8,128)(2,1)S(1)} %bitcast_dynamic-update-slice_fusion.rest_0_), channel_id=1, source_target_pairs={{0,16},{2,18},{4,20},{6,22},{9,25},{11,27},{13,29},{15,31},{16,0},... | collective-permute-start | bytes 3784712 | tf_op jit(solution)/shard_map/ppermute | solution.py:48
  8.6 3.4 %collective-permute-start.2 = (bf16[448,1408]{1,0:T(8,128)(2,1)S(1)}, bf16[448,1408]{1,0:T(8,128)(2,1)}, u32[]{:S(2)}, u32[]{:S(2)}) collective-permute-start(bf16[448,1408]{1,0:T(8,128)(2,1)S(1)} %bitcast_dynamic-update-slice_fusion.rest_0_), channel_id=1, source_target_pairs={{0,4},{2,6},{4,0},{6,2},{9,13},{11,15},{13,9},{15,11},{16,20},{18,... | collective-permute-start | bytes 3784712 | tf_op jit(solution)/shard_map/ppermute | solution.py:48
  12.1 3.0 %constant_dynamic-slice_fusion = bf16[256,3584]{1,0:T(8,128)(2,1)} fusion(bf16[512,3584]{1,0:T(8,128)(2,1)} %hidden.1, s32[]{:T(128)S(6)} %select_n.77), kind=kLoop, calls=%fused_computation.26 | loop fusion | bytes 3670020 | tf_op jit(solution)/shard_map/dynamic_slice | solution.py:444
  15.1 2.0 collective-permute-start.7
  22.5 16.6 %collective-permute-done.3 = bf16[224,896]{1,0:T(8,128)(2,1)} collective-permute-done((bf16[224,896]{1,0:T(8,128)(2,1)}, bf16[224,896]{1,0:T(8,128)(2,1)}, u32[]{:S(2)}, u32[]{:S(2)}) %collective-permute-start.3) | collective-permute-done | bytes 401440 | tf_op jit(solution)/shard_map/ppermute | solution.py:48
  39.1 1.4 collective-permute-start.10
  40.5 1.9 collective-permute-start.4
  42.5 1.6 collective-permute-start.9
  45.3 2.4 %collective-permute-start.5 = (bf16[448,1408]{1,0:T(8,128)(2,1)S(1)}, bf16[448,1408]{1,0:T(8,128)(2,1)S(1)}, u32[]{:S(2)}, u32[]{:S(2)}) collective-permute-start(bf16[448,1408]{1,0:T(8,128)(2,1)S(1)} %collective-permute-done.rest_1_), channel_id=1, source_target_pairs={{0,4},{2,6},{4,0},{6,2},{9,13},{11,15},{13,9},{15,11},{16,20},{18,... | collective-permute-start | bytes 3784712 | tf_op jit(solution)/shard_map/ppermute | solution.py:48
  47.8 1.4 collective-permute-start.11
  49.1 1.4 collective-permute-done.9
  50.5 3.4 %collective-permute-start.6 = (bf16[448,1408]{1,0:T(8,128)(2,1)}, bf16[448,1408]{1,0:T(8,128)(2,1)S(1)}, u32[]{:S(2)}, u32[]{:S(2)}) collective-permute-start(bf16[448,1408]{1,0:T(8,128)(2,1)} %collective-permute-done.1.rest_2_), channel_id=1, source_target_pairs={{0,4},{2,6},{4,0},{6,2},{9,13},{11,15},{13,9},{15,11},{16,20},{18,... | collective-permute-start | bytes 3784712 | tf_op jit(solution)/shard_map/ppermute | solution.py:48
  53.9 10.5 %collective-permute-start.12 = (bf16[448,1408]{1,0:T(8,128)(2,1)}, bf16[448,1408]{1,0:T(8,128)(2,1)S(1)}, u32[]{:S(2)}, u32[]{:S(2)}) collective-permute-start(bf16[448,1408]{1,0:T(8,128)(2,1)} %collective-permute-done.1.rest_2_), channel_id=1, source_target_pairs={{0,1},{2,3},{4,5},{6,7},{9,8},{11,10},{13,12},{15,14},{16,17},{18,... | collective-permute-start | bytes 3784712 | tf_op jit(solution)/shard_map/ppermute | solution.py:48
  64.5 7.4 %collective-permute-done.4.rest_4_ = bf16[448,1408]{1,0:T(8,128)(2,1)S(1)} collective-permute-done((bf16[448,1408]{1,0:T(8,128)(2,1)S(1)}, bf16[448,1408]{1,0:T(8,128)(2,1)S(1)}, u32[]{:S(2)}, u32[]{:S(2)}) %collective-permute-start.4) | collective-permute-done | bytes 1261600 | tf_op jit(solution)/shard_map/ppermute | solution.py:48
  71.9 1.4 collective-permute-start.13
  73.3 4.5 %collective-permute-done.6.rest_6_ = bf16[448,1408]{1,0:T(8,128)(2,1)S(1)} collective-permute-done((bf16[448,1408]{1,0:T(8,128)(2,1)}, bf16[448,1408]{1,0:T(8,128)(2,1)S(1)}, u32[]{:S(2)}, u32[]{:S(2)}) %collective-permute-start.6) | collective-permute-done | bytes 1261600 | tf_op jit(solution)/shard_map/ppermute | solution.py:48
  77.8 1.4 collective-permute-start.15
  79.2 1.4 collective-permute-start.16
  80.6 1.4 collective-permute-start.17
  82.0 1.9 collective-permute-start.14
  83.9 3.1 %collective-permute-start.20 = (bf16[448,1408]{1,0:T(8,128)(2,1)S(1)}, bf16[448,1408]{1,0:T(8,128)(2,1)}, u32[]{:S(2)}, u32[]{:S(2)}) collective-permute-start(bf16[448,1408]{1,0:T(8,128)(2,1)S(1)} %collective-permute-done.4.rest_4_), channel_id=1, source_target_pairs={{0,4},{2,6},{4,0},{6,2},{9,13},{11,15},{13,9},{15,11},{16,20},{18,... | collective-permute-start | bytes 3784712 | tf_op jit(solution)/shard_map/ppermute | solution.py:48
  87.0 2.0 collective-permute-start.18
  89.0 3.5 %collective-permute-start.19 = (bf16[448,896]{1,0:T(8,128)(2,1)S(1)}, bf16[448,896]{1,0:T(8,128)(2,1)}, u32[]{:S(2)}, u32[]{:S(2)}) collective-permute-start(bf16[448,896]{1,0:T(8,128)(2,1)S(1)} %bitcast.35), channel_id=1, source_target_pairs={{0,8},{1,9},{2,10},{3,11},{4,12},{5,13},{6,14},{7,15},{8,0},{9,1},... | collective-permute-start | bytes 2408456 | tf_op jit(solution)/shard_map/ppermute | solution.py:48
  92.5 5.5 %norm_pool.1 = (bf16[512,3584]{1,0:T(8,128)(2,1)}, bf16[64,3584]{1,0:T(8,128)(2,1)}) custom-call(s32[8]{0:T(128)} %stack.39.info, bf16[512,3584]{1,0:T(8,128)(2,1)} %hidden.1, bf16[256,3584]{1,0:T(8,128)(2,1)} %collective-permute-done.7.first, bf16[256,3584]{1,0:T(8,128)(2,1)} %collective-permute-done.14.second, f32[1,3584]{1,0:T(1,128)} %reshape.25.gain), custom_call_target="tpu_custom_call" | custom-call | flops 234881024 | bytes 7340032 | tf_op jit(solution)/shard_map/norm_pool/pallas_call | solution.py:99
  98.1 4.9 %collective-permute-done.20.rest_7_ = bf16[448,1408]{1,0:T(8,128)(2,1)} collective-permute-done((bf16[448,1408]{1,0:T(8,128)(2,1)S(1)}, bf16[448,1408]{1,0:T(8,128)(2,1)}, u32[]{:S(2)}, u32[]{:S(2)}) %collective-permute-start.20) | collective-permute-done | bytes 1261600 | tf_op jit(solution)/shard_map/ppermute | solution.py:48
  103.0 6.1 %collective-permute-done.19.rest_1_ = bf16[448,896]{1,0:T(8,128)(2,1)} collective-permute-done((bf16[448,896]{1,0:T(8,128)(2,1)S(1)}, bf16[448,896]{1,0:T(8,128)(2,1)}, u32[]{:S(2)}, u32[]{:S(2)}) %collective-permute-start.19) | collective-permute-done | bytes 802848 | tf_op jit(solution)/shard_map/ppermute | solution.py:48
  109.0 3.4 %collective-permute-start.21 = (bf16[448,1408]{1,0:T(8,128)(2,1)}, bf16[448,1408]{1,0:T(8,128)(2,1)S(1)}, u32[]{:S(2)}, u32[]{:S(2)}) collective-permute-start(bf16[448,1408]{1,0:T(8,128)(2,1)} %collective-permute-done.20.rest_7_), channel_id=1, source_target_pairs={{0,1},{2,3},{4,5},{6,7},{9,8},{11,10},{13,12},{15,14},{16,17},{18,... | collective-permute-start | bytes 3784712 | tf_op jit(solution)/shard_map/ppermute | solution.py:48
  113.1 1.3 collective-permute-start.25
  114.4 1.6 collective-permute-start.26
  118.3 6.3 %project.2.rest_0_ = bf16[576,256]{1,0:T(8,128)(2,1)} custom-call(s32[8]{0:T(128)} %stack.39.info, bf16[512,3584]{1,0:T(8,128)(2,1)} %get-tuple-element.86.normed, bf16[64,3584]{1,0:T(8,128)(2,1)} %get-tuple-element.76.pooled, f32[1,512]{1,0:T(1,128)} %bitcast.38, bf16[448,1408]{1,0:T(8,128)(2,1)} %copy-done, bf16[448,1408]{1,0:T(8,128)(2,1)} %copy-done.4, ...), custom_call_target="tpu_custom_call" | custom-call | flops 1056964608 | bytes 7798784 | tf_op jit(solution)/shard_map/project/pallas_call | solution.py:214
  125.2 9.3 %project.3.queries = bf16[512,896]{1,0:T(8,128)(2,1)} custom-call(s32[8]{0:T(128)} %stack.39.info, bf16[512,3584]{1,0:T(8,128)(2,1)} %get-tuple-element.86.normed, f32[1,896]{1,0:T(1,128)} %reshape.29.bias, bf16[448,1408]{1,0:T(8,128)(2,1)} %copy-done, bf16[448,1408]{1,0:T(8,128)(2,1)} %copy-done.4, bf16[448,1408]{1,0:T(8,128)(2,1)} %collective-permute-done.1.rest_2_, ...), custom_call_target="tpu_custom_call" | custom-call | flops 3288334336 | bytes 10092544 | tf_op jit(solution)/shard_map/project/pallas_call | solution.py:214
  134.5 5.7 %collective-permute-done.22.rest_1_ = bf16[576,256]{1,0:T(8,128)(2,1)S(1)} collective-permute-done((bf16[576,256]{1,0:T(8,128)(2,1)}, bf16[576,256]{1,0:T(8,128)(2,1)S(1)}, u32[]{:S(2)}, u32[]{:S(2)}) %collective-permute-start.22) | collective-permute-done | bytes 294944 | tf_op jit(solution)/shard_map/ppermute | solution.py:48
  140.2 1.5 collective-permute-start.29
  142.9 1.6 collective-permute-start.30
  146.1 3.8 %collective-permute-start.28 = (bf16[256,256]{1,0:T(8,128)(2,1)S(1)}, bf16[256,256]{1,0:T(8,128)(2,1)S(1)}, u32[]{:S(2)}, u32[]{:S(2)}) collective-permute-start(bf16[256,256]{1,0:T(8,128)(2,1)S(1)} %pad_maximum_fusion.1), channel_id=1, source_target_pairs={{0,16},{1,17},{2,18},{3,19},{4,20},{5,21},{6,22},{7,23},{8,24},{9,... | collective-permute-start | bytes 393224 | tf_op jit(solution)/shard_map/ppermute | solution.py:48
  149.9 6.8 %collective-permute-done.28.rest_4_ = bf16[256,256]{1,0:T(8,128)(2,1)S(1)} collective-permute-done((bf16[256,256]{1,0:T(8,128)(2,1)S(1)}, bf16[256,256]{1,0:T(8,128)(2,1)S(1)}, u32[]{:S(2)}, u32[]{:S(2)}) %collective-permute-start.28) | collective-permute-done | bytes 131104 | tf_op jit(solution)/shard_map/ppermute | solution.py:48
  157.3 6.8 %attend.2 = bf16[256,896]{1,0:T(8,128)(2,1)} custom-call(s32[8]{0:T(128)} %stack.39.info, s32[2]{0:T(128)} %ratios.3, bf16[512,896]{1,0:T(8,128)(2,1)} %project.3.queries, bf16[576,256]{1,0:T(8,128)(2,1)} %project.2.rest_0_, bf16[576,256]{1,0:T(8,128)(2,1)} %copy-done.29, bf16[576,256]{1,0:T(8,128)(2,1)} %copy-done.30, bf16[576,256]{1,0:T(8,128)(2,1)} %copy-done.31, ...), custom_call_target="tpu_custom_call" | custom-call | flops 2113929216 | bytes 1835008 | tf_op jit(solution)/shard_map/attend/pallas_call | solution.py:298
  165.2 1.6 collective-permute-start.32
  167.8 7.5 %attend.3 = bf16[256,896]{1,0:T(8,128)(2,1)} custom-call(s32[8]{0:T(128)} %stack.39.info, s32[2]{0:T(128)} %ratios.3, bf16[512,896]{1,0:T(8,128)(2,1)} %project.3.queries, bf16[576,256]{1,0:T(8,128)(2,1)} %project.2.rest_0_, bf16[576,256]{1,0:T(8,128)(2,1)} %copy-done.29, bf16[576,256]{1,0:T(8,128)(2,1)} %copy-done.30, bf16[576,256]{1,0:T(8,128)(2,1)} %copy-done.31, ...), custom_call_target="tpu_custom_call" | custom-call | flops 2113929216 | bytes 1835008 | tf_op jit(solution)/shard_map/attend/pallas_call | solution.py:298
  178.3 6.3 %collective-permute-done.32.rest_7_ = bf16[448,896]{1,0:T(8,128)(2,1)S(1)} collective-permute-done((bf16[448,896]{1,0:T(8,128)(2,1)S(1)}, bf16[448,896]{1,0:T(8,128)(2,1)S(1)}, u32[]{:S(2)}, u32[]{:S(2)}) %collective-permute-start.32) | collective-permute-done | bytes 802848 | tf_op jit(solution)/shard_map/ppermute | solution.py:48
  185.5 7.9 %out_project.2 = (bf16[2,256,896]{2,1,0:T(8,128)(2,1)}, bf16[2,256,896]{2,1,0:T(8,128)(2,1)}) custom-call(s32[8]{0:T(128)} %stack.39.info, bf16[256,896]{1,0:T(8,128)(2,1)} %broadcast_select_fusion.3.attention, bf16[448,896]{1,0:T(8,128)(2,1)} %bitcast.30, bf16[448,896]{1,0:T(8,128)(2,1)} %collective-permute-done.19.rest_1_, bf16[448,896]{1,0:T(8,128)(2,1)} %copy-done.16, ...), custom_call_target="tpu_custom_call" | custom-call | flops 1644167168 | bytes 6422528 | tf_op jit(solution)/shard_map/out_project/pallas_call | solution.py:343
  195.1 1.5 collective-permute-done.34
  197.8 7.9 %out_project.3 = (bf16[2,256,896]{2,1,0:T(8,128)(2,1)}, bf16[2,256,896]{2,1,0:T(8,128)(2,1)}) custom-call(s32[8]{0:T(128)} %stack.39.info, bf16[256,896]{1,0:T(8,128)(2,1)} %broadcast_select_fusion.2.attention, bf16[448,896]{1,0:T(8,128)(2,1)} %bitcast.31, bf16[448,896]{1,0:T(8,128)(2,1)} %collective-permute-done.19.rest_1_, bf16[448,896]{1,0:T(8,128)(2,1)} %copy-done.16, ...), custom_call_target="tpu_custom_call" | custom-call | flops 1644167168 | bytes 6422528 | tf_op jit(solution)/shard_map/out_project/pallas_call | solution.py:343
  205.7 4.1 %collective-permute-done.35 = bf16[256,896]{1,0:T(8,128)(2,1)S(1)} collective-permute-done((bf16[256,896]{1,0:T(8,128)(2,1)S(1)}, bf16[256,896]{1,0:T(8,128)(2,1)S(1)}, u32[]{:S(2)}, u32[]{:S(2)}) %collective-permute-start.35) | collective-permute-done | bytes 458784 | tf_op jit(solution)/shard_map/ppermute | solution.py:48
  209.8 2.7 %collective-permute-done.36 = bf16[2,256,896]{2,1,0:T(8,128)(2,1)S(1)} collective-permute-done((bf16[2,256,896]{2,1,0:T(8,128)(2,1)}, bf16[2,256,896]{2,1,0:T(8,128)(2,1)S(1)}, u32[]{:S(2)}, u32[]{:S(2)}) %collective-permute-start.36) | collective-permute-done | bytes 917536 | tf_op jit(solution)/shard_map/ppermute | solution.py:48
  212.5 1.4 convert_add_fusion
  214.9 11.7 %collective-permute-done.37 = bf16[256,896]{1,0:T(8,128)(2,1)S(1)} collective-permute-done((bf16[256,896]{1,0:T(8,128)(2,1)S(1)}, bf16[256,896]{1,0:T(8,128)(2,1)S(1)}, u32[]{:S(2)}, u32[]{:S(2)}) %collective-permute-start.37) | collective-permute-done | bytes 458784 | tf_op jit(solution)/shard_map/ppermute | solution.py:48
  (136 shorter events, 24.5 us)
Async XLA Ops:
  1.4 37.8 %copy-start = (bf16[448,1408]{1,0:T(8,128)(2,1)}, bf16[448,1408]{1,0:T(8,128)(2,1)S(1)}, u32[]{:S(2)}) copy-start(bf16[448,1408]{1,0:T(8,128)(2,1)S(1)} %bitcast_dynamic-update-slice_fusion.rest_0_) | copy-start | bytes 3784708
  1.4 39.1 %collective-permute-start = (bf16[448,1408]{1,0:T(8,128)(2,1)S(1)}, bf16[448,1408]{1,0:T(8,128)(2,1)S(1)}, u32[]{:S(2)}, u32[]{:S(2)}) collective-permute-start(bf16[448,1408]{1,0:T(8,128)(2,1)S(1)} %bitcast_dynamic-update-slice_fusion.rest_0_), channel_id=1, source_target_pairs={{1,9},{3,11},{5,13},{7,15},{8,0},{10,2},{12,4},{14,6},{17,25},{19,... | collective-permute-start | bytes 3784712 | tf_op jit(solution)/shard_map/ppermute | solution.py:48
  2.7 37.8 %collective-permute-start.1 = (bf16[448,1408]{1,0:T(8,128)(2,1)S(1)}, bf16[448,1408]{1,0:T(8,128)(2,1)}, u32[]{:S(2)}, u32[]{:S(2)}) collective-permute-start(bf16[448,1408]{1,0:T(8,128)(2,1)S(1)} %bitcast_dynamic-update-slice_fusion.rest_0_), channel_id=1, source_target_pairs={{0,16},{2,18},{4,20},{6,22},{9,25},{11,27},{13,29},{15,31},{16,0},... | collective-permute-start | bytes 3784712 | tf_op jit(solution)/shard_map/ppermute | solution.py:48
  8.6 31.9 %collective-permute-start.2 = (bf16[448,1408]{1,0:T(8,128)(2,1)S(1)}, bf16[448,1408]{1,0:T(8,128)(2,1)}, u32[]{:S(2)}, u32[]{:S(2)}) collective-permute-start(bf16[448,1408]{1,0:T(8,128)(2,1)S(1)} %bitcast_dynamic-update-slice_fusion.rest_0_), channel_id=1, source_target_pairs={{0,4},{2,6},{4,0},{6,2},{9,13},{11,15},{13,9},{15,11},{16,20},{18,... | collective-permute-start | bytes 3784712 | tf_op jit(solution)/shard_map/ppermute | solution.py:48
  15.0 29.0 %copy-start.25 = (f32[896]{0:T(1024)S(1)}, f32[896]{0:T(1024)}, u32[]{:S(2)}) copy-start(f32[896]{0:T(1024)} %param.13) | copy-start | bytes 10756
  15.0 29.0 %copy-start.27 = (f32[2,128]{1,0:T(2,128)S(1)}, f32[2,128]{1,0:T(2,128)}, u32[]{:S(2)}) copy-start(f32[2,128]{1,0:T(2,128)} %param.17) | copy-start | bytes 3076
  15.1 29.0 %copy-start.28 = (f32[2,128]{1,0:T(2,128)S(1)}, f32[2,128]{1,0:T(2,128)}, u32[]{:S(2)}) copy-start(f32[2,128]{1,0:T(2,128)} %param.15) | copy-start | bytes 3076
  15.1 38.9 %collective-permute-start.7 = (bf16[256,3584]{1,0:T(8,128)(2,1)}, bf16[256,3584]{1,0:T(8,128)(2,1)}, u32[]{:S(2)}, u32[]{:S(2)}) collective-permute-start(bf16[256,3584]{1,0:T(8,128)(2,1)} %constant_dynamic-slice_fusion), channel_id=1, source_target_pairs={{1,8},{3,10},{5,12},{7,14},{8,1},{10,3},{12,5},{14,7},{17,24},{19,... | collective-permute-start | bytes 5505032 | tf_op jit(solution)/shard_map/ppermute | solution.py:48
  17.9 21.2 %collective-permute-start.3 = (bf16[224,896]{1,0:T(8,128)(2,1)}, bf16[224,896]{1,0:T(8,128)(2,1)}, u32[]{:S(2)}, u32[]{:S(2)}) collective-permute-start(bf16[224,896]{1,0:T(8,128)(2,1)} %slice.50), channel_id=1, source_target_pairs={{0,4},{1,5},{2,6},{3,7},{4,0},{5,1},{6,2},{7,3},{8,12},{9,13},{10,... | collective-permute-start | bytes 1204232 | tf_op jit(solution)/shard_map/ppermute | solution.py:48
  39.1 8.6 %collective-permute-start.10 = (bf16[448,1408]{1,0:T(8,128)(2,1)S(1)}, bf16[448,1408]{1,0:T(8,128)(2,1)S(1)}, u32[]{:S(2)}, u32[]{:S(2)}) collective-permute-start(bf16[448,1408]{1,0:T(8,128)(2,1)S(1)} %bitcast_dynamic-update-slice_fusion.rest_0_), channel_id=1, source_target_pairs={{0,1},{2,3},{4,5},{6,7},{9,8},{11,10},{13,12},{15,14},{16,17},{18,... | collective-permute-start | bytes 3784712 | tf_op jit(solution)/shard_map/ppermute | solution.py:48
  40.5 57.5 %copy-start.4 = (bf16[448,1408]{1,0:T(8,128)(2,1)}, bf16[448,1408]{1,0:T(8,128)(2,1)S(1)}, u32[]{:S(2)}) copy-start(bf16[448,1408]{1,0:T(8,128)(2,1)S(1)} %collective-permute-done.rest_1_) | copy-start | bytes 3784708
  40.5 31.4 %collective-permute-start.4 = (bf16[448,1408]{1,0:T(8,128)(2,1)S(1)}, bf16[448,1408]{1,0:T(8,128)(2,1)S(1)}, u32[]{:S(2)}, u32[]{:S(2)}) collective-permute-start(bf16[448,1408]{1,0:T(8,128)(2,1)S(1)} %collective-permute-done.rest_1_), channel_id=1, source_target_pairs={{0,16},{2,18},{4,20},{6,22},{9,25},{11,27},{13,29},{15,31},{16,0},... | collective-permute-start | bytes 3784712 | tf_op jit(solution)/shard_map/ppermute | solution.py:48
  42.5 8.0 %collective-permute-start.9 = (bf16[224,896]{1,0:T(8,128)(2,1)S(1)}, bf16[224,896]{1,0:T(8,128)(2,1)}, u32[]{:S(2)}, u32[]{:S(2)}) collective-permute-start(bf16[224,896]{1,0:T(8,128)(2,1)S(1)} %slice.39), channel_id=1, source_target_pairs={{0,4},{1,5},{2,6},{3,7},{4,0},{5,1},{6,2},{7,3},{8,12},{9,13},{10,... | collective-permute-start | bytes 1204232 | tf_op jit(solution)/shard_map/ppermute | solution.py:48
  44.1 1.2 collective-permute-start.8
  45.3 28.0 %collective-permute-start.5 = (bf16[448,1408]{1,0:T(8,128)(2,1)S(1)}, bf16[448,1408]{1,0:T(8,128)(2,1)S(1)}, u32[]{:S(2)}, u32[]{:S(2)}) collective-permute-start(bf16[448,1408]{1,0:T(8,128)(2,1)S(1)} %collective-permute-done.rest_1_), channel_id=1, source_target_pairs={{0,4},{2,6},{4,0},{6,2},{9,13},{11,15},{13,9},{15,11},{16,20},{18,... | collective-permute-start | bytes 3784712 | tf_op jit(solution)/shard_map/ppermute | solution.py:48
  47.8 44.7 %copy-start.5 = (bf16[448,1408]{1,0:T(8,128)(2,1)}, bf16[448,1408]{1,0:T(8,128)(2,1)S(1)}, u32[]{:S(2)}) copy-start(bf16[448,1408]{1,0:T(8,128)(2,1)S(1)} %collective-permute-done.10.rest_8_) | copy-start | bytes 3784708
  47.8 30.0 %collective-permute-start.11 = (bf16[448,1408]{1,0:T(8,128)(2,1)S(1)}, bf16[448,1408]{1,0:T(8,128)(2,1)S(1)}, u32[]{:S(2)}, u32[]{:S(2)}) collective-permute-start(bf16[448,1408]{1,0:T(8,128)(2,1)S(1)} %collective-permute-done.rest_1_), channel_id=1, source_target_pairs={{0,1},{2,3},{4,5},{6,7},{9,8},{11,10},{13,12},{15,14},{16,17},{18,... | collective-permute-start | bytes 3784712 | tf_op jit(solution)/shard_map/ppermute | solution.py:48
  50.5 27.3 %collective-permute-start.6 = (bf16[448,1408]{1,0:T(8,128)(2,1)}, bf16[448,1408]{1,0:T(8,128)(2,1)S(1)}, u32[]{:S(2)}, u32[]{:S(2)}) collective-permute-start(bf16[448,1408]{1,0:T(8,128)(2,1)} %collective-permute-done.1.rest_2_), channel_id=1, source_target_pairs={{0,4},{2,6},{4,0},{6,2},{9,13},{11,15},{13,9},{15,11},{16,20},{18,... | collective-permute-start | bytes 3784712 | tf_op jit(solution)/shard_map/ppermute | solution.py:48
  53.9 23.9 %collective-permute-start.12 = (bf16[448,1408]{1,0:T(8,128)(2,1)}, bf16[448,1408]{1,0:T(8,128)(2,1)S(1)}, u32[]{:S(2)}, u32[]{:S(2)}) collective-permute-start(bf16[448,1408]{1,0:T(8,128)(2,1)} %collective-permute-done.1.rest_2_), channel_id=1, source_target_pairs={{0,1},{2,3},{4,5},{6,7},{9,8},{11,10},{13,12},{15,14},{16,17},{18,... | collective-permute-start | bytes 3784712 | tf_op jit(solution)/shard_map/ppermute | solution.py:48
  71.9 26.1 %copy-start.6 = (bf16[448,1408]{1,0:T(8,128)(2,1)}, bf16[448,1408]{1,0:T(8,128)(2,1)S(1)}, u32[]{:S(2)}) copy-start(bf16[448,1408]{1,0:T(8,128)(2,1)S(1)} %collective-permute-done.4.rest_4_) | copy-start | bytes 3784708
  71.9 5.9 %collective-permute-start.13 = (bf16[448,1408]{1,0:T(8,128)(2,1)}, bf16[448,1408]{1,0:T(8,128)(2,1)S(1)}, u32[]{:S(2)}, u32[]{:S(2)}) collective-permute-start(bf16[448,1408]{1,0:T(8,128)(2,1)} %collective-permute-done.2.rest_3_), channel_id=1, source_target_pairs={{0,1},{2,3},{4,5},{6,7},{9,8},{11,10},{13,12},{15,14},{16,17},{18,... | collective-permute-start | bytes 3784712 | tf_op jit(solution)/shard_map/ppermute | solution.py:48
  77.8 20.3 %copy-start.8 = (bf16[448,1408]{1,0:T(8,128)(2,1)}, bf16[448,1408]{1,0:T(8,128)(2,1)S(1)}, u32[]{:S(2)}) copy-start(bf16[448,1408]{1,0:T(8,128)(2,1)S(1)} %collective-permute-done.11.rest_9_) | copy-start | bytes 3784708
  77.8 20.3 %copy-start.10 = (bf16[448,1408]{1,0:T(8,128)(2,1)}, bf16[448,1408]{1,0:T(8,128)(2,1)S(1)}, u32[]{:S(2)}) copy-start(bf16[448,1408]{1,0:T(8,128)(2,1)S(1)} %collective-permute-done.12.rest_10_) | copy-start | bytes 3784708
  77.8 9.1 %collective-permute-start.15 = (bf16[448,1408]{1,0:T(8,128)(2,1)S(1)}, bf16[448,1408]{1,0:T(8,128)(2,1)S(1)}, u32[]{:S(2)}, u32[]{:S(2)}) collective-permute-start(bf16[448,1408]{1,0:T(8,128)(2,1)S(1)} %collective-permute-done.4.rest_4_), channel_id=1, source_target_pairs={{0,1},{2,3},{4,5},{6,7},{9,8},{11,10},{13,12},{15,14},{16,17},{18,... | collective-permute-start | bytes 3784712 | tf_op jit(solution)/shard_map/ppermute | solution.py:48
  79.2 7.8 %collective-permute-start.16 = (bf16[448,1408]{1,0:T(8,128)(2,1)S(1)}, bf16[448,1408]{1,0:T(8,128)(2,1)S(1)}, u32[]{:S(2)}, u32[]{:S(2)}) collective-permute-start(bf16[448,1408]{1,0:T(8,128)(2,1)S(1)} %collective-permute-done.5.rest_5_), channel_id=1, source_target_pairs={{0,1},{2,3},{4,5},{6,7},{9,8},{11,10},{13,12},{15,14},{16,17},{18,... | collective-permute-start | bytes 3784712 | tf_op jit(solution)/shard_map/ppermute | solution.py:48
  80.6 6.4 %collective-permute-start.17 = (bf16[448,1408]{1,0:T(8,128)(2,1)S(1)}, bf16[448,1408]{1,0:T(8,128)(2,1)S(1)}, u32[]{:S(2)}, u32[]{:S(2)}) collective-permute-start(bf16[448,1408]{1,0:T(8,128)(2,1)S(1)} %collective-permute-done.6.rest_6_), channel_id=1, source_target_pairs={{0,1},{2,3},{4,5},{6,7},{9,8},{11,10},{13,12},{15,14},{16,17},{18,... | collective-permute-start | bytes 3784712 | tf_op jit(solution)/shard_map/ppermute | solution.py:48
  82.0 10.5 %collective-permute-start.14 = (bf16[256,3584]{1,0:T(8,128)(2,1)}, bf16[256,3584]{1,0:T(8,128)(2,1)}, u32[]{:S(2)}, u32[]{:S(2)}) collective-permute-start(bf16[256,3584]{1,0:T(8,128)(2,1)} %collective-permute-done.7.first), channel_id=1, source_target_pairs={{1,3},{3,1},{5,7},{7,5},{8,10},{10,8},{12,14},{14,12},{17,19},{19,... | collective-permute-start | bytes 5505032 | tf_op jit(solution)/shard_map/ppermute | solution.py:48
  83.9 19.1 %collective-permute-start.20 = (bf16[448,1408]{1,0:T(8,128)(2,1)S(1)}, bf16[448,1408]{1,0:T(8,128)(2,1)}, u32[]{:S(2)}, u32[]{:S(2)}) collective-permute-start(bf16[448,1408]{1,0:T(8,128)(2,1)S(1)} %collective-permute-done.4.rest_4_), channel_id=1, source_target_pairs={{0,4},{2,6},{4,0},{6,2},{9,13},{11,15},{13,9},{15,11},{16,20},{18,... | collective-permute-start | bytes 3784712 | tf_op jit(solution)/shard_map/ppermute | solution.py:48
  87.0 15.9 %collective-permute-start.18 = (bf16[448,896]{1,0:T(8,128)(2,1)S(1)}, bf16[448,896]{1,0:T(8,128)(2,1)}, u32[]{:S(2)}, u32[]{:S(2)}) collective-permute-start(bf16[448,896]{1,0:T(8,128)(2,1)S(1)} %bitcast.34), channel_id=1, source_target_pairs={{8,16},{9,17},{10,18},{11,19},{12,20},{13,21},{14,22},{15,23},{16,... | collective-permute-start | bytes 2408456 | tf_op jit(solution)/shard_map/ppermute | solution.py:48
  89.0 20.0 %collective-permute-start.19 = (bf16[448,896]{1,0:T(8,128)(2,1)S(1)}, bf16[448,896]{1,0:T(8,128)(2,1)}, u32[]{:S(2)}, u32[]{:S(2)}) collective-permute-start(bf16[448,896]{1,0:T(8,128)(2,1)S(1)} %bitcast.35), channel_id=1, source_target_pairs={{0,8},{1,9},{2,10},{3,11},{4,12},{5,13},{6,14},{7,15},{8,0},{9,1},... | collective-permute-start | bytes 2408456 | tf_op jit(solution)/shard_map/ppermute | solution.py:48
  109.0 8.1 %collective-permute-start.21 = (bf16[448,1408]{1,0:T(8,128)(2,1)}, bf16[448,1408]{1,0:T(8,128)(2,1)S(1)}, u32[]{:S(2)}, u32[]{:S(2)}) collective-permute-start(bf16[448,1408]{1,0:T(8,128)(2,1)} %collective-permute-done.20.rest_7_), channel_id=1, source_target_pairs={{0,1},{2,3},{4,5},{6,7},{9,8},{11,10},{13,12},{15,14},{16,17},{18,... | collective-permute-start | bytes 3784712 | tf_op jit(solution)/shard_map/ppermute | solution.py:48
  112.4 27.7 %collective-permute-start.24 = (bf16[448,896]{1,0:T(8,128)(2,1)}, bf16[448,896]{1,0:T(8,128)(2,1)S(1)}, u32[]{:S(2)}, u32[]{:S(2)}) collective-permute-start(bf16[448,896]{1,0:T(8,128)(2,1)} %collective-permute-done.19.rest_1_), channel_id=1, source_target_pairs={{8,16},{9,17},{10,18},{11,19},{12,20},{13,21},{14,22},{15,23},{16,... | collective-permute-start | bytes 2408456 | tf_op jit(solution)/shard_map/ppermute | solution.py:48
  113.1 27.0 %collective-permute-start.25 = (bf16[448,896]{1,0:T(8,128)(2,1)}, bf16[448,896]{1,0:T(8,128)(2,1)}, u32[]{:S(2)}, u32[]{:S(2)}) collective-permute-start(bf16[448,896]{1,0:T(8,128)(2,1)} %collective-permute-done.18), channel_id=1, source_target_pairs={{8,0},{9,1},{10,2},{11,3},{12,4},{13,5},{14,6},{15,7},{16,24},{17,... | collective-permute-start | bytes 2408456 | tf_op jit(solution)/shard_map/ppermute | solution.py:48
  114.4 25.7 %collective-permute-start.26 = (bf16[448,896]{1,0:T(8,128)(2,1)}, bf16[448,896]{1,0:T(8,128)(2,1)S(1)}, u32[]{:S(2)}, u32[]{:S(2)}) collective-permute-start(bf16[448,896]{1,0:T(8,128)(2,1)} %collective-permute-done.19.rest_1_), channel_id=1, source_target_pairs={{0,4},{1,5},{2,6},{3,7},{4,0},{5,1},{6,2},{7,3},{8,12},{9,13},{10,... | collective-permute-start | bytes 2408456 | tf_op jit(solution)/shard_map/ppermute | solution.py:48
  124.6 15.6 %collective-permute-start.22 = (bf16[576,256]{1,0:T(8,128)(2,1)}, bf16[576,256]{1,0:T(8,128)(2,1)S(1)}, u32[]{:S(2)}, u32[]{:S(2)}) collective-permute-start(bf16[576,256]{1,0:T(8,128)(2,1)} %project.2.rest_0_), channel_id=1, source_target_pairs={{0,4},{1,5},{2,6},{3,7},{4,0},{5,1},{6,2},{7,3},{8,12},{9,13},{10,... | collective-permute-start | bytes 884744 | tf_op jit(solution)/shard_map/ppermute | solution.py:48
  125.2 15.0 %collective-permute-start.23 = (bf16[576,256]{1,0:T(8,128)(2,1)}, bf16[576,256]{1,0:T(8,128)(2,1)S(1)}, u32[]{:S(2)}, u32[]{:S(2)}) collective-permute-start(bf16[576,256]{1,0:T(8,128)(2,1)} %project.2.rest_0_), channel_id=1, source_target_pairs={{0,1},{1,0},{2,3},{3,2},{4,5},{5,4},{6,7},{7,6},{8,9},{9,8},{10,11... | collective-permute-start | bytes 884744 | tf_op jit(solution)/shard_map/ppermute | solution.py:48
  140.2 24.3 %collective-permute-start.29 = (bf16[448,896]{1,0:T(8,128)(2,1)S(1)}, bf16[448,896]{1,0:T(8,128)(2,1)S(1)}, u32[]{:S(2)}, u32[]{:S(2)}) collective-permute-start(bf16[448,896]{1,0:T(8,128)(2,1)S(1)} %collective-permute-done.24), channel_id=1, source_target_pairs={{8,0},{9,1},{10,2},{11,3},{12,4},{13,5},{14,6},{15,7},{16,24},{17,... | collective-permute-start | bytes 2408456 | tf_op jit(solution)/shard_map/ppermute | solution.py:48
  142.9 21.2 %copy-start.2 = (bf16[448,896]{1,0:T(8,128)(2,1)}, bf16[448,896]{1,0:T(8,128)(2,1)S(1)}, u32[]{:S(2)}) copy-start(bf16[448,896]{1,0:T(8,128)(2,1)S(1)} %broadcast_select_fusion.1.rest_4_) | copy-start | bytes 2408452
  142.9 21.5 %collective-permute-start.30 = (bf16[448,896]{1,0:T(8,128)(2,1)S(1)}, bf16[448,896]{1,0:T(8,128)(2,1)S(1)}, u32[]{:S(2)}, u32[]{:S(2)}) collective-permute-start(bf16[448,896]{1,0:T(8,128)(2,1)S(1)} %broadcast_select_fusion.1.rest_4_), channel_id=1, source_target_pairs={{0,4},{1,5},{2,6},{3,7},{4,0},{5,1},{6,2},{7,3},{8,12},{9,13},{10,... | collective-permute-start | bytes 2408456 | tf_op jit(solution)/shard_map/ppermute | solution.py:48
  144.5 1.6 collective-permute-start.27
  146.1 10.6 %collective-permute-start.28 = (bf16[256,256]{1,0:T(8,128)(2,1)S(1)}, bf16[256,256]{1,0:T(8,128)(2,1)S(1)}, u32[]{:S(2)}, u32[]{:S(2)}) collective-permute-start(bf16[256,256]{1,0:T(8,128)(2,1)S(1)} %pad_maximum_fusion.1), channel_id=1, source_target_pairs={{0,16},{1,17},{2,18},{3,19},{4,20},{5,21},{6,22},{7,23},{8,24},{9,... | collective-permute-start | bytes 393224 | tf_op jit(solution)/shard_map/ppermute | solution.py:48
  164.4 10.9 %collective-permute-start.31 = (bf16[256,896]{1,0:T(8,128)(2,1)}, bf16[256,896]{1,0:T(8,128)(2,1)S(1)}, u32[]{:S(2)}, u32[]{:S(2)}) collective-permute-start(bf16[256,896]{1,0:T(8,128)(2,1)} %attend.2), channel_id=1, source_target_pairs={{1,8},{3,10},{5,12},{7,14},{8,1},{10,3},{12,5},{14,7},{17,24},{19,... | collective-permute-start | bytes 1376264 | tf_op jit(solution)/shard_map/ppermute | solution.py:48
  165.2 19.4 %collective-permute-start.32 = (bf16[448,896]{1,0:T(8,128)(2,1)S(1)}, bf16[448,896]{1,0:T(8,128)(2,1)S(1)}, u32[]{:S(2)}, u32[]{:S(2)}) collective-permute-start(bf16[448,896]{1,0:T(8,128)(2,1)S(1)} %broadcast_select_fusion.rest_6_), channel_id=1, source_target_pairs={{0,4},{1,5},{2,6},{3,7},{4,0},{5,1},{6,2},{7,3},{8,12},{9,13},{10,... | collective-permute-start | bytes 2408456 | tf_op jit(solution)/shard_map/ppermute | solution.py:48
  175.4 18.0 %collective-permute-start.33 = (bf16[256,896]{1,0:T(8,128)(2,1)}, bf16[256,896]{1,0:T(8,128)(2,1)S(1)}, u32[]{:S(2)}, u32[]{:S(2)}) collective-permute-start(bf16[256,896]{1,0:T(8,128)(2,1)} %attend.3), channel_id=1, source_target_pairs={{1,8},{3,10},{5,12},{7,14},{8,1},{10,3},{12,5},{14,7},{17,24},{19,... | collective-permute-start | bytes 1376264 | tf_op jit(solution)/shard_map/ppermute | solution.py:48
  193.4 3.2 %collective-permute-start.34 = (bf16[2,256,896]{2,1,0:T(8,128)(2,1)}, bf16[2,256,896]{2,1,0:T(8,128)(2,1)S(1)}, u32[]{:S(2)}, u32[]{:S(2)}) collective-permute-start(bf16[2,256,896]{2,1,0:T(8,128)(2,1)} %get-tuple-element.112), channel_id=1, source_target_pairs={{0,1},{1,0},{2,3},{3,2},{4,5},{5,4},{6,7},{7,6},{8,9},{9,8},{10,11... | collective-permute-start | bytes 2752520 | tf_op jit(solution)/shard_map/ppermute | solution.py:48
  196.9 12.9 %collective-permute-start.35 = (bf16[256,896]{1,0:T(8,128)(2,1)S(1)}, bf16[256,896]{1,0:T(8,128)(2,1)S(1)}, u32[]{:S(2)}, u32[]{:S(2)}) collective-permute-start(bf16[256,896]{1,0:T(8,128)(2,1)S(1)} %fusion.2), channel_id=1, source_target_pairs={{0,2},{1,3},{2,0},{3,1},{4,6},{5,7},{6,4},{7,5},{8,10},{9,11},{10,... | collective-permute-start | bytes 1376264 | tf_op jit(solution)/shard_map/ppermute | solution.py:48
  209.8 2.7 %collective-permute-start.36 = (bf16[2,256,896]{2,1,0:T(8,128)(2,1)}, bf16[2,256,896]{2,1,0:T(8,128)(2,1)S(1)}, u32[]{:S(2)}, u32[]{:S(2)}) collective-permute-start(bf16[2,256,896]{2,1,0:T(8,128)(2,1)} %get-tuple-element.120), channel_id=1, source_target_pairs={{0,1},{1,0},{2,3},{3,2},{4,5},{5,4},{6,7},{7,6},{8,9},{9,8},{10,11... | collective-permute-start | bytes 2752520 | tf_op jit(solution)/shard_map/ppermute | solution.py:48
  213.9 12.6 %collective-permute-start.37 = (bf16[256,896]{1,0:T(8,128)(2,1)S(1)}, bf16[256,896]{1,0:T(8,128)(2,1)S(1)}, u32[]{:S(2)}, u32[]{:S(2)}) collective-permute-start(bf16[256,896]{1,0:T(8,128)(2,1)S(1)} %fusion.3), channel_id=1, source_target_pairs={{0,2},{1,3},{2,0},{3,1},{4,6},{5,7},{6,4},{7,5},{8,10},{9,11},{10,... | collective-permute-start | bytes 1376264 | tf_op jit(solution)/shard_map/ppermute | solution.py:48
  (24 other events, 171.2 us)

commit v6 on v5

--- a/solution.py
+++ b/solution.py
@@ -312,46 +312,48 @@
     )(info, ratios, queries, *keyvals, *beacons)
 
 
-def out_kernel(keys, info, attention, *rest):
+def out_kernel(y_flip, keys, info, attention, *rest):
     refs, (away, kept, weights, sems) = rest[:-4], rest[-4:]
     rows = refs[0].shape[0]
-    width = kept.shape[2]
+    width = kept.shape[1]
     per_group = width // rows
 
     for i, key in enumerate(keys):
         block = block_of(info, key)
-        group = (block // per_group) ^ (2 * info[1] + info[7])
+        group = block // per_group
+        side = (group % 2) ^ info[7]
         spot = pl.multiple_of((block % per_group) * rows, 16)
-        pltpu.make_async_copy(
-            refs[i], weights.at[group, pl.ds(spot, rows), :], sems.at[group]
-        ).start()
-    for out, j, group in ((away, 1, 3), (away, 0, 1), (kept, 1, 2), (kept, 0, 0)):
-        pltpu.make_async_copy(weights.at[group], weights.at[group], sems.at[group]).wait()
-        out[j] = lax.dot_general(
+        copy = pltpu.make_async_copy(
+            refs[i], weights.at[side, pl.ds(spot, rows), :], sems.at[side]
+        )
+        pl.when(group // 2 == (info[1] ^ y_flip))(copy.start)
+    for out, side in ((away, 1), (kept, 0)):
+        pltpu.make_async_copy(weights.at[side], weights.at[side], sems.at[side]).wait()
+        out[...] = lax.dot_general(
             attention[...],
-            weights[group],
+            weights[side],
             (((1,), (1,)), ((), ())),
             preferred_element_type=jnp.float32,
         ).astype(jnp.bfloat16)
 
 
-def out_project(info, attention, pieces):
+def out_project(y_flip, info, attention, pieces):
     tokens, depth = attention.shape
     keys = tuple(pieces)
     width = len(keys) * pieces[keys[0]].shape[0] // KVH
-    shape = jax.ShapeDtypeStruct((2, tokens, width), jnp.bfloat16)
+    shape = jax.ShapeDtypeStruct((tokens, width), jnp.bfloat16)
     return pl.pallas_call(
-        functools.partial(out_kernel, keys),
+        functools.partial(out_kernel, y_flip, keys),
         out_shape=(shape, shape),
         in_specs=[smem(), vmem()] + [hbm()] * len(keys),
         out_specs=(vmem(), vmem()),
         scratch_shapes=[
-            pltpu.VMEM((KVH, width, depth), jnp.bfloat16),
-            pltpu.SemaphoreType.DMA((KVH,)),
+            pltpu.VMEM((2, width, depth), jnp.bfloat16),
+            pltpu.SemaphoreType.DMA((2,)),
         ],
         compiler_params=params(),
         cost_estimate=pl.CostEstimate(
-            flops=8 * tokens * width * depth, bytes_accessed=8 * width * depth, transcendentals=0
+            flops=4 * tokens * width * depth, bytes_accessed=4 * width * depth, transcendentals=0
         ),
         name="out_project",
     )(info, attention, *[pieces[k] for k in keys])
@@ -582,8 +584,7 @@
         return send(value, n_seq, lambda big, l, x, y, c: (big, l, x, 1 - y, c))
 
     def add(kept, from_core):
-        sums = kept.astype(jnp.float32) + from_core.astype(jnp.float32)
-        return sums[0], sums[1].astype(jnp.bfloat16)
+        return kept.astype(jnp.float32) + from_core.astype(jnp.float32)
 
     part = rows_dev // 2
     early = attend_rows(0, part)
@@ -596,21 +597,24 @@
     late = attend_rows(part, part)
     late, early, early_swapped = together(late, early, early_swapped)
     late_swapped = swap_back(late)
-    early_away, early_kept = out_project(info, jnp.where(matched, early, early_swapped), outs)
-    early_away, early_kept, late, late_swapped = together(
-        early_away, early_kept, late, late_swapped
-    )
-    early_near, early_far = add(early_kept, swap_core(early_away))
+    early = jnp.where(matched, early, early_swapped)
+    early_away, early_kept = out_project(1, info, early, outs)
+    early_away, early_kept, late_swapped = together(early_away, early_kept, late_swapped)
     late = jnp.where(matched, late, late_swapped)
-    late, early_near, early_far = together(late, early_near, early_far)
+    early_core = swap_core(early_away)
+    late_away, late_kept = out_project(1, info, late, outs)
+    late_away, late_kept, early_core = together(late_away, late_kept, early_core)
+    early_far = add(early_kept, early_core).astype(jnp.bfloat16)
     early_from_y = swap_y(early_far)
-    late_away, late_kept = out_project(info, late, outs)
-    late_away, late_kept, early_from_y = together(late_away, late_kept, early_from_y)
-    late_near, late_far = add(late_kept, swap_core(late_away))
-    results = [(early_near, early_from_y), (late_near, swap_y(late_far))]
-    return jnp.concatenate(
-        [(near + from_y.astype(jnp.float32)).astype(jnp.bfloat16) for near, from_y in results], axis=0
-    )
+    late_core = swap_core(late_away)
+    late_core, early_far = together(late_core, early_far)
+    late_far = add(late_kept, late_core).astype(jnp.bfloat16)
+    early, late, late_far = together(early, late, late_far)
+    late_from_y = swap_y(late_far)
+    away, kept = out_project(0, info, jnp.concatenate([early, late], axis=0), outs)
+    kept, away, early_from_y, late_from_y = together(kept, away, early_from_y, late_from_y)
+    from_y = jnp.concatenate([early_from_y, late_from_y], axis=0)
+    return (add(kept, swap_core(away)) + from_y.astype(jnp.float32)).astype(jnp.bfloat16)
 
 
 def solution(mesh):

time: 229 us -> 229 us (level)
  waiting for transfers between devices: 81.9 us -> 74.9 us
  starting transfers between devices: 71.9 us -> 76.1 us
    ppermute x38 -> x39, waiting for transfers between devices: 81.9 us -> 74.9 us  [send(): return lax.ppermute(value, AXES, moves(n_seq, rule))]
    ppermute x38 -> x39, starting transfers between devices: 71.9 us -> 76.1 us  [send(): return lax.ppermute(value, AXES, moves(n_seq, rule))]
    convert_element_type x2 -> x3, other arithmetic: 0.19 us -> 2.66 us  [the longest x1 2.44 us: on_device(): (add(kept, swap_core(away)) + from_y.astype(jnp.float32)).astype(jnp.bflo...]
    pallas_call x2 -> x3, Pallas kernels: 15.7 us -> 17.2 us  [out_project(): pl.pallas_call(functools.partial(out_kernel, y_flip, keys), out_shape=(sh...]
    unnamed x71 -> x79, local copies, waits for them, and re-layouts: 5.12 us -> 5.15 us
  transfers between devices with their start and end apart: 38 -> 39, of which waited for: 16 -> 15; matrix products, arithmetic and copies ran while one was open for 6% -> 6% of each run, Pallas kernels for 22% -> 23%
where the time goes in v6:
time: 229 us; the launch traced here: 227 us
  starting transfers between devices  76.1 us (33%)
  waiting for transfers between devices  74.9 us (33%)
  Pallas kernels  52.5 us (23%)
  local copies, waits for them, and re-layouts  13.8 us (6%)
  other arithmetic  7.46 us (3%)
  between operations  2.72 us (1%)
    ppermute x39, starting transfers between devices, send(): return lax.ppermute(value, AXES, moves(n_seq, rule))  76.1 us
    ppermute x39, waiting for transfers between devices, send(): return lax.ppermute(value, AXES, moves(n_seq, rule))  74.9 us
    pallas_call x3, Pallas kernels, out_project(): pl.pallas_call(functools.partial(out_kernel, y_flip, keys), out_shape=(sh...  17.2 us
    pallas_call x2, Pallas kernels, project(): pl.pallas_call(functools.partial(kernel, keys), out_shape=jax.ShapeDtypeS...  15.6 us
    pallas_call x2, Pallas kernels, attend(): pl.pallas_call(functools.partial(attend_kernel, tokens, slots, len(beacon...  14.2 us
    pallas_call x1, Pallas kernels, norm_and_pool(): pl.pallas_call(norm_kernel, out_shape=(jax.ShapeDtypeStruct((rows, width)...  5.49 us
    unnamed x79, local copies, waits for them, and re-layouts  5.15 us
  transfers between devices with their start and end apart: 39, of which 15 were waited for; matrix products, arithmetic and copies ran while one was open for 6% of the time, Pallas kernels for 23%

profile of v6, /device:TPU:0, one launch (start us, length us, event | category | flops | bytes accessed | tf_op | source)
XLA Modules:
  0.0 227.5 jit_solution(333850467083019102)
XLA Ops:
  2.7 5.9 %collective-permute-start.1 = (bf16[448,1408]{1,0:T(8,128)(2,1)S(1)}, bf16[448,1408]{1,0:T(8,128)(2,1)}, u32[]{:S(2)}, u32[]{:S(2)}) collective-permute-start(bf16[448,1408]{1,0:T(8,128)(2,1)S(1)} %bitcast_dynamic-update-slice_fusion.rest_0_), channel_id=1, source_target_pairs={{0,16},{2,18},{4,20},{6,22},{9,25},{11,27},{13,29},{15,31},{16,0},... | collective-permute-start | bytes 3784712 | tf_op jit(solution)/shard_map/ppermute | solution.py:48
  8.6 3.4 %collective-permute-start.2 = (bf16[448,1408]{1,0:T(8,128)(2,1)S(1)}, bf16[448,1408]{1,0:T(8,128)(2,1)}, u32[]{:S(2)}, u32[]{:S(2)}) collective-permute-start(bf16[448,1408]{1,0:T(8,128)(2,1)S(1)} %bitcast_dynamic-update-slice_fusion.rest_0_), channel_id=1, source_target_pairs={{0,4},{2,6},{4,0},{6,2},{9,13},{11,15},{13,9},{15,11},{16,20},{18,... | collective-permute-start | bytes 3784712 | tf_op jit(solution)/shard_map/ppermute | solution.py:48
  12.1 2.9 %constant_dynamic-slice_fusion = bf16[256,3584]{1,0:T(8,128)(2,1)} fusion(bf16[512,3584]{1,0:T(8,128)(2,1)} %hidden.1, s32[]{:T(128)S(6)} %select_n.77), kind=kLoop, calls=%fused_computation.18 | loop fusion | bytes 3670020 | tf_op jit(solution)/shard_map/dynamic_slice | solution.py:446
  15.0 2.1 collective-permute-start.7
  22.9 16.2 %collective-permute-done.3 = bf16[224,896]{1,0:T(8,128)(2,1)} collective-permute-done((bf16[224,896]{1,0:T(8,128)(2,1)}, bf16[224,896]{1,0:T(8,128)(2,1)}, u32[]{:S(2)}, u32[]{:S(2)}) %collective-permute-start.3) | collective-permute-done | bytes 401440 | tf_op jit(solution)/shard_map/ppermute | solution.py:48
  39.1 1.4 collective-permute-start.10
  40.5 1.9 collective-permute-start.4
  42.5 1.6 collective-permute-start.9
  45.3 2.4 %collective-permute-start.5 = (bf16[448,1408]{1,0:T(8,128)(2,1)S(1)}, bf16[448,1408]{1,0:T(8,128)(2,1)S(1)}, u32[]{:S(2)}, u32[]{:S(2)}) collective-permute-start(bf16[448,1408]{1,0:T(8,128)(2,1)S(1)} %collective-permute-done.rest_1_), channel_id=1, source_target_pairs={{0,4},{2,6},{4,0},{6,2},{9,13},{11,15},{13,9},{15,11},{16,20},{18,... | collective-permute-start | bytes 3784712 | tf_op jit(solution)/shard_map/ppermute | solution.py:48
  47.8 1.4 collective-permute-start.11
  49.1 1.4 collective-permute-done.9
  50.5 3.4 %collective-permute-start.6 = (bf16[448,1408]{1,0:T(8,128)(2,1)}, bf16[448,1408]{1,0:T(8,128)(2,1)S(1)}, u32[]{:S(2)}, u32[]{:S(2)}) collective-permute-start(bf16[448,1408]{1,0:T(8,128)(2,1)} %collective-permute-done.1.rest_2_), channel_id=1, source_target_pairs={{0,4},{2,6},{4,0},{6,2},{9,13},{11,15},{13,9},{15,11},{16,20},{18,... | collective-permute-start | bytes 3784712 | tf_op jit(solution)/shard_map/ppermute | solution.py:48
  53.9 10.5 %collective-permute-start.12 = (bf16[448,1408]{1,0:T(8,128)(2,1)}, bf16[448,1408]{1,0:T(8,128)(2,1)S(1)}, u32[]{:S(2)}, u32[]{:S(2)}) collective-permute-start(bf16[448,1408]{1,0:T(8,128)(2,1)} %collective-permute-done.1.rest_2_), channel_id=1, source_target_pairs={{0,1},{2,3},{4,5},{6,7},{9,8},{11,10},{13,12},{15,14},{16,17},{18,... | collective-permute-start | bytes 3784712 | tf_op jit(solution)/shard_map/ppermute | solution.py:48
  64.5 7.4 %collective-permute-done.4.rest_4_ = bf16[448,1408]{1,0:T(8,128)(2,1)S(1)} collective-permute-done((bf16[448,1408]{1,0:T(8,128)(2,1)S(1)}, bf16[448,1408]{1,0:T(8,128)(2,1)S(1)}, u32[]{:S(2)}, u32[]{:S(2)}) %collective-permute-start.4) | collective-permute-done | bytes 1261600 | tf_op jit(solution)/shard_map/ppermute | solution.py:48
  73.3 4.5 %collective-permute-done.6.rest_6_ = bf16[448,1408]{1,0:T(8,128)(2,1)S(1)} collective-permute-done((bf16[448,1408]{1,0:T(8,128)(2,1)}, bf16[448,1408]{1,0:T(8,128)(2,1)S(1)}, u32[]{:S(2)}, u32[]{:S(2)}) %collective-permute-start.6) | collective-permute-done | bytes 1261600 | tf_op jit(solution)/shard_map/ppermute | solution.py:48
  77.8 1.4 collective-permute-start.15
  79.2 1.4 collective-permute-start.16
  80.6 1.4 collective-permute-start.17
  82.0 1.9 collective-permute-start.14
  83.9 3.1 %collective-permute-start.20 = (bf16[448,1408]{1,0:T(8,128)(2,1)S(1)}, bf16[448,1408]{1,0:T(8,128)(2,1)}, u32[]{:S(2)}, u32[]{:S(2)}) collective-permute-start(bf16[448,1408]{1,0:T(8,128)(2,1)S(1)} %collective-permute-done.4.rest_4_), channel_id=1, source_target_pairs={{0,4},{2,6},{4,0},{6,2},{9,13},{11,15},{13,9},{15,11},{16,20},{18,... | collective-permute-start | bytes 3784712 | tf_op jit(solution)/shard_map/ppermute | solution.py:48
  87.0 2.1 collective-permute-start.18
  89.1 3.3 %collective-permute-start.19 = (bf16[448,896]{1,0:T(8,128)(2,1)S(1)}, bf16[448,896]{1,0:T(8,128)(2,1)S(1)}, u32[]{:S(2)}, u32[]{:S(2)}) collective-permute-start(bf16[448,896]{1,0:T(8,128)(2,1)S(1)} %bitcast.24), channel_id=1, source_target_pairs={{0,8},{1,9},{2,10},{3,11},{4,12},{5,13},{6,14},{7,15},{8,0},{9,1},... | collective-permute-start | bytes 2408456 | tf_op jit(solution)/shard_map/ppermute | solution.py:48
  92.5 5.5 %norm_pool.1 = (bf16[512,3584]{1,0:T(8,128)(2,1)}, bf16[64,3584]{1,0:T(8,128)(2,1)}) custom-call(s32[8]{0:T(128)} %stack.39.info, bf16[512,3584]{1,0:T(8,128)(2,1)} %hidden.1, bf16[256,3584]{1,0:T(8,128)(2,1)} %collective-permute-done.7.first, bf16[256,3584]{1,0:T(8,128)(2,1)} %collective-permute-done.14.second, f32[1,3584]{1,0:T(1,128)} %reshape.23.gain), custom_call_target="tpu_custom_call" | custom-call | flops 234881024 | bytes 7340032 | tf_op jit(solution)/shard_map/norm_pool/pallas_call | solution.py:99
  98.1 4.9 %collective-permute-done.20.rest_7_ = bf16[448,1408]{1,0:T(8,128)(2,1)} collective-permute-done((bf16[448,1408]{1,0:T(8,128)(2,1)S(1)}, bf16[448,1408]{1,0:T(8,128)(2,1)}, u32[]{:S(2)}, u32[]{:S(2)}) %collective-permute-start.20) | collective-permute-done | bytes 1261600 | tf_op jit(solution)/shard_map/ppermute | solution.py:48
  103.0 5.9 %collective-permute-done.19.rest_1_ = bf16[448,896]{1,0:T(8,128)(2,1)S(1)} collective-permute-done((bf16[448,896]{1,0:T(8,128)(2,1)S(1)}, bf16[448,896]{1,0:T(8,128)(2,1)S(1)}, u32[]{:S(2)}, u32[]{:S(2)}) %collective-permute-start.19) | collective-permute-done | bytes 802848 | tf_op jit(solution)/shard_map/ppermute | solution.py:48
  108.9 3.4 %collective-permute-start.21 = (bf16[448,1408]{1,0:T(8,128)(2,1)}, bf16[448,1408]{1,0:T(8,128)(2,1)S(1)}, u32[]{:S(2)}, u32[]{:S(2)}) collective-permute-start(bf16[448,1408]{1,0:T(8,128)(2,1)} %collective-permute-done.20.rest_7_), channel_id=1, source_target_pairs={{0,1},{2,3},{4,5},{6,7},{9,8},{11,10},{13,12},{15,14},{16,17},{18,... | collective-permute-start | bytes 3784712 | tf_op jit(solution)/shard_map/ppermute | solution.py:48
  112.3 1.6 collective-permute-start.24
  115.1 1.6 collective-permute-start.26
  119.0 6.3 %project.2.rest_0_ = bf16[576,256]{1,0:T(8,128)(2,1)} custom-call(s32[8]{0:T(128)} %stack.39.info, bf16[512,3584]{1,0:T(8,128)(2,1)} %get-tuple-element.92.normed, bf16[64,3584]{1,0:T(8,128)(2,1)} %get-tuple-element.82.pooled, f32[1,512]{1,0:T(1,128)} %bitcast.27, bf16[448,1408]{1,0:T(8,128)(2,1)} %copy-done.4, bf16[448,1408]{1,0:T(8,128)(2,1)} %copy-done.9, ...), custom_call_target="tpu_custom_call" | custom-call | flops 1056964608 | bytes 7798784 | tf_op jit(solution)/shard_map/project/pallas_call | solution.py:214
  125.9 9.3 %project.3.queries = bf16[512,896]{1,0:T(8,128)(2,1)} custom-call(s32[8]{0:T(128)} %stack.39.info, bf16[512,3584]{1,0:T(8,128)(2,1)} %get-tuple-element.92.normed, f32[1,896]{1,0:T(1,128)} %reshape.27.bias, bf16[448,1408]{1,0:T(8,128)(2,1)} %copy-done.4, bf16[448,1408]{1,0:T(8,128)(2,1)} %copy-done.9, bf16[448,1408]{1,0:T(8,128)(2,1)} %collective-permute-done.1.rest_2_, ...), custom_call_target="tpu_custom_call" | custom-call | flops 3288334336 | bytes 10092544 | tf_op jit(solution)/shard_map/project/pallas_call | solution.py:214
  135.2 5.5 %collective-permute-done.22.rest_1_ = bf16[576,256]{1,0:T(8,128)(2,1)S(1)} collective-permute-done((bf16[576,256]{1,0:T(8,128)(2,1)}, bf16[576,256]{1,0:T(8,128)(2,1)S(1)}, u32[]{:S(2)}, u32[]{:S(2)}) %collective-permute-start.22) | collective-permute-done | bytes 294944 | tf_op jit(solution)/shard_map/ppermute | solution.py:48
  140.7 1.5 collective-permute-start.29
  143.4 1.6 collective-permute-start.30
  146.6 5.1 %collective-permute-start.28 = (bf16[256,256]{1,0:T(8,128)(2,1)S(1)}, bf16[256,256]{1,0:T(8,128)(2,1)S(1)}, u32[]{:S(2)}, u32[]{:S(2)}) collective-permute-start(bf16[256,256]{1,0:T(8,128)(2,1)S(1)} %pad_maximum_fusion.1), channel_id=1, source_target_pairs={{0,16},{1,17},{2,18},{3,19},{4,20},{5,21},{6,22},{7,23},{8,24},{9,... | collective-permute-start | bytes 393224 | tf_op jit(solution)/shard_map/ppermute | solution.py:48
  151.6 6.7 %collective-permute-done.28.rest_4_ = bf16[256,256]{1,0:T(8,128)(2,1)S(1)} collective-permute-done((bf16[256,256]{1,0:T(8,128)(2,1)S(1)}, bf16[256,256]{1,0:T(8,128)(2,1)S(1)}, u32[]{:S(2)}, u32[]{:S(2)}) %collective-permute-start.28) | collective-permute-done | bytes 131104 | tf_op jit(solution)/shard_map/ppermute | solution.py:48
  159.0 6.8 %attend.2 = bf16[256,896]{1,0:T(8,128)(2,1)} custom-call(s32[8]{0:T(128)} %stack.39.info, s32[2]{0:T(128)} %ratios.3, bf16[512,896]{1,0:T(8,128)(2,1)} %project.3.queries, bf16[576,256]{1,0:T(8,128)(2,1)} %project.2.rest_0_, bf16[576,256]{1,0:T(8,128)(2,1)} %copy-done.33, bf16[576,256]{1,0:T(8,128)(2,1)} %copy-done.34, bf16[576,256]{1,0:T(8,128)(2,1)} %copy-done.35, ...), custom_call_target="tpu_custom_call" | custom-call | flops 2113929216 | bytes 1835008 | tf_op jit(solution)/shard_map/attend/pallas_call | solution.py:298
  166.6 1.4 collective-permute-start.32
  168.0 7.4 %attend.3 = bf16[256,896]{1,0:T(8,128)(2,1)} custom-call(s32[8]{0:T(128)} %stack.39.info, s32[2]{0:T(128)} %ratios.3, bf16[512,896]{1,0:T(8,128)(2,1)} %project.3.queries, bf16[576,256]{1,0:T(8,128)(2,1)} %project.2.rest_0_, bf16[576,256]{1,0:T(8,128)(2,1)} %copy-done.33, bf16[576,256]{1,0:T(8,128)(2,1)} %copy-done.34, bf16[576,256]{1,0:T(8,128)(2,1)} %copy-done.35, ...), custom_call_target="tpu_custom_call" | custom-call | flops 2113929216 | bytes 1835008 | tf_op jit(solution)/shard_map/attend/pallas_call | solution.py:298
  179.6 6.1 %collective-permute-done.32.rest_7_ = bf16[448,896]{1,0:T(8,128)(2,1)S(1)} collective-permute-done((bf16[448,896]{1,0:T(8,128)(2,1)S(1)}, bf16[448,896]{1,0:T(8,128)(2,1)S(1)}, u32[]{:S(2)}, u32[]{:S(2)}) %collective-permute-start.32) | collective-permute-done | bytes 802848 | tf_op jit(solution)/shard_map/ppermute | solution.py:48
  186.6 5.2 %out_project.3 = (bf16[256,896]{1,0:T(8,128)(2,1)}, bf16[256,896]{1,0:T(8,128)(2,1)}) custom-call(s32[8]{0:T(128)} %stack.39.info, bf16[256,896]{1,0:T(8,128)(2,1)} %broadcast_select_fusion.3.attention, bf16[448,896]{1,0:T(8,128)(2,1)} %bitcast.18, bf16[448,896]{1,0:T(8,128)(2,1)} %copy-done.5, bf16[448,896]{1,0:T(8,128)(2,1)} %copy-done.3, ...), custom_call_target="tpu_custom_call" | custom-call | flops 822083584 | bytes 3211264 | tf_op jit(solution)/shard_map/out_project/pallas_call | solution.py:345
  193.9 5.3 %out_project.4 = (bf16[256,896]{1,0:T(8,128)(2,1)}, bf16[256,896]{1,0:T(8,128)(2,1)}) custom-call(s32[8]{0:T(128)} %stack.39.info, bf16[256,896]{1,0:T(8,128)(2,1)} %broadcast_select_fusion.2.attention, bf16[448,896]{1,0:T(8,128)(2,1)} %bitcast.19, bf16[448,896]{1,0:T(8,128)(2,1)} %copy-done.5, bf16[448,896]{1,0:T(8,128)(2,1)} %copy-done.3, ...), custom_call_target="tpu_custom_call" | custom-call | flops 822083584 | bytes 3211264 | tf_op jit(solution)/shard_map/out_project/pallas_call | solution.py:345
  199.5 1.7 collective-permute-start.36
  201.5 1.7 collective-permute-start.37
  204.3 6.6 %out_project.5 = (bf16[512,896]{1,0:T(8,128)(2,1)}, bf16[512,896]{1,0:T(8,128)(2,1)}) custom-call(s32[8]{0:T(128)} %stack.39.info, bf16[512,896]{1,0:T(8,128)(2,1)} %pad_maximum_fusion.attention, bf16[448,896]{1,0:T(8,128)(2,1)} %bitcast.20, bf16[448,896]{1,0:T(8,128)(2,1)} %copy-done.5, bf16[448,896]{1,0:T(8,128)(2,1)} %copy-done.3, ...), custom_call_target="tpu_custom_call" | custom-call | flops 1644167168 | bytes 3211264 | tf_op jit(solution)/shard_map/out_project/pallas_call | solution.py:345
  210.9 2.0 collective-permute-done.36
  212.9 9.4 %collective-permute-done.37 = bf16[256,896]{1,0:T(8,128)(2,1)S(1)} collective-permute-done((bf16[256,896]{1,0:T(8,128)(2,1)S(1)}, bf16[256,896]{1,0:T(8,128)(2,1)S(1)}, u32[]{:S(2)}, u32[]{:S(2)}) %collective-permute-start.37) | collective-permute-done | bytes 458784 | tf_op jit(solution)/shard_map/ppermute | solution.py:48
  222.3 2.7 %collective-permute-done.38 = bf16[512,896]{1,0:T(8,128)(2,1)S(1)} collective-permute-done((bf16[512,896]{1,0:T(8,128)(2,1)}, bf16[512,896]{1,0:T(8,128)(2,1)S(1)}, u32[]{:S(2)}, u32[]{:S(2)}) %collective-permute-start.38) | collective-permute-done | bytes 917536 | tf_op jit(solution)/shard_map/ppermute | solution.py:48
  225.0 2.4 %add_convert_fusion = bf16[512,896]{1,0:T(8,128)(2,1)} fusion(bf16[512,896]{1,0:T(8,128)(2,1)S(1)} %collective-permute-done.38, bf16[512,896]{1,0:T(8,128)(2,1)} %get-tuple-element.129, bf16[256,896]{1,0:T(8,128)(2,1)S(1)} %collective-permute-done.37, bf16[256,896]{1,0:T(8,128)(2,1)S(1)} %collective-permute-done.36), kind=kLoop, calls=%fused_computation | loop fusion | flops 4128768 | bytes 3670016 | tf_op jit(solution)/shard_map/convert_element_type | solution.py:617
  (143 shorter events, 26.2 us)
Async XLA Ops:
  1.4 37.8 %copy-start.4 = (bf16[448,1408]{1,0:T(8,128)(2,1)}, bf16[448,1408]{1,0:T(8,128)(2,1)S(1)}, u32[]{:S(2)}) copy-start(bf16[448,1408]{1,0:T(8,128)(2,1)S(1)} %bitcast_dynamic-update-slice_fusion.rest_0_) | copy-start | bytes 3784708
  1.4 39.1 %collective-permute-start = (bf16[448,1408]{1,0:T(8,128)(2,1)S(1)}, bf16[448,1408]{1,0:T(8,128)(2,1)S(1)}, u32[]{:S(2)}, u32[]{:S(2)}) collective-permute-start(bf16[448,1408]{1,0:T(8,128)(2,1)S(1)} %bitcast_dynamic-update-slice_fusion.rest_0_), channel_id=1, source_target_pairs={{1,9},{3,11},{5,13},{7,15},{8,0},{10,2},{12,4},{14,6},{17,25},{19,... | collective-permute-start | bytes 3784712 | tf_op jit(solution)/shard_map/ppermute | solution.py:48
  2.7 37.8 %collective-permute-start.1 = (bf16[448,1408]{1,0:T(8,128)(2,1)S(1)}, bf16[448,1408]{1,0:T(8,128)(2,1)}, u32[]{:S(2)}, u32[]{:S(2)}) collective-permute-start(bf16[448,1408]{1,0:T(8,128)(2,1)S(1)} %bitcast_dynamic-update-slice_fusion.rest_0_), channel_id=1, source_target_pairs={{0,16},{2,18},{4,20},{6,22},{9,25},{11,27},{13,29},{15,31},{16,0},... | collective-permute-start | bytes 3784712 | tf_op jit(solution)/shard_map/ppermute | solution.py:48
  8.6 31.9 %collective-permute-start.2 = (bf16[448,1408]{1,0:T(8,128)(2,1)S(1)}, bf16[448,1408]{1,0:T(8,128)(2,1)}, u32[]{:S(2)}, u32[]{:S(2)}) collective-permute-start(bf16[448,1408]{1,0:T(8,128)(2,1)S(1)} %bitcast_dynamic-update-slice_fusion.rest_0_), channel_id=1, source_target_pairs={{0,4},{2,6},{4,0},{6,2},{9,13},{11,15},{13,9},{15,11},{16,20},{18,... | collective-permute-start | bytes 3784712 | tf_op jit(solution)/shard_map/ppermute | solution.py:48
  15.0 29.0 %copy-start.29 = (f32[896]{0:T(1024)S(1)}, f32[896]{0:T(1024)}, u32[]{:S(2)}) copy-start(f32[896]{0:T(1024)} %param.13) | copy-start | bytes 10756
  15.0 29.0 %copy-start.31 = (f32[2,128]{1,0:T(2,128)S(1)}, f32[2,128]{1,0:T(2,128)}, u32[]{:S(2)}) copy-start(f32[2,128]{1,0:T(2,128)} %param.17) | copy-start | bytes 3076
  15.0 29.0 %copy-start.32 = (f32[2,128]{1,0:T(2,128)S(1)}, f32[2,128]{1,0:T(2,128)}, u32[]{:S(2)}) copy-start(f32[2,128]{1,0:T(2,128)} %param.15) | copy-start | bytes 3076
  15.0 38.9 %collective-permute-start.7 = (bf16[256,3584]{1,0:T(8,128)(2,1)}, bf16[256,3584]{1,0:T(8,128)(2,1)}, u32[]{:S(2)}, u32[]{:S(2)}) collective-permute-start(bf16[256,3584]{1,0:T(8,128)(2,1)} %constant_dynamic-slice_fusion), channel_id=1, source_target_pairs={{1,8},{3,10},{5,12},{7,14},{8,1},{10,3},{12,5},{14,7},{17,24},{19,... | collective-permute-start | bytes 5505032 | tf_op jit(solution)/shard_map/ppermute | solution.py:48
  17.9 21.2 %collective-permute-start.3 = (bf16[224,896]{1,0:T(8,128)(2,1)}, bf16[224,896]{1,0:T(8,128)(2,1)}, u32[]{:S(2)}, u32[]{:S(2)}) collective-permute-start(bf16[224,896]{1,0:T(8,128)(2,1)} %slice.32), channel_id=1, source_target_pairs={{0,4},{1,5},{2,6},{3,7},{4,0},{5,1},{6,2},{7,3},{8,12},{9,13},{10,... | collective-permute-start | bytes 1204232 | tf_op jit(solution)/shard_map/ppermute | solution.py:48
  39.1 8.6 %collective-permute-start.10 = (bf16[448,1408]{1,0:T(8,128)(2,1)S(1)}, bf16[448,1408]{1,0:T(8,128)(2,1)S(1)}, u32[]{:S(2)}, u32[]{:S(2)}) collective-permute-start(bf16[448,1408]{1,0:T(8,128)(2,1)S(1)} %bitcast_dynamic-update-slice_fusion.rest_0_), channel_id=1, source_target_pairs={{0,1},{2,3},{4,5},{6,7},{9,8},{11,10},{13,12},{15,14},{16,17},{18,... | collective-permute-start | bytes 3784712 | tf_op jit(solution)/shard_map/ppermute | solution.py:48
  40.5 57.6 %copy-start.9 = (bf16[448,1408]{1,0:T(8,128)(2,1)}, bf16[448,1408]{1,0:T(8,128)(2,1)S(1)}, u32[]{:S(2)}) copy-start(bf16[448,1408]{1,0:T(8,128)(2,1)S(1)} %collective-permute-done.rest_1_) | copy-start | bytes 3784708
  40.5 31.4 %collective-permute-start.4 = (bf16[448,1408]{1,0:T(8,128)(2,1)S(1)}, bf16[448,1408]{1,0:T(8,128)(2,1)S(1)}, u32[]{:S(2)}, u32[]{:S(2)}) collective-permute-start(bf16[448,1408]{1,0:T(8,128)(2,1)S(1)} %collective-permute-done.rest_1_), channel_id=1, source_target_pairs={{0,16},{2,18},{4,20},{6,22},{9,25},{11,27},{13,29},{15,31},{16,0},... | collective-permute-start | bytes 3784712 | tf_op jit(solution)/shard_map/ppermute | solution.py:48
  42.5 8.0 %collective-permute-start.9 = (bf16[224,896]{1,0:T(8,128)(2,1)S(1)}, bf16[224,896]{1,0:T(8,128)(2,1)}, u32[]{:S(2)}, u32[]{:S(2)}) collective-permute-start(bf16[224,896]{1,0:T(8,128)(2,1)S(1)} %slice.25), channel_id=1, source_target_pairs={{0,4},{1,5},{2,6},{3,7},{4,0},{5,1},{6,2},{7,3},{8,12},{9,13},{10,... | collective-permute-start | bytes 1204232 | tf_op jit(solution)/shard_map/ppermute | solution.py:48
  44.1 1.2 collective-permute-start.8
  45.3 28.0 %collective-permute-start.5 = (bf16[448,1408]{1,0:T(8,128)(2,1)S(1)}, bf16[448,1408]{1,0:T(8,128)(2,1)S(1)}, u32[]{:S(2)}, u32[]{:S(2)}) collective-permute-start(bf16[448,1408]{1,0:T(8,128)(2,1)S(1)} %collective-permute-done.rest_1_), channel_id=1, source_target_pairs={{0,4},{2,6},{4,0},{6,2},{9,13},{11,15},{13,9},{15,11},{16,20},{18,... | collective-permute-start | bytes 3784712 | tf_op jit(solution)/shard_map/ppermute | solution.py:48
  47.8 44.7 %copy-start.10 = (bf16[448,1408]{1,0:T(8,128)(2,1)}, bf16[448,1408]{1,0:T(8,128)(2,1)S(1)}, u32[]{:S(2)}) copy-start(bf16[448,1408]{1,0:T(8,128)(2,1)S(1)} %collective-permute-done.10.rest_8_) | copy-start | bytes 3784708
  47.8 30.0 %collective-permute-start.11 = (bf16[448,1408]{1,0:T(8,128)(2,1)S(1)}, bf16[448,1408]{1,0:T(8,128)(2,1)S(1)}, u32[]{:S(2)}, u32[]{:S(2)}) collective-permute-start(bf16[448,1408]{1,0:T(8,128)(2,1)S(1)} %collective-permute-done.rest_1_), channel_id=1, source_target_pairs={{0,1},{2,3},{4,5},{6,7},{9,8},{11,10},{13,12},{15,14},{16,17},{18,... | collective-permute-start | bytes 3784712 | tf_op jit(solution)/shard_map/ppermute | solution.py:48
  50.5 27.3 %collective-permute-start.6 = (bf16[448,1408]{1,0:T(8,128)(2,1)}, bf16[448,1408]{1,0:T(8,128)(2,1)S(1)}, u32[]{:S(2)}, u32[]{:S(2)}) collective-permute-start(bf16[448,1408]{1,0:T(8,128)(2,1)} %collective-permute-done.1.rest_2_), channel_id=1, source_target_pairs={{0,4},{2,6},{4,0},{6,2},{9,13},{11,15},{13,9},{15,11},{16,20},{18,... | collective-permute-start | bytes 3784712 | tf_op jit(solution)/shard_map/ppermute | solution.py:48
  53.9 23.9 %collective-permute-start.12 = (bf16[448,1408]{1,0:T(8,128)(2,1)}, bf16[448,1408]{1,0:T(8,128)(2,1)S(1)}, u32[]{:S(2)}, u32[]{:S(2)}) collective-permute-start(bf16[448,1408]{1,0:T(8,128)(2,1)} %collective-permute-done.1.rest_2_), channel_id=1, source_target_pairs={{0,1},{2,3},{4,5},{6,7},{9,8},{11,10},{13,12},{15,14},{16,17},{18,... | collective-permute-start | bytes 3784712 | tf_op jit(solution)/shard_map/ppermute | solution.py:48
  71.9 26.1 %copy-start.11 = (bf16[448,1408]{1,0:T(8,128)(2,1)}, bf16[448,1408]{1,0:T(8,128)(2,1)S(1)}, u32[]{:S(2)}) copy-start(bf16[448,1408]{1,0:T(8,128)(2,1)S(1)} %collective-permute-done.4.rest_4_) | copy-start | bytes 3784708
  71.9 5.9 %collective-permute-start.13 = (bf16[448,1408]{1,0:T(8,128)(2,1)}, bf16[448,1408]{1,0:T(8,128)(2,1)S(1)}, u32[]{:S(2)}, u32[]{:S(2)}) collective-permute-start(bf16[448,1408]{1,0:T(8,128)(2,1)} %collective-permute-done.2.rest_3_), channel_id=1, source_target_pairs={{0,1},{2,3},{4,5},{6,7},{9,8},{11,10},{13,12},{15,14},{16,17},{18,... | collective-permute-start | bytes 3784712 | tf_op jit(solution)/shard_map/ppermute | solution.py:48
  77.8 20.3 %copy-start.13 = (bf16[448,1408]{1,0:T(8,128)(2,1)}, bf16[448,1408]{1,0:T(8,128)(2,1)S(1)}, u32[]{:S(2)}) copy-start(bf16[448,1408]{1,0:T(8,128)(2,1)S(1)} %collective-permute-done.11.rest_9_) | copy-start | bytes 3784708
  77.8 9.1 %collective-permute-start.15 = (bf16[448,1408]{1,0:T(8,128)(2,1)S(1)}, bf16[448,1408]{1,0:T(8,128)(2,1)S(1)}, u32[]{:S(2)}, u32[]{:S(2)}) collective-permute-start(bf16[448,1408]{1,0:T(8,128)(2,1)S(1)} %collective-permute-done.4.rest_4_), channel_id=1, source_target_pairs={{0,1},{2,3},{4,5},{6,7},{9,8},{11,10},{13,12},{15,14},{16,17},{18,... | collective-permute-start | bytes 3784712 | tf_op jit(solution)/shard_map/ppermute | solution.py:48
  79.2 7.8 %collective-permute-start.16 = (bf16[448,1408]{1,0:T(8,128)(2,1)S(1)}, bf16[448,1408]{1,0:T(8,128)(2,1)S(1)}, u32[]{:S(2)}, u32[]{:S(2)}) collective-permute-start(bf16[448,1408]{1,0:T(8,128)(2,1)S(1)} %collective-permute-done.5.rest_5_), channel_id=1, source_target_pairs={{0,1},{2,3},{4,5},{6,7},{9,8},{11,10},{13,12},{15,14},{16,17},{18,... | collective-permute-start | bytes 3784712 | tf_op jit(solution)/shard_map/ppermute | solution.py:48
  80.6 6.4 %collective-permute-start.17 = (bf16[448,1408]{1,0:T(8,128)(2,1)S(1)}, bf16[448,1408]{1,0:T(8,128)(2,1)S(1)}, u32[]{:S(2)}, u32[]{:S(2)}) collective-permute-start(bf16[448,1408]{1,0:T(8,128)(2,1)S(1)} %collective-permute-done.6.rest_6_), channel_id=1, source_target_pairs={{0,1},{2,3},{4,5},{6,7},{9,8},{11,10},{13,12},{15,14},{16,17},{18,... | collective-permute-start | bytes 3784712 | tf_op jit(solution)/shard_map/ppermute | solution.py:48
  82.0 10.6 %collective-permute-start.14 = (bf16[256,3584]{1,0:T(8,128)(2,1)}, bf16[256,3584]{1,0:T(8,128)(2,1)}, u32[]{:S(2)}, u32[]{:S(2)}) collective-permute-start(bf16[256,3584]{1,0:T(8,128)(2,1)} %collective-permute-done.7.first), channel_id=1, source_target_pairs={{1,3},{3,1},{5,7},{7,5},{8,10},{10,8},{12,14},{14,12},{17,19},{19,... | collective-permute-start | bytes 5505032 | tf_op jit(solution)/shard_map/ppermute | solution.py:48
  83.9 19.1 %collective-permute-start.20 = (bf16[448,1408]{1,0:T(8,128)(2,1)S(1)}, bf16[448,1408]{1,0:T(8,128)(2,1)}, u32[]{:S(2)}, u32[]{:S(2)}) collective-permute-start(bf16[448,1408]{1,0:T(8,128)(2,1)S(1)} %collective-permute-done.4.rest_4_), channel_id=1, source_target_pairs={{0,4},{2,6},{4,0},{6,2},{9,13},{11,15},{13,9},{15,11},{16,20},{18,... | collective-permute-start | bytes 3784712 | tf_op jit(solution)/shard_map/ppermute | solution.py:48
  87.0 15.9 %collective-permute-start.18 = (bf16[448,896]{1,0:T(8,128)(2,1)S(1)}, bf16[448,896]{1,0:T(8,128)(2,1)}, u32[]{:S(2)}, u32[]{:S(2)}) collective-permute-start(bf16[448,896]{1,0:T(8,128)(2,1)S(1)} %bitcast.23), channel_id=1, source_target_pairs={{8,16},{9,17},{10,18},{11,19},{12,20},{13,21},{14,22},{15,23},{16,... | collective-permute-start | bytes 2408456 | tf_op jit(solution)/shard_map/ppermute | solution.py:48
  89.1 19.8 %collective-permute-start.19 = (bf16[448,896]{1,0:T(8,128)(2,1)S(1)}, bf16[448,896]{1,0:T(8,128)(2,1)S(1)}, u32[]{:S(2)}, u32[]{:S(2)}) collective-permute-start(bf16[448,896]{1,0:T(8,128)(2,1)S(1)} %bitcast.24), channel_id=1, source_target_pairs={{0,8},{1,9},{2,10},{3,11},{4,12},{5,13},{6,14},{7,15},{8,0},{9,1},... | collective-permute-start | bytes 2408456 | tf_op jit(solution)/shard_map/ppermute | solution.py:48
  108.9 9.0 %collective-permute-start.21 = (bf16[448,1408]{1,0:T(8,128)(2,1)}, bf16[448,1408]{1,0:T(8,128)(2,1)S(1)}, u32[]{:S(2)}, u32[]{:S(2)}) collective-permute-start(bf16[448,1408]{1,0:T(8,128)(2,1)} %collective-permute-done.20.rest_7_), channel_id=1, source_target_pairs={{0,1},{2,3},{4,5},{6,7},{9,8},{11,10},{13,12},{15,14},{16,17},{18,... | collective-permute-start | bytes 3784712 | tf_op jit(solution)/shard_map/ppermute | solution.py:48
  112.3 28.3 %collective-permute-start.24 = (bf16[448,896]{1,0:T(8,128)(2,1)S(1)}, bf16[448,896]{1,0:T(8,128)(2,1)}, u32[]{:S(2)}, u32[]{:S(2)}) collective-permute-start(bf16[448,896]{1,0:T(8,128)(2,1)S(1)} %collective-permute-done.19.rest_1_), channel_id=1, source_target_pairs={{8,16},{9,17},{10,18},{11,19},{12,20},{13,21},{14,22},{15,23},{16,... | collective-permute-start | bytes 2408456 | tf_op jit(solution)/shard_map/ppermute | solution.py:48
  113.9 26.8 %collective-permute-start.25 = (bf16[448,896]{1,0:T(8,128)(2,1)}, bf16[448,896]{1,0:T(8,128)(2,1)}, u32[]{:S(2)}, u32[]{:S(2)}) collective-permute-start(bf16[448,896]{1,0:T(8,128)(2,1)} %collective-permute-done.18), channel_id=1, source_target_pairs={{8,0},{9,1},{10,2},{11,3},{12,4},{13,5},{14,6},{15,7},{16,24},{17,... | collective-permute-start | bytes 2408456 | tf_op jit(solution)/shard_map/ppermute | solution.py:48
  115.1 25.5 %collective-permute-start.26 = (bf16[448,896]{1,0:T(8,128)(2,1)S(1)}, bf16[448,896]{1,0:T(8,128)(2,1)S(1)}, u32[]{:S(2)}, u32[]{:S(2)}) collective-permute-start(bf16[448,896]{1,0:T(8,128)(2,1)S(1)} %collective-permute-done.19.rest_1_), channel_id=1, source_target_pairs={{0,4},{1,5},{2,6},{3,7},{4,0},{5,1},{6,2},{7,3},{8,12},{9,13},{10,... | collective-permute-start | bytes 2408456 | tf_op jit(solution)/shard_map/ppermute | solution.py:48
  125.3 15.4 %collective-permute-start.22 = (bf16[576,256]{1,0:T(8,128)(2,1)}, bf16[576,256]{1,0:T(8,128)(2,1)S(1)}, u32[]{:S(2)}, u32[]{:S(2)}) collective-permute-start(bf16[576,256]{1,0:T(8,128)(2,1)} %project.2.rest_0_), channel_id=1, source_target_pairs={{0,4},{1,5},{2,6},{3,7},{4,0},{5,1},{6,2},{7,3},{8,12},{9,13},{10,... | collective-permute-start | bytes 884744 | tf_op jit(solution)/shard_map/ppermute | solution.py:48
  125.9 14.8 %collective-permute-start.23 = (bf16[576,256]{1,0:T(8,128)(2,1)}, bf16[576,256]{1,0:T(8,128)(2,1)S(1)}, u32[]{:S(2)}, u32[]{:S(2)}) collective-permute-start(bf16[576,256]{1,0:T(8,128)(2,1)} %project.2.rest_0_), channel_id=1, source_target_pairs={{0,1},{1,0},{2,3},{3,2},{4,5},{5,4},{6,7},{7,6},{8,9},{9,8},{10,11... | collective-permute-start | bytes 884744 | tf_op jit(solution)/shard_map/ppermute | solution.py:48
  140.7 25.1 %collective-permute-start.29 = (bf16[448,896]{1,0:T(8,128)(2,1)}, bf16[448,896]{1,0:T(8,128)(2,1)S(1)}, u32[]{:S(2)}, u32[]{:S(2)}) collective-permute-start(bf16[448,896]{1,0:T(8,128)(2,1)} %collective-permute-done.24), channel_id=1, source_target_pairs={{8,0},{9,1},{10,2},{11,3},{12,4},{13,5},{14,6},{15,7},{16,24},{17,... | collective-permute-start | bytes 2408456 | tf_op jit(solution)/shard_map/ppermute | solution.py:48
  143.4 22.4 %copy-start.1 = (bf16[448,896]{1,0:T(8,128)(2,1)}, bf16[448,896]{1,0:T(8,128)(2,1)S(1)}, u32[]{:S(2)}) copy-start(bf16[448,896]{1,0:T(8,128)(2,1)S(1)} %broadcast_select_fusion.1.rest_4_) | copy-start | bytes 2408452
  143.4 22.4 %collective-permute-start.30 = (bf16[448,896]{1,0:T(8,128)(2,1)S(1)}, bf16[448,896]{1,0:T(8,128)(2,1)S(1)}, u32[]{:S(2)}, u32[]{:S(2)}) collective-permute-start(bf16[448,896]{1,0:T(8,128)(2,1)S(1)} %broadcast_select_fusion.1.rest_4_), channel_id=1, source_target_pairs={{0,4},{1,5},{2,6},{3,7},{4,0},{5,1},{6,2},{7,3},{8,12},{9,13},{10,... | collective-permute-start | bytes 2408456 | tf_op jit(solution)/shard_map/ppermute | solution.py:48
  145.0 1.6 collective-permute-start.27
  146.6 11.8 %collective-permute-start.28 = (bf16[256,256]{1,0:T(8,128)(2,1)S(1)}, bf16[256,256]{1,0:T(8,128)(2,1)S(1)}, u32[]{:S(2)}, u32[]{:S(2)}) collective-permute-start(bf16[256,256]{1,0:T(8,128)(2,1)S(1)} %pad_maximum_fusion.1), channel_id=1, source_target_pairs={{0,16},{1,17},{2,18},{3,19},{4,20},{5,21},{6,22},{7,23},{8,24},{9,... | collective-permute-start | bytes 393224 | tf_op jit(solution)/shard_map/ppermute | solution.py:48
  165.8 9.6 %collective-permute-start.31 = (bf16[256,896]{1,0:T(8,128)(2,1)}, bf16[256,896]{1,0:T(8,128)(2,1)S(1)}, u32[]{:S(2)}, u32[]{:S(2)}) collective-permute-start(bf16[256,896]{1,0:T(8,128)(2,1)} %attend.2), channel_id=1, source_target_pairs={{1,8},{3,10},{5,12},{7,14},{8,1},{10,3},{12,5},{14,7},{17,24},{19,... | collective-permute-start | bytes 1376264 | tf_op jit(solution)/shard_map/ppermute | solution.py:48
  166.6 19.0 %collective-permute-start.32 = (bf16[448,896]{1,0:T(8,128)(2,1)S(1)}, bf16[448,896]{1,0:T(8,128)(2,1)S(1)}, u32[]{:S(2)}, u32[]{:S(2)}) collective-permute-start(bf16[448,896]{1,0:T(8,128)(2,1)S(1)} %broadcast_select_fusion.rest_6_), channel_id=1, source_target_pairs={{0,4},{1,5},{2,6},{3,7},{4,0},{5,1},{6,2},{7,3},{8,12},{9,13},{10,... | collective-permute-start | bytes 2408456 | tf_op jit(solution)/shard_map/ppermute | solution.py:48
  175.5 16.4 %collective-permute-start.33 = (bf16[256,896]{1,0:T(8,128)(2,1)}, bf16[256,896]{1,0:T(8,128)(2,1)S(1)}, u32[]{:S(2)}, u32[]{:S(2)}) collective-permute-start(bf16[256,896]{1,0:T(8,128)(2,1)} %attend.3), channel_id=1, source_target_pairs={{1,8},{3,10},{5,12},{7,14},{8,1},{10,3},{12,5},{14,7},{17,24},{19,... | collective-permute-start | bytes 1376264 | tf_op jit(solution)/shard_map/ppermute | solution.py:48
  191.9 7.4 %collective-permute-start.34 = (bf16[256,896]{1,0:T(8,128)(2,1)}, bf16[256,896]{1,0:T(8,128)(2,1)S(1)}, u32[]{:S(2)}, u32[]{:S(2)}) collective-permute-start(bf16[256,896]{1,0:T(8,128)(2,1)} %get-tuple-element.118), channel_id=1, source_target_pairs={{0,1},{1,0},{2,3},{3,2},{4,5},{5,4},{6,7},{7,6},{8,9},{9,8},{10,11... | collective-permute-start | bytes 1376264 | tf_op jit(solution)/shard_map/ppermute | solution.py:48
  199.3 2.1 collective-permute-start.35
  199.5 13.4 %collective-permute-start.36 = (bf16[256,896]{1,0:T(8,128)(2,1)S(1)}, bf16[256,896]{1,0:T(8,128)(2,1)S(1)}, u32[]{:S(2)}, u32[]{:S(2)}) collective-permute-start(bf16[256,896]{1,0:T(8,128)(2,1)S(1)} %add_convert_fusion.2), channel_id=1, source_target_pairs={{0,2},{1,3},{2,0},{3,1},{4,6},{5,7},{6,4},{7,5},{8,10},{9,11},{10,... | collective-permute-start | bytes 1376264 | tf_op jit(solution)/shard_map/ppermute | solution.py:48
  201.5 20.8 %collective-permute-start.37 = (bf16[256,896]{1,0:T(8,128)(2,1)S(1)}, bf16[256,896]{1,0:T(8,128)(2,1)S(1)}, u32[]{:S(2)}, u32[]{:S(2)}) collective-permute-start(bf16[256,896]{1,0:T(8,128)(2,1)S(1)} %add_convert_fusion.1), channel_id=1, source_target_pairs={{0,2},{1,3},{2,0},{3,1},{4,6},{5,7},{6,4},{7,5},{8,10},{9,11},{10,... | collective-permute-start | bytes 1376264 | tf_op jit(solution)/shard_map/ppermute | solution.py:48
  222.3 2.7 %collective-permute-start.38 = (bf16[512,896]{1,0:T(8,128)(2,1)}, bf16[512,896]{1,0:T(8,128)(2,1)S(1)}, u32[]{:S(2)}, u32[]{:S(2)}) collective-permute-start(bf16[512,896]{1,0:T(8,128)(2,1)} %get-tuple-element.130), channel_id=1, source_target_pairs={{0,1},{1,0},{2,3},{3,2},{4,5},{5,4},{6,7},{7,6},{8,9},{9,8},{10,11... | collective-permute-start | bytes 2752520 | tf_op jit(solution)/shard_map/ppermute | solution.py:48
  (29 other events, 206.7 us)
